TPU v7x, 512 devices: a whole 4x8x8 slice. The times are simulated.
512 devices in a mesh: dp: 64 (over z, y_lo, core), tensor: 8 (over y_hi, x).
Axes of the slice: x: 4, y: 8 (y_hi: 2, y_lo: 4; y = y_hi * 4 + y_lo), z: 8, core: 2. Of those that a mesh axis runs over, the one named last changes fastest.
Arguments:
- tokens: bfloat16 [24576, 8192], P(('dp', 'tensor')), may hold values from -6 to 6
- grad_gate: bfloat16 [24576, 28672], P('dp', 'tensor'), may hold values from -1.25 to 1.25
- basis: bfloat16 [8192, 256], P(('dp', 'tensor')), may hold values from -0.375 to 0.375
- first_moment: float32 [256, 28672], P('dp', 'tensor'), may hold values from -0.375 to 0.375
- second_moment: float32 [256, 28672], P('dp', 'tensor'), may hold values from 0.02 to 0.2
Outputs:
- update: bfloat16 [8192, 28672], P('dp', 'tensor')
- first_out: float32 [256, 28672], P('dp', 'tensor')
- second_out: float32 [256, 28672], P('dp', 'tensor')
All inputs are finite; a program needn't handle non-finite values.
Results may differ from a plain program's by a relative error of at most 0.0057.
Values may be sent and summed in bfloat16 or wider, within the bound.
No kernel may reach another device: no remote copies, remote signals or barrier semaphores. Data moves between devices by JAX's collectives and lax.ppermute only.
A program may use at most 64 MiB of HBM per device.

v0:
```python
import math

import jax
import jax.numpy as jnp
from jax import lax
from jax.sharding import PartitionSpec as P

STEP = 10


BETA_ONE = 0.9
BETA_TWO = 0.95
EPS = 1e-08


def per_device(tokens, grad_gate, basis, first_moment, second_moment):
    data_count = lax.axis_size("dp")
    tensor_count = lax.axis_size("tensor")
    block_rows = basis.shape[0]
    owner_rows = block_rows * tensor_count
    whole_basis = lax.all_gather(basis, ("dp", "tensor"), axis=0, tiled=True)
    local_coefficients = lax.dot_general(
        whole_basis, tokens, (((0,), (1,)), ((), ())), preferred_element_type=jnp.float32
    ).astype(jnp.bfloat16)
    coefficients = lax.all_gather(local_coefficients, "tensor", axis=1, tiled=True)
    owner_basis = lax.dynamic_slice_in_dim(
        whole_basis, lax.axis_index("dp") * owner_rows, owner_rows, 0
    )
    token_count = grad_gate.shape[0] * data_count
    inverse_root = 1.0 / math.sqrt(token_count)
    grad = lax.psum_scatter(
        jnp.dot(coefficients, grad_gate, preferred_element_type=jnp.float32) * inverse_root,
        "dp",
        scatter_dimension=0,
        tiled=True,
    )
    first_out = BETA_ONE * first_moment + (1.0 - BETA_ONE) * grad
    second_out = BETA_TWO * second_moment + (1.0 - BETA_TWO) * grad * grad
    corrected = first_out / (1.0 - BETA_ONE**STEP)
    scaled = jnp.sqrt(second_out / (1.0 - BETA_TWO**STEP)) + EPS
    direction = (corrected / scaled).astype(jnp.bfloat16)
    update = jnp.dot(
        owner_basis,
        lax.all_gather(direction, "dp", axis=0, tiled=True),
        preferred_element_type=jnp.float32,
    ).astype(jnp.bfloat16)
    return (update, first_out, second_out)


def solution(mesh):
    placed = (
        P(("dp", "tensor"), None),
        P("dp", "tensor"),
        P(("dp", "tensor"), None),
        P("dp", "tensor"),
        P("dp", "tensor"),
    )
    return jax.shard_map(
        per_device,
        mesh=mesh,
        in_specs=placed,
        out_specs=(P("dp", "tensor"), P("dp", "tensor"), P("dp", "tensor")),
        check_vma=False,
    )
```

profile of v0, /device:TPU:1, one launch (start us, length us, event | category | flops | bytes accessed | tf_op | source)
XLA Modules:
  0.0 2139.3 jit_solution(6565265967979014289)
XLA Ops:
  7.2 0.0 copy-start
  7.2 0.0 all-gather.4.cloned.1.call-start
  7.2 0.7 all-gather.4.cloned.1.call-update
  7.9 0.0 all-reduce.3.cloned.1.call-start
  8.0 1394.2 %all-gather.4.cloned.1.call-done = bf16[8192,256]{1,0:T(8,128)(2,1)} async-done(((bf16[16,256]{1,0:T(8,128)(2,1)}), bf16[8192,256]{1,0:T(8,128)(2,1)}) %all-gather.4.cloned.1.call-update) | async-done | bytes 4194320 | tf_op jit(solution)/shard_map/all_gather | solution.py:21
  1402.1 3.3 convolution_convert_fusion.1
  1405.4 37.8 %all_gather.10 = bf16[256,384]{0,1:T(8,128)(2,1)S(1)} all-gather(bf16[256,48]{0,1:T(8,128)(2,1)S(1)} %convolution_convert_fusion.1), channel_id=1, replica_groups=mesh['dp'=64,'tensor'=8] {'tensor'}, dimensions={1}, use_global_device_ids=true | all-gather | bytes 221184 | tf_op jit(solution)/shard_map/all_gather | solution.py:25
  1443.1 0.0 copy-done
  1443.2 0.0 copy-start.1
  1443.2 0.0 copy-start.2
  1443.2 3.1 convolution_multiply_fusion
  1446.2 0.0 all-reduce.3.cloned.1.call-update
  1446.2 0.0 all-gather.6.cloned.1.call-start
  1446.3 1.3 dynamic-slice
  1448.2 557.1 %all-reduce.3.cloned.1.call-done = f32[256,3584]{1,0:T(8,128)} async-done(((f32[256,3584]{1,0:T(8,128)}), f32[256,3584]{1,0:T(8,128)}) %all-reduce.3.cloned.1.call-update) | async-done | bytes 3670032
  2005.3 0.0 copy-done.1
  2005.3 0.0 copy-done.2
  2005.3 1.6 fusion.3
  2006.9 0.0 all-gather.6.cloned.1.call-update
  2007.0 119.0 %all-gather.6.cloned.1.call-done = bf16[64,4,3584]{2,1,0:T(4,128)(2,1)} async-done(((bf16[1,4,3584]{2,1,0:T(4,128)(2,1)}), bf16[64,4,3584]{2,1,0:T(4,128)(2,1)}) %all-gather.6.cloned.1.call-update) | async-done | bytes 1835024 | tf_op jit(solution)/shard_map/all_gather | solution.py:44
  2126.0 3.9 reshape.7
  2129.9 2.9 convolution_convert_fusion
Async XLA Ops:
  7.2 1436.0 %copy-start = (bf16[384,3584]{1,0:T(8,128)(2,1)S(1)}, bf16[384,3584]{1,0:T(8,128)(2,1)}, u32[]{:S(2)}) copy-start(bf16[384,3584]{1,0:T(8,128)(2,1)} %param.6) | copy-start | bytes 8257540
  7.2 1394.9 %all-gather.4.cloned.1.call-start = ((), (), s32[]{:S(2)}) async-start(), calls=%async_computation | async-start | bytes 4202496 | tf_op jit(solution)/shard_map/all_gather | solution.py:21
  7.9 1997.4 %all-reduce.3.cloned.1.call-start = ((), (), s32[]{:S(2)}) async-start(), calls=%async_computation.2 | async-start | bytes 7340032
  1443.2 562.2 %copy-start.1 = (f32[4,3584]{1,0:T(4,128)S(1)}, f32[4,3584]{1,0:T(4,128)}, u32[]{:S(2)}) copy-start(f32[4,3584]{1,0:T(4,128)} %param.8) | copy-start | bytes 172036
  1443.2 562.2 %copy-start.2 = (f32[4,3584]{1,0:T(4,128)S(1)}, f32[4,3584]{1,0:T(4,128)}, u32[]{:S(2)}) copy-start(f32[4,3584]{1,0:T(4,128)} %param.9) | copy-start | bytes 172036
  1446.2 679.8 %all-gather.6.cloned.1.call-start = ((), (), s32[]{:S(2)}) async-start(), calls=%async_computation.1 | async-start | bytes 1863680 | tf_op jit(solution)/shard_map/all_gather | solution.py:44
Sparse Core Ops, SparseCore 0:
  10.2 1391.8 all-gather.3
  1446.4 558.9 all-reduce.2
  2008.3 117.6 all-gather.5
where the time goes:
time: 2140 us
  waiting for transfers between devices  2070 us (97%)
  blocking collectives  37.8 us (2%)
    all_gather x1, waiting for transfers between devices, per_device(): whole_basis = lax.all_gather(basis, ('dp', 'tensor'), axis=0, tiled=True)  1390 us
    unnamed x4, waiting for transfers between devices  558 us
    all_gather x1, waiting for transfers between devices, per_device(): lax.all_gather(direction, 'dp', axis=0, tiled=True)  119 us
  transfers between devices with their start and end apart: 3, of which 3 were waited for; matrix products, arithmetic and copies ran while one was open for 0% of the time, Pallas kernels for 0%

commit v1 on v0

v1 whole, which is shorter than its diff:
```python
import functools
import math

import jax
import jax.numpy as jnp
from jax import lax
from jax.experimental import pallas as pl
from jax.experimental.pallas import tpu as pltpu
from jax.sharding import Mesh
from jax.sharding import PartitionSpec as P

STEP = 10


BETA_ONE = 0.9
BETA_TWO = 0.95
EPS = 1e-08

Z, Y_LO, CORE, Y_HI, X = 8, 4, 2, 2, 4
CLASSES = CORE * X
OWNERS = Z * Y_LO
VMEM_LIMIT = 24 * 1024 * 1024
F32, BF16 = jnp.float32, jnp.bfloat16


def call(body, out_shape, flops, moved):
    return pl.pallas_call(
        body,
        out_shape=out_shape,
        compiler_params=pltpu.CompilerParams(vmem_limit_bytes=VMEM_LIMIT),
        cost_estimate=pl.CostEstimate(flops=flops, bytes_accessed=moved, transcendentals=0),
    )


def iota(shape, axis):
    return lax.broadcasted_iota(jnp.int32, shape, axis)


def one_hot(condition):
    return jnp.where(condition, 1.0, 0.0).astype(BF16)


def split_features(tokens_ref, out_ref):
    rows = tokens_ref.shape[0]
    width = Y_LO * 128
    p, q = iota((width, width), 0), iota((width, width), 1)
    place = ((p >> 4) & 3) * 128 + (p >> 7) * 32 + ((p >> 6) & 1) * 16 + (p & 15)
    move = one_hot(place == q)
    for z in range(Z):
        for core in range(CORE):
            block = jnp.concatenate(
                [
                    tokens_ref[:, pl.ds(((z * Y_LO + y) * CORE + core) * 128, 128)]
                    for y in range(Y_LO)
                ],
                axis=1,
            )
            moved = jnp.dot(block, move, preferred_element_type=F32).astype(BF16)
            for x in range(X):
                out_ref[pl.ds((core * X + x) * rows, rows), pl.ds(z * 128, 128)] = moved[
                    :, x * 128 : (x + 1) * 128
                ]


def partial_coefficients(tokens_ref, basis_ref, out_ref):
    out_ref[...] = jnp.dot(
        tokens_ref[...], basis_ref[...], preferred_element_type=F32
    ).astype(BF16)


def sum_coefficients(parts_ref, basis_ref, out_ref):
    rows = parts_ref.shape[0] // CLASSES
    own = basis_ref.shape[0]
    total = parts_ref[0:rows, :].astype(F32)
    for part in range(1, CLASSES):
        total += parts_ref[part * rows : (part + 1) * rows, :].astype(F32)
    total = total.astype(BF16)
    basis = basis_ref[...]
    count = out_ref.shape[0] // (rows + own)
    for copy in range(count):
        start = copy * (rows + own)
        out_ref[start : start + rows, :] = total
        out_ref[start + rows : start + rows + own, :] = basis


def rank_of(row, core):
    return (row >> 3) * 8 + core * 4 + (row & 3)


def project(scale, core_ref, gathered_ref, grad_ref, out_ref):
    core = core_ref[0]
    width = out_ref.shape[1]
    chunk = gathered_ref.shape[0] // 8
    tokens = chunk - 16
    coefficients = jnp.concatenate(
        [gathered_ref[t * chunk : t * chunk + tokens, :] for t in range(8)], axis=0
    )
    rank = coefficients.shape[1]
    rows = out_ref.shape[0]
    place = one_hot(rank_of(iota((rows, rank), 0), core) == iota((rows, rank), 1))
    arranged = lax.dot_general(
        place, coefficients, (((1,), (1,)), ((), ())), preferred_element_type=F32
    ).astype(BF16)
    tile = 256
    first_half = (iota((rows, tile), 0) & 4) == 0
    for start in range(0, width, tile):
        low = jnp.dot(
            arranged, grad_ref[:, start : start + tile], preferred_element_type=F32
        )
        high = jnp.dot(
            arranged,
            grad_ref[:, width + start : width + start + tile],
            preferred_element_type=F32,
        )
        out_ref[:, start : start + tile] = (
            jnp.where(first_half, low, high) * scale
        ).astype(out_ref.dtype)


def add_halves(mine_ref, theirs_ref, out_ref):
    out_ref[...] = (mine_ref[...] + theirs_ref[...].astype(F32)).astype(BF16)


def adam(parts_ref, first_ref, second_ref, first_out_ref, second_out_ref, out_ref):
    rows, width = 4, parts_ref.shape[1]
    total = parts_ref[0:16, :].astype(F32)
    for part in range(1, parts_ref.shape[0] // 16):
        total += parts_ref[part * 16 : (part + 1) * 16, :].astype(F32)
    total = total[0:8, :] + total[8:16, :]
    directions = []
    for half in range(2):
        grad = total[half * rows : (half + 1) * rows, :]
        columns = slice(half * width, (half + 1) * width)
        first_out = BETA_ONE * first_ref[:, columns] + (1.0 - BETA_ONE) * grad
        second_out = BETA_TWO * second_ref[:, columns] + (1.0 - BETA_TWO) * grad * grad
        first_out_ref[:, columns] = first_out
        second_out_ref[:, columns] = second_out
        corrected = first_out / (1.0 - BETA_ONE**STEP)
        scaled = jnp.sqrt(second_out / (1.0 - BETA_TWO**STEP)) + EPS
        directions.append(corrected / scaled)
    block = jnp.concatenate(directions + directions, axis=0).astype(BF16)
    for part in range(out_ref.shape[0] // 16):
        out_ref[part * 16 : (part + 1) * 16, :] = block


def expand(core_ref, gathered_ref, mine_ref, theirs_ref, out_ref):
    core = core_ref[0]
    chunk = gathered_ref.shape[0] // 8
    basis = jnp.concatenate(
        [gathered_ref[t * chunk + chunk - 16 : (t + 1) * chunk, :] for t in range(8)], axis=0
    )
    rank = basis.shape[1]
    width = mine_ref.shape[1]
    r, place = iota((rank, rank), 0), iota((rank, rank), 1)
    for half in range(2):
        in_half = ((place >> 2) & 1) == half
        own = one_hot((r == rank_of(place, core)) & in_half)
        other = one_hot((r == rank_of(place, 1 - core)) & in_half)
        own_basis = jnp.dot(basis, own, preferred_element_type=F32).astype(BF16)
        other_basis = jnp.dot(basis, other, preferred_element_type=F32).astype(BF16)
        tile = 256
        for start in range(0, width, tile):
            out_ref[:, half * width + start : half * width + start + tile] = (
                jnp.dot(
                    own_basis, mine_ref[:, start : start + tile], preferred_element_type=F32
                )
                + jnp.dot(
                    other_basis, theirs_ref[:, start : start + tile], preferred_element_type=F32
                )
            ).astype(BF16)


def per_device(tokens, grad_gate, basis, first_moment, second_moment):
    rows, features = tokens.shape
    own, rank = basis.shape
    group_tokens, columns = grad_gate.shape
    half_columns = columns // 2
    scale = 1.0 / math.sqrt(group_tokens * Z * Y_LO * CORE)
    shape = jax.ShapeDtypeStruct
    core = lax.axis_index("core").astype(jnp.int32)
    core_index = core.reshape(1)
    swap = [(0, 1), (1, 0)]

    basis_axes, class_axes, owner_axes = ("z", "y_lo", "y_hi"), ("core", "x"), ("z", "y_lo")
    tensor_axes = ("y_hi", "x")

    def exchange(array, axes):
        return lax.all_to_all(array, axes, 0, 0, tiled=True)

    copies = Z * Y_LO * Y_HI
    class_basis = exchange(
        jnp.broadcast_to(basis[None], (copies, own, rank)).reshape(copies * own, rank), basis_axes
    )
    split = call(
        split_features,
        shape((CLASSES * rows, features // CLASSES), BF16),
        2 * rows * features * 512,
        4 * rows * features,
    )(tokens)
    class_tokens = exchange(split, class_axes)
    parts = call(
        partial_coefficients,
        shape((CLASSES * rows, rank), BF16),
        2 * rows * features * rank,
        2 * (rows * features + copies * own * rank),
    )(class_tokens, class_basis)
    parts = exchange(parts, class_axes)
    chunk = rows + own
    summed = call(
        sum_coefficients,
        shape((8 * chunk, rank), BF16),
        CLASSES * rows * rank,
        4 * 8 * chunk * rank,
    )(parts, basis)
    gathered = exchange(summed, tensor_axes)

    smem = pl.BlockSpec(memory_space=pltpu.SMEM)
    vmem = pl.BlockSpec(memory_space=pltpu.VMEM)

    def projected(which, dtype):
        return pl.pallas_call(
            functools.partial(project, scale),
            out_shape=shape((rank, half_columns), dtype),
            in_specs=[smem, vmem, vmem],
            out_specs=vmem,
            compiler_params=pltpu.CompilerParams(vmem_limit_bytes=VMEM_LIMIT),
            cost_estimate=pl.CostEstimate(
                flops=2 * rank * group_tokens * columns,
                bytes_accessed=2 * group_tokens * columns + 2 * rank * columns,
                transcendentals=0,
            ),
        )(which, gathered, grad_gate)

    theirs = lax.ppermute(projected(1 - core_index, BF16), "core", swap)
    mine = projected(core_index, F32)
    pair = call(
        add_halves, shape((rank, half_columns), BF16), rank * half_columns, 8 * rank * half_columns
    )(mine, theirs)
    owned = exchange(pair, owner_axes)
    first_out, second_out, direction = call(
        adam,
        (
            shape(first_moment.shape, F32),
            shape(second_moment.shape, F32),
            shape((rank, half_columns), BF16),
        ),
        rank * half_columns,
        4 * rank * half_columns,
    )(owned, first_moment, second_moment)
    directions = exchange(direction, owner_axes)
    others = lax.ppermute(directions, "core", swap)
    update = pl.pallas_call(
        expand,
        out_shape=shape((own * 8, columns), BF16),
        in_specs=[smem, vmem, vmem, vmem],
        out_specs=vmem,
        compiler_params=pltpu.CompilerParams(vmem_limit_bytes=VMEM_LIMIT),
        cost_estimate=pl.CostEstimate(
            flops=4 * own * 8 * rank * columns,
            bytes_accessed=4 * rank * columns,
            transcendentals=0,
        ),
    )(core_index, gathered, directions, others)
    return (update, first_out, second_out)


def solution(mesh):
    names = ("z", "y_lo", "core", "y_hi", "x")
    fine = Mesh(mesh.devices.reshape(Z, Y_LO, CORE, Y_HI, X), names)
    data, tensor = names[:3], names[3:]
    placed = (P(names, None), P(data, tensor), P(names, None), P(data, tensor), P(data, tensor))
    return jax.shard_map(
        per_device,
        mesh=fine,
        in_specs=placed,
        out_specs=(P(data, tensor), P(data, tensor), P(data, tensor)),
        check_vma=False,
    )
```

time: 2140 us -> 159 us (0.07)
  waiting for transfers between devices: 2070 us -> 12.9 us
  blocking collectives: 37.8 us -> 123 us
    all_gather x2 -> x0, waiting for transfers between devices: 1510 us -> none  [the longest x1 1390 us: per_device(): whole_basis = lax.all_gather(basis, ('dp', 'tensor'), axis=0, tiled=True)]
    unnamed x4 -> x0, waiting for transfers between devices: 558 us -> none
    all_to_all x0 -> x5, blocking collectives: none -> 123 us  [exchange(): return lax.all_to_all(array, axes, 0, 0, tiled=True)]
    all_gather x1 -> x0, blocking collectives: 37.8 us -> none  [per_device(): lax.all_gather(local_coefficients, 'tensor', axis=1, tiled=True)]
  transfers between devices with their start and end apart: 3 -> 3, of which waited for: 3 -> 3; matrix products, arithmetic and copies ran while one was open for 0% -> 0% of each run, Pallas kernels for 0% -> 1%
where the time goes in v1:
time: 159 us
  blocking collectives  123 us (77%)
  waiting for transfers between devices  12.9 us (8%)
  starting transfers between devices  12.4 us (8%)
  Pallas kernels  8.42 us (5%)
    all_to_all x5, blocking collectives, exchange(): return lax.all_to_all(array, axes, 0, 0, tiled=True)  123 us
    all_to_all x1, waiting for transfers between devices, exchange(): return lax.all_to_all(array, axes, 0, 0, tiled=True)  10.1 us
    ppermute x1, starting transfers between devices, per_device(): others = lax.ppermute(directions, 'core', swap)  5.13 us
    ppermute x1, starting transfers between devices, per_device(): theirs = lax.ppermute(projected(1 - core_index, BF16), 'core', swap)  3.9 us
    all_to_all x1, starting transfers between devices, exchange(): return lax.all_to_all(array, axes, 0, 0, tiled=True)  3.41 us
  transfers between devices with their start and end apart: 3, of which 3 were waited for; matrix products, arithmetic and copies ran while one was open for 0% of the time, Pallas kernels for 1%

profile of v1, /device:TPU:1, one launch (start us, length us, event | category | flops | bytes accessed | tf_op | source)
XLA Modules:
  0.0 158.5 jit_solution(9807162140640394253)
XLA Ops:
  0.6 0.0 copy-start.1
  0.6 1.1 copy-done.1
  1.8 1.7 %shard_map.76 = bf16[384,1024]{1,0:T(8,128)(2,1)S(1)} custom-call(bf16[48,8192]{1,0:T(8,128)(2,1)S(1)} %copy-done.1), custom_call_target="tpu_custom_call" | custom-call | flops 402653184 | bytes 1572864 | tf_op jit(solution)/shard_map/pallas_call | solution.py:194
  3.5 0.0 copy-start
  3.5 21.7 %all_to_all.63 = bf16[8,48,1024]{2,1,0:T(8,128)(2,1)S(1)} all-to-all(bf16[8,48,1024]{2,1,0:T(8,128)(2,1)S(1)} %bitcast.20), channel_id=1, replica_groups=mesh['z'=8,'y_lo'=4,'core'=2,'y_hi'=2,'x'=4] {'core','x'}, dimensions={0} | all-to-all | bytes 1572864 | tf_op jit(solution)/shard_map/all_to_all | solution.py:188
  25.3 32.3 %all_to_all.64 = bf16[64,16,256]{2,1,0:T(8,128)(2,1)S(1)} all-to-all(bf16[64,16,256]{2,1,0:T(8,128)(2,1)S(1)} %broadcast_in_dim.2), channel_id=1, replica_groups=mesh['z'=8,'y_lo'=4,'core'=2,'y_hi'=2,'x'=4] {'z','y_lo','y_hi'}, dimensions={0} | all-to-all | bytes 1048576 | tf_op jit(solution)/shard_map/all_to_all | solution.py:188
  57.6 0.4 shard_map.77
  58.0 10.2 %all_to_all.65 = bf16[8,48,256]{2,1,0:T(8,128)(2,1)S(1)} all-to-all(bf16[8,48,256]{2,1,0:T(8,128)(2,1)S(1)} %bitcast.24), channel_id=1, replica_groups=mesh['z'=8,'y_lo'=4,'core'=2,'y_hi'=2,'x'=4] {'core','x'}, dimensions={0} | all-to-all | bytes 393216 | tf_op jit(solution)/shard_map/all_to_all | solution.py:188
  68.2 0.7 shard_map.78
  68.9 3.4 %all-to-all-start.3 = ((bf16[8,64,256]{2,1,0:T(8,128)(2,1)}), bf16[8,64,256]{2,1,0:T(8,128)(2,1)S(1)}, u32[]{:S(2)}, u32[]{:S(2)}) async-start(bf16[8,64,256]{2,1,0:T(8,128)(2,1)} %bitcast.6), calls=%async_computation.3 | async-start | bytes 524288 | tf_op jit(solution)/shard_map/all_to_all | solution.py:188
  72.3 10.1 %all-to-all-done.3 = bf16[8,64,256]{2,1,0:T(8,128)(2,1)S(1)} async-done(((bf16[8,64,256]{2,1,0:T(8,128)(2,1)}), bf16[8,64,256]{2,1,0:T(8,128)(2,1)S(1)}, u32[]{:S(2)}, u32[]{:S(2)}) %all-to-all-start.3) | async-done | bytes 262176 | tf_op jit(solution)/shard_map/all_to_all | solution.py:188
  82.4 1.3 shard_map.80
  83.8 3.9 %collective-permute-start = (bf16[256,1792]{1,0:T(8,128)(2,1)S(1)}, bf16[256,1792]{1,0:T(8,128)(2,1)S(1)}, u32[]{:S(2)}, u32[]{:S(2)}) collective-permute-start(bf16[256,1792]{1,0:T(8,128)(2,1)S(1)} %shard_map.80), channel_id=1, source_target_pairs={{0,8},{8,0},{1,9},{9,1},{2,10},{10,2},{3,11},{11,3},{4,12},{12,4},... | collective-permute-start | bytes 2752520 | tf_op jit(solution)/shard_map/ppermute | solution.py:234
  87.7 1.3 shard_map.79.mine_ref
  89.0 0.0 copy-start.2
  89.0 0.0 copy-start.3
  89.0 0.7 collective-permute-done.theirs_ref
  89.7 0.3 shard_map.81
  90.0 28.8 %all_to_all.66 = bf16[32,8,1792]{2,1,0:T(8,128)(2,1)S(1)} all-to-all(bf16[32,8,1792]{2,1,0:T(8,128)(2,1)S(1)} %bitcast.15), channel_id=1, replica_groups=mesh['z'=8,'y_lo'=4,'core'=2,'y_hi'=2,'x'=4] {'z','y_lo'}, dimensions={0} | all-to-all | bytes 1835008 | tf_op jit(solution)/shard_map/all_to_all | solution.py:188
  118.8 0.8 shard_map.82
  119.5 29.8 %all_to_all.67 = bf16[32,8,1792]{2,1,0:T(8,128)(2,1)S(1)} all-to-all(bf16[32,8,1792]{2,1,0:T(8,128)(2,1)S(1)} %bitcast.22), channel_id=1, replica_groups=mesh['z'=8,'y_lo'=4,'core'=2,'y_hi'=2,'x'=4] {'z','y_lo'}, dimensions={0} | all-to-all | bytes 1835008 | tf_op jit(solution)/shard_map/all_to_all | solution.py:188
  149.3 5.1 %collective-permute-start.1 = (bf16[256,1792]{1,0:T(8,128)(2,1)S(1)}, bf16[256,1792]{1,0:T(8,128)(2,1)S(1)}, u32[]{:S(2)}, u32[]{:S(2)}) collective-permute-start(bf16[256,1792]{1,0:T(8,128)(2,1)S(1)} %bitcast.16), channel_id=1, source_target_pairs={{0,8},{8,0},{1,9},{9,1},{2,10},{10,2},{3,11},{11,3},{4,12},{12,4},... | collective-permute-start | bytes 2752520 | tf_op jit(solution)/shard_map/ppermute | solution.py:251
  154.5 2.1 %collective-permute-done.1.theirs_ref = bf16[256,1792]{1,0:T(8,128)(2,1)S(1)} collective-permute-done((bf16[256,1792]{1,0:T(8,128)(2,1)S(1)}, bf16[256,1792]{1,0:T(8,128)(2,1)S(1)}, u32[]{:S(2)}, u32[]{:S(2)}) %collective-permute-start.1) | collective-permute-done | bytes 917536 | tf_op jit(solution)/shard_map/ppermute | solution.py:251
  156.5 2.0 %shard_map.83 = bf16[128,3584]{1,0:T(8,128)(2,1)} custom-call(s32[1]{0:T(128)} %bitcast.core_ref, bf16[512,256]{1,0:T(8,128)(2,1)S(1)} %bitcast.14, bf16[256,1792]{1,0:T(8,128)(2,1)S(1)} %bitcast.17, bf16[256,1792]{1,0:T(8,128)(2,1)S(1)} %collective-permute-done.1.theirs_ref), custom_call_target="tpu_custom_call" | custom-call | flops 469762048 | bytes 3670016 | tf_op jit(solution)/shard_map/pallas_call | solution.py:252
  (6 shorter events, 0.0 us)
Async XLA Ops:
  0.6 1.1 copy-start.1
  1.8 23.5 %copy-start.4 = (bf16[16,256]{1,0:T(8,128)(2,1)S(1)}, bf16[16,256]{1,0:T(8,128)(2,1)}, u32[]{:S(2)}) copy-start(bf16[16,256]{1,0:T(8,128)(2,1)} %basis_ref.1) | copy-start | bytes 24580
  3.5 79.0 %copy-start = (bf16[384,3584]{1,0:T(8,128)(2,1)S(1)}, bf16[384,3584]{1,0:T(8,128)(2,1)}, u32[]{:S(2)}) copy-start(bf16[384,3584]{1,0:T(8,128)(2,1)} %grad_ref.3) | copy-start | bytes 8257540
  68.9 13.5 %all-to-all-start.3 = ((bf16[8,64,256]{2,1,0:T(8,128)(2,1)}), bf16[8,64,256]{2,1,0:T(8,128)(2,1)S(1)}, u32[]{:S(2)}, u32[]{:S(2)}) async-start(bf16[8,64,256]{2,1,0:T(8,128)(2,1)} %bitcast.6), calls=%async_computation.3 | async-start | bytes 524288 | tf_op jit(solution)/shard_map/all_to_all | solution.py:188
  83.8 6.0 %collective-permute-start = (bf16[256,1792]{1,0:T(8,128)(2,1)S(1)}, bf16[256,1792]{1,0:T(8,128)(2,1)S(1)}, u32[]{:S(2)}, u32[]{:S(2)}) collective-permute-start(bf16[256,1792]{1,0:T(8,128)(2,1)S(1)} %shard_map.80), channel_id=1, source_target_pairs={{0,8},{8,0},{1,9},{9,1},{2,10},{10,2},{3,11},{11,3},{4,12},{12,4},... | collective-permute-start | bytes 2752520 | tf_op jit(solution)/shard_map/ppermute | solution.py:234
  89.0 29.8 %copy-start.2 = (f32[4,3584]{1,0:T(4,128)S(1)}, f32[4,3584]{1,0:T(4,128)}, u32[]{:S(2)}) copy-start(f32[4,3584]{1,0:T(4,128)} %first_ref.1) | copy-start | bytes 172036
  89.0 29.8 %copy-start.3 = (f32[4,3584]{1,0:T(4,128)S(1)}, f32[4,3584]{1,0:T(4,128)}, u32[]{:S(2)}) copy-start(f32[4,3584]{1,0:T(4,128)} %second_ref.1) | copy-start | bytes 172036
  149.3 7.2 %collective-permute-start.1 = (bf16[256,1792]{1,0:T(8,128)(2,1)S(1)}, bf16[256,1792]{1,0:T(8,128)(2,1)S(1)}, u32[]{:S(2)}, u32[]{:S(2)}) collective-permute-start(bf16[256,1792]{1,0:T(8,128)(2,1)S(1)} %bitcast.16), channel_id=1, source_target_pairs={{0,8},{8,0},{1,9},{9,1},{2,10},{10,2},{3,11},{11,3},{4,12},{12,4},... | collective-permute-start | bytes 2752520 | tf_op jit(solution)/shard_map/ppermute | solution.py:251

commit v2 on v0

v2 whole, which is shorter than its diff:
```python
import functools
import math

import jax
import jax.numpy as jnp
from jax import lax
from jax.experimental import pallas as pl
from jax.experimental.pallas import tpu as pltpu
from jax.sharding import Mesh
from jax.sharding import PartitionSpec as P

STEP = 10


BETA_ONE = 0.9
BETA_TWO = 0.95
EPS = 1e-08

Z, Y_LO, CORE, Y_HI, X = 8, 4, 2, 2, 4
CLASSES = CORE * X
OWNERS = Z * Y_LO
SPLIT_FLOPS = 2 * 48 * 8192 * 512
VMEM_LIMIT = 24 * 1024 * 1024
F32, BF16 = jnp.float32, jnp.bfloat16


def call(body, out_shape, flops, moved, placed=False):
    vmem = pl.BlockSpec(memory_space=pltpu.VMEM)
    smem = pl.BlockSpec(memory_space=pltpu.SMEM)

    def run(*operands):
        specs = [smem if placed and n == 0 else vmem for n in range(len(operands))]
        return pl.pallas_call(
            body,
            out_shape=out_shape,
            in_specs=specs,
            out_specs=jax.tree.map(lambda _: vmem, out_shape),
            compiler_params=pltpu.CompilerParams(vmem_limit_bytes=VMEM_LIMIT),
            cost_estimate=pl.CostEstimate(flops=flops, bytes_accessed=moved, transcendentals=0),
        )(*operands)

    return run


def iota(shape, axis):
    return lax.broadcasted_iota(jnp.int32, shape, axis)


def one_hot(condition):
    return jnp.where(condition, 1.0, 0.0).astype(BF16)


def split_features(at_ref, tokens_ref, *out_refs):
    core, here = at_ref[0], at_ref[1]
    width = Y_LO * 128
    p, q = iota((width, width), 0), iota((width, width), 1)
    steps = (((p >> 4) & 3) - here) & 3
    move = one_hot(steps * 128 + (p >> 7) * 32 + ((p >> 6) & 1) * 16 + (p & 15) == q)
    for z in range(Z):
        for step in range(CORE):
            side = core if step == 0 else 1 - core
            block = jnp.concatenate(
                [
                    tokens_ref[
                        :,
                        pl.ds(pl.multiple_of((z * Y_LO + y) * CORE * 128 + side * 128, 128), 128),
                    ]
                    for y in range(Y_LO)
                ],
                axis=1,
            )
            moved = jnp.dot(block, move, preferred_element_type=F32).astype(BF16)
            for x in range(X):
                out_refs[x][step, :, z * 128 : (z + 1) * 128] = moved[:, x * 128 : (x + 1) * 128]


def partial_coefficients(at_ref, basis_ref, sibling_ref, *refs):
    *token_refs, out_ref = refs
    core, here = at_ref[0], at_ref[1]
    rows = sibling_ref.shape[1]
    tokens = jnp.concatenate(
        [ref[0] for ref in token_refs] + [sibling_ref[step] for step in range(X)], axis=0
    )
    parts = jnp.dot(tokens, basis_ref[...], preferred_element_type=F32).astype(out_ref.dtype)
    for source in range(CLASSES):
        side = core if source < X else 1 - core
        place = side * X + ((here - source) & 3)
        out_ref[place] = parts[source * rows : (source + 1) * rows, :]


def sum_coefficients(parts_ref, basis_ref, out_ref):
    rows = parts_ref.shape[1]
    own = basis_ref.shape[0]
    total = parts_ref[0].astype(F32)
    for part in range(1, CLASSES):
        total += parts_ref[part].astype(F32)
    total = total.astype(BF16)
    basis = basis_ref[...]
    for copy in range(out_ref.shape[0]):
        out_ref[copy, 0:rows, :] = total
        out_ref[copy, rows : rows + own, :] = basis


def project(scale, at_ref, gathered_ref, grad_ref, other_ref, out_ref):
    core = at_ref[0]
    rank, width = out_ref.shape
    rows = gathered_ref.shape[1] - 16
    eye = one_hot(iota((rank, rank), 0) == iota((rank, rank), 1))

    def coefficients(side):
        stacked = jnp.concatenate(
            [gathered_ref[side * 8 + t, 0:rows, :] for t in range(8)], axis=0
        )
        return lax.dot_general(
            eye, stacked, (((1,), (1,)), ((), ())), preferred_element_type=F32
        ).astype(BF16)

    own, other = coefficients(core), coefficients(1 - core)
    tile = 256
    for start in range(0, width, tile):
        columns = pl.ds(pl.multiple_of(core * width + start, 128), tile)
        total = jnp.dot(own, grad_ref[:, columns], preferred_element_type=F32) + jnp.dot(
            other, other_ref[:, start : start + tile], preferred_element_type=F32
        )
        out_ref[:, start : start + tile] = (total * scale).astype(BF16)


def adam(
    at_ref, parts_ref, moments_ref, other_ref, kept_ref, sent_ref, out_ref
):
    core = at_ref[0]
    rows = 4
    total = parts_ref[0:16, :].astype(F32)
    for part in range(1, parts_ref.shape[0] // 16):
        total += parts_ref[part * 16 : (part + 1) * 16, :].astype(F32)
    grad = total[0:8, :] + total[8:16, :]

    def both(own, other):
        return jnp.where(
            core == 0,
            jnp.concatenate([own, other], axis=0),
            jnp.concatenate([other, own], axis=0),
        )

    first = both(moments_ref[0:rows, :], other_ref[0:rows, :])
    second = both(moments_ref[rows : 2 * rows, :], other_ref[rows : 2 * rows, :])
    first_out = BETA_ONE * first + (1.0 - BETA_ONE) * grad
    second_out = BETA_TWO * second + (1.0 - BETA_TWO) * grad * grad
    corrected = first_out / (1.0 - BETA_ONE**STEP)
    scaled = jnp.sqrt(second_out / (1.0 - BETA_TWO**STEP)) + EPS
    direction = corrected / scaled
    low = jnp.concatenate([first_out[0:rows, :], second_out[0:rows, :]], axis=0)
    high = jnp.concatenate([first_out[rows:, :], second_out[rows:, :]], axis=0)
    kept_ref[...] = jnp.where(core == 0, low, high)
    sent_ref[...] = jnp.where(core == 0, high, low)
    block = jnp.concatenate([direction, direction], axis=0).astype(BF16)
    for part in range(out_ref.shape[0] // 16):
        out_ref[part * 16 : (part + 1) * 16, :] = block


def group_basis(gathered_ref, side):
    rows = gathered_ref.shape[1]
    return jnp.concatenate(
        [gathered_ref[side * 8 + t, rows - 16 : rows, :] for t in range(8)], axis=0
    )


def expand_sent(
    at_ref, gathered_ref, directions_ref, kept_ref, other_ref, out_ref, first_ref, second_ref
):
    core = at_ref[0]
    basis = group_basis(gathered_ref, 1 - core)
    width = out_ref.shape[1]
    tile = 256
    for start in range(0, width, tile):
        out_ref[:, start : start + tile] = jnp.dot(
            basis, directions_ref[:, start : start + tile], preferred_element_type=F32
        ).astype(BF16)
    mine = pl.ds(pl.multiple_of(core * width, 128), width)
    theirs = pl.ds(pl.multiple_of((1 - core) * width, 128), width)
    first_ref[:, mine] = kept_ref[0:4, :]
    first_ref[:, theirs] = other_ref[0:4, :]
    second_ref[:, mine] = kept_ref[4:8, :]
    second_ref[:, theirs] = other_ref[4:8, :]


def expand(at_ref, gathered_ref, directions_ref, received_ref, out_ref):
    core = at_ref[0]
    basis = group_basis(gathered_ref, core)
    width = received_ref.shape[1]
    tile = 256
    for start in range(0, width, tile):
        mine = pl.ds(pl.multiple_of(core * width + start, 128), tile)
        theirs = pl.ds(pl.multiple_of((1 - core) * width + start, 128), tile)
        out_ref[:, mine] = jnp.dot(
            basis, directions_ref[:, start : start + tile], preferred_element_type=F32
        ).astype(BF16)
        out_ref[:, theirs] = received_ref[:, start : start + tile]


def per_device(tokens, grad_gate, basis, first_moment, second_moment):
    rows, features = tokens.shape
    own, rank = basis.shape
    group_tokens, columns = grad_gate.shape
    half = columns // 2
    moment_rows = first_moment.shape[0]
    scale = 1.0 / math.sqrt(group_tokens * Z * Y_LO * CORE)
    shape = jax.ShapeDtypeStruct
    core = lax.axis_index("core").astype(jnp.int32)
    at = jnp.stack([core, lax.axis_index("x").astype(jnp.int32)])
    swap = [(0, 1), (1, 0)]

    def exchange(array, axes):
        return lax.all_to_all(array, axes, 0, 0, tiled=True)

    def half_of(array, side):
        return lax.dynamic_slice_in_dim(array, side * half, half, 1)

    copies = Z * Y_LO * Y_HI
    class_basis = exchange(
        jnp.broadcast_to(basis[None], (copies, own, rank)), ("z", "y_lo", "y_hi")
    ).reshape(copies * own, rank)

    block = shape((CORE, rows, features // CLASSES), BF16)
    blocks = call(split_features, (block,) * X, SPLIT_FLOPS, 0, True)(at, tokens)
    held = [blocks[0]] + [
        lax.ppermute(blocks[step], "x", [(x, (x + step) % X) for x in range(X)])
        for step in range(1, X)
    ]
    sibling = lax.ppermute(jnp.stack([each[1] for each in held]), "core", swap)
    other_grad = lax.ppermute(half_of(grad_gate, 1 - core), "core", swap)
    moments = jnp.concatenate([first_moment, second_moment], axis=0)
    other_moments = lax.ppermute(half_of(moments, 1 - core), "core", swap)
    own_moments = half_of(moments, core)

    parts = call(
        partial_coefficients,
        shape((CLASSES, rows, rank), BF16),
        2 * rows * features * rank,
        2 * (rows * features + copies * own * rank),
        True,
    )(at, class_basis, sibling, *held)
    parts = exchange(parts, ("core", "x"))
    takers = CORE * Y_HI * X
    summed = call(
        sum_coefficients,
        shape((takers, rows + own, rank), BF16),
        CLASSES * rows * rank,
        2 * takers * (rows + own) * rank,
    )(parts, basis)
    gathered = exchange(summed, ("core", "y_hi", "x"))
    pair = call(
        functools.partial(project, scale),
        shape((rank, half), BF16),
        2 * rank * group_tokens * columns,
        2 * group_tokens * columns,
        True,
    )(at, gathered, grad_gate, other_grad)
    owned = exchange(pair, ("z", "y_lo"))
    kept, sent, direction = call(
        adam,
        (
            shape((2 * moment_rows, half), F32),
            shape((2 * moment_rows, half), F32),
            shape((rank, half), BF16),
        ),
        rank * half,
        4 * rank * half,
        True,
    )(at, owned, own_moments, other_moments)
    directions = exchange(direction, ("z", "y_lo"))
    other = lax.ppermute(sent, "core", swap)
    update_rows = own * Y_HI * X
    to_send, first_out, second_out = call(
        expand_sent,
        (
            shape((update_rows, half), BF16),
            shape(first_moment.shape, F32),
            shape(second_moment.shape, F32),
        ),
        2 * update_rows * rank * half,
        2 * rank * half,
        True,
    )(at, gathered, directions, kept, other)
    received = lax.ppermute(to_send, "core", swap)
    update = call(
        expand,
        shape((update_rows, columns), BF16),
        2 * update_rows * rank * half,
        2 * rank * columns,
        True,
    )(at, gathered, directions, received)
    return (update, first_out, second_out)


def solution(mesh):
    names = ("z", "y_lo", "core", "y_hi", "x")
    fine = Mesh(mesh.devices.reshape(Z, Y_LO, CORE, Y_HI, X), names)
    data, tensor = names[:3], names[3:]
    placed = (P(names, None), P(data, tensor), P(names, None), P(data, tensor), P(data, tensor))
    return jax.shard_map(
        per_device,
        mesh=fine,
        in_specs=placed,
        out_specs=(P(data, tensor), P(data, tensor), P(data, tensor)),
        check_vma=False,
    )
```

time: 2140 us -> 167 us (0.08)
  waiting for transfers between devices: 2070 us -> 59.9 us
  starting transfers between devices: 0.12 us -> 70.8 us
  blocking collectives: 37.8 us -> 10.5 us
    all_gather x2 -> x0, waiting for transfers between devices: 1510 us -> none  [the longest x1 1390 us: per_device(): whole_basis = lax.all_gather(basis, ('dp', 'tensor'), axis=0, tiled=True)]
    unnamed x4 -> x0, waiting for transfers between devices: 558 us -> none
    all_to_all x0 -> x4, waiting for transfers between devices: none -> 54.3 us  [exchange(): return lax.all_to_all(array, axes, 0, 0, tiled=True)]
    all_to_all x0 -> x4, starting transfers between devices: none -> 43.2 us  [exchange(): return lax.all_to_all(array, axes, 0, 0, tiled=True)]
    all_gather x1 -> x0, blocking collectives: 37.8 us -> none  [per_device(): lax.all_gather(local_coefficients, 'tensor', axis=1, tiled=True)]
    ppermute x0 -> x8, starting transfers between devices: none -> 27.5 us  [the longest x3 10.5 us: per_device(): lax.ppermute(blocks[step], 'x', [(x, (x + step) % X) for x in range(X)])]
  transfers between devices with their start and end apart: 3 -> 12, of which waited for: 3 -> 8; matrix products, arithmetic and copies ran while one was open for 0% -> 3% of each run, Pallas kernels for 0% -> 3%
where the time goes in v2:
time: 167 us; the launch traced here: 166 us
  starting transfers between devices  70.8 us (42%)
  waiting for transfers between devices  59.9 us (36%)
  Pallas kernels  12.3 us (7%)
  local copies, waits for them, and re-layouts  10.7 us (6%)
  blocking collectives  10.5 us (6%)
    all_to_all x4, waiting for transfers between devices, exchange(): return lax.all_to_all(array, axes, 0, 0, tiled=True)  54.3 us
    all_to_all x4, starting transfers between devices, exchange(): return lax.all_to_all(array, axes, 0, 0, tiled=True)  43.2 us
    pallas_call x7, Pallas kernels, run(): pl.pallas_call(body, out_shape=out_shape, in_specs=specs, out_specs=jax.t...  12.3 us
    ppermute x3, starting transfers between devices, per_device(): lax.ppermute(blocks[step], 'x', [(x, (x + step) % X) for x in range(X)])  10.5 us
    all_to_all x1, blocking collectives, exchange(): return lax.all_to_all(array, axes, 0, 0, tiled=True)  10.5 us
    ppermute x1, starting transfers between devices, per_device(): received = lax.ppermute(to_send, 'core', swap)  5.16 us
    unnamed x18, local copies, waits for them, and re-layouts  4.59 us
    ppermute x1, starting transfers between devices, per_device(): sibling = lax.ppermute(jnp.stack([each[1] for each in held]), 'core', swap)  3.93 us
  transfers between devices with their start and end apart: 12, of which 8 were waited for; matrix products, arithmetic and copies ran while one was open for 3% of the time, Pallas kernels for 3%

profile of v2, /device:TPU:1, one launch (start us, length us, event | category | flops | bytes accessed | tf_op | source)
XLA Modules:
  0.0 166.1 jit_solution(12901991082146283232)
XLA Ops:
  0.6 1.5 broadcast_in_dim.2
  2.2 17.1 %all-to-all-start = ((bf16[64,16,256]{2,1,0:T(8,128)(2,1)}), bf16[64,16,256]{2,1,0:T(8,128)(2,1)S(1)}, u32[]{:S(2)}, u32[]{:S(2)}) async-start(bf16[64,16,256]{2,1,0:T(8,128)(2,1)} %broadcast_in_dim.2), calls=%async_computation | async-start | bytes 1048576 | tf_op jit(solution)/shard_map/all_to_all | solution.py:214
  20.5 3.1 %shard_map.76 = (bf16[2,48,1024]{2,1,0:T(8,128)(2,1)S(1)}, bf16[2,48,1024]{2,1,0:T(8,128)(2,1)}, bf16[2,48,1024]{2,1,0:T(8,128)(2,1)}, bf16[2,48,1024]{2,1,0:T(8,128)(2,1)}) custom-call(s32[2]{0:T(128)S(1)} %pad_add_fusion.at_ref, bf16[48,8192]{1,0:T(8,128)(2,1)S(1)} %copy-done.6), custom_call_target="tpu_custom_call" | custom-call | flops 402653184 | tf_op jit(solution)/shard_map/pallas_call | solution.py:33
  23.7 3.1 %collective-permute-start = (bf16[2,48,1024]{2,1,0:T(8,128)(2,1)}, bf16[2,48,1024]{2,1,0:T(8,128)(2,1)}, u32[]{:S(2)}, u32[]{:S(2)}) collective-permute-start(bf16[2,48,1024]{2,1,0:T(8,128)(2,1)} %get-tuple-element.14), channel_id=1, source_target_pairs={{0,1},{1,2},{2,3},{3,0},{4,5},{5,6},{6,7},{7,4},{8,9},{9,10},{10,1... | collective-permute-start | bytes 589832 | tf_op jit(solution)/shard_map/ppermute | solution.py:227
  26.8 4.4 %collective-permute-start.1 = (bf16[2,48,1024]{2,1,0:T(8,128)(2,1)}, bf16[2,48,1024]{2,1,0:T(8,128)(2,1)}, u32[]{:S(2)}, u32[]{:S(2)}) collective-permute-start(bf16[2,48,1024]{2,1,0:T(8,128)(2,1)} %get-tuple-element.15), channel_id=1, source_target_pairs={{0,2},{1,3},{2,0},{3,1},{4,6},{5,7},{6,4},{7,5},{8,10},{9,11},{10,... | collective-permute-start | bytes 589832 | tf_op jit(solution)/shard_map/ppermute | solution.py:227
  31.1 3.1 %collective-permute-start.2 = (bf16[2,48,1024]{2,1,0:T(8,128)(2,1)}, bf16[2,48,1024]{2,1,0:T(8,128)(2,1)}, u32[]{:S(2)}, u32[]{:S(2)}) collective-permute-start(bf16[2,48,1024]{2,1,0:T(8,128)(2,1)} %get-tuple-element.16), channel_id=1, source_target_pairs={{0,3},{1,0},{2,1},{3,2},{4,7},{5,4},{6,5},{7,6},{8,11},{9,8},{10,9... | collective-permute-start | bytes 589832 | tf_op jit(solution)/shard_map/ppermute | solution.py:227
  35.8 1.9 %collective-permute-done.1.refs_2_ = bf16[2,48,1024]{2,1,0:T(8,128)(2,1)} collective-permute-done((bf16[2,48,1024]{2,1,0:T(8,128)(2,1)}, bf16[2,48,1024]{2,1,0:T(8,128)(2,1)}, u32[]{:S(2)}, u32[]{:S(2)}) %collective-permute-start.1) | collective-permute-done | bytes 196640 | tf_op jit(solution)/shard_map/ppermute | solution.py:227
  40.9 3.9 %collective-permute-start.3 = (bf16[4,48,1024]{2,1,0:T(8,128)(2,1)S(1)}, bf16[4,48,1024]{2,1,0:T(8,128)(2,1)S(1)}, u32[]{:S(2)}, u32[]{:S(2)}) collective-permute-start(bf16[4,48,1024]{2,1,0:T(8,128)(2,1)S(1)} %pad_maximum_fusion), channel_id=1, source_target_pairs={{0,8},{8,0},{1,9},{9,1},{2,10},{10,2},{3,11},{11,3},{4,12},{12,4},... | collective-permute-start | bytes 1179656 | tf_op jit(solution)/shard_map/ppermute | solution.py:230
  46.1 1.9 %collective-permute-start.4 = (bf16[384,1792]{1,0:T(8,128)(2,1)}, bf16[384,1792]{1,0:T(8,128)(2,1)}, u32[]{:S(2)}, u32[]{:S(2)}) collective-permute-start(bf16[384,1792]{1,0:T(8,128)(2,1)} %constant_dynamic-slice_fusion), channel_id=1, source_target_pairs={{0,8},{8,0},{1,9},{9,1},{2,10},{10,2},{3,11},{11,3},{4,12},{12,4},... | collective-permute-start | bytes 4128776 | tf_op jit(solution)/shard_map/ppermute | solution.py:231
  49.8 1.5 shard_map.77
  51.3 10.5 %all_to_all.37.parts_ref = bf16[8,48,256]{2,1,0:T(8,128)(2,1)S(1)} all-to-all(bf16[8,48,256]{2,1,0:T(8,128)(2,1)S(1)} %shard_map.77), channel_id=1, replica_groups=mesh['z'=8,'y_lo'=4,'core'=2,'y_hi'=2,'x'=4] {'core','x'}, dimensions={0} | all-to-all | bytes 393216 | tf_op jit(solution)/shard_map/all_to_all | solution.py:214
  62.6 8.0 %all-to-all-start.2 = ((bf16[16,64,256]{2,1,0:T(8,128)(2,1)}), bf16[16,64,256]{2,1,0:T(8,128)(2,1)S(1)}, u32[]{:S(2)}, u32[]{:S(2)}) async-start(bf16[16,64,256]{2,1,0:T(8,128)(2,1)} %copy-done.2), calls=%async_computation.2 | async-start | bytes 1048576 | tf_op jit(solution)/shard_map/all_to_all | solution.py:214
  70.7 16.6 %all-to-all-done.2.gathered_ref = bf16[16,64,256]{2,1,0:T(8,128)(2,1)S(1)} async-done(((bf16[16,64,256]{2,1,0:T(8,128)(2,1)}), bf16[16,64,256]{2,1,0:T(8,128)(2,1)S(1)}, u32[]{:S(2)}, u32[]{:S(2)}) %all-to-all-start.2) | async-done | bytes 524320 | tf_op jit(solution)/shard_map/all_to_all | solution.py:214
  87.3 2.8 %shard_map.79 = bf16[256,1792]{1,0:T(8,128)(2,1)S(1)} custom-call(s32[2]{0:T(128)S(1)} %pad_add_fusion.at_ref, bf16[16,64,256]{2,1,0:T(8,128)(2,1)S(1)} %all-to-all-done.2.gathered_ref, bf16[384,3584]{1,0:T(8,128)(2,1)S(1)} %copy-done, bf16[384,1792]{1,0:T(8,128)(2,1)} %collective-permute-done.4.other_ref), custom_call_target="tpu_custom_call" | custom-call | flops 704643072 | bytes 2752512 | tf_op jit(solution)/shard_map/pallas_call | solution.py:33
  91.0 10.6 %all-to-all-start.3 = ((bf16[32,8,1792]{2,1,0:T(8,128)(2,1)}), bf16[32,8,1792]{2,1,0:T(8,128)(2,1)S(1)}, u32[]{:S(2)}, u32[]{:S(2)}) async-start(bf16[32,8,1792]{2,1,0:T(8,128)(2,1)} %bitcast.10), calls=%async_computation.3 | async-start | bytes 1835008 | tf_op jit(solution)/shard_map/all_to_all | solution.py:214
  101.8 2.6 %collective-permute-start.5 = (f32[8,1792]{1,0:T(8,128)S(1)}, f32[8,1792]{1,0:T(8,128)S(1)}, u32[]{:S(2)}, u32[]{:S(2)}) collective-permute-start(f32[8,1792]{1,0:T(8,128)S(1)} %get-tuple-element.23), channel_id=1, source_target_pairs={{0,8},{8,0},{1,9},{9,1},{2,10},{10,2},{3,11},{11,3},{4,12},{12,4},... | collective-permute-start | bytes 172040 | tf_op jit(solution)/shard_map/ppermute | solution.py:233
  105.3 19.4 %all-to-all-done.3 = bf16[32,8,1792]{2,1,0:T(8,128)(2,1)S(1)} async-done(((bf16[32,8,1792]{2,1,0:T(8,128)(2,1)}), bf16[32,8,1792]{2,1,0:T(8,128)(2,1)S(1)}, u32[]{:S(2)}, u32[]{:S(2)}) %all-to-all-start.3) | async-done | bytes 917536 | tf_op jit(solution)/shard_map/all_to_all | solution.py:214
  124.6 1.7 %shard_map.80 = (f32[8,1792]{1,0:T(8,128)S(1)}, f32[8,1792]{1,0:T(8,128)S(1)}, bf16[256,1792]{1,0:T(8,128)(2,1)}) custom-call(s32[2]{0:T(128)S(1)} %pad_add_fusion.at_ref, bf16[256,1792]{1,0:T(8,128)(2,1)S(1)} %bitcast.9, f32[8,1792]{1,0:T(8,128)S(1)} %get-tuple-element.24.moments_ref, f32[8,1792]{1,0:T(8,128)S(1)} %collective-permute-done.5.other_ref), custom_call_target="tpu_custom_call" | custom-call | flops 458752 | bytes 1835008 | tf_op jit(solution)/shard_map/pallas_call | solution.py:33
  126.3 7.4 %all-to-all-start.4 = ((bf16[32,8,1792]{2,1,0:T(8,128)(2,1)}), bf16[32,8,1792]{2,1,0:T(8,128)(2,1)S(1)}, u32[]{:S(2)}, u32[]{:S(2)}) async-start(bf16[32,8,1792]{2,1,0:T(8,128)(2,1)} %bitcast.5), calls=%async_computation.4 | async-start | bytes 1835008 | tf_op jit(solution)/shard_map/all_to_all | solution.py:214
  133.7 3.4 %collective-permute-start.6 = (f32[8,1792]{1,0:T(8,128)S(1)}, f32[8,1792]{1,0:T(8,128)S(1)}, u32[]{:S(2)}, u32[]{:S(2)}) collective-permute-start(f32[8,1792]{1,0:T(8,128)S(1)} %get-tuple-element.19), channel_id=1, source_target_pairs={{0,8},{8,0},{1,9},{9,1},{2,10},{10,2},{3,11},{11,3},{4,12},{12,4},... | collective-permute-start | bytes 172040 | tf_op jit(solution)/shard_map/ppermute | solution.py:272
  138.0 18.3 %all-to-all-done.4 = bf16[32,8,1792]{2,1,0:T(8,128)(2,1)S(1)} async-done(((bf16[32,8,1792]{2,1,0:T(8,128)(2,1)}), bf16[32,8,1792]{2,1,0:T(8,128)(2,1)S(1)}, u32[]{:S(2)}, u32[]{:S(2)}) %all-to-all-start.4) | async-done | bytes 917536 | tf_op jit(solution)/shard_map/all_to_all | solution.py:214
  157.7 5.2 %collective-permute-start.7 = (bf16[128,1792]{1,0:T(8,128)(2,1)S(1)}, bf16[128,1792]{1,0:T(8,128)(2,1)S(1)}, u32[]{:S(2)}, u32[]{:S(2)}) collective-permute-start(bf16[128,1792]{1,0:T(8,128)(2,1)S(1)} %get-tuple-element.20), channel_id=1, source_target_pairs={{0,8},{8,0},{1,9},{9,1},{2,10},{10,2},{3,11},{11,3},{4,12},{12,4},... | collective-permute-start | bytes 1376264 | tf_op jit(solution)/shard_map/ppermute | solution.py:285
  162.9 1.4 collective-permute-done.7.received_ref
  164.3 1.8 %shard_map.82 = bf16[128,3584]{1,0:T(8,128)(2,1)} custom-call(s32[2]{0:T(128)S(1)} %pad_add_fusion.at_ref, bf16[16,64,256]{2,1,0:T(8,128)(2,1)S(1)} %all-to-all-done.2.gathered_ref, bf16[256,1792]{1,0:T(8,128)(2,1)S(1)} %bitcast.8, bf16[128,1792]{1,0:T(8,128)(2,1)S(1)} %collective-permute-done.7.received_ref), custom_call_target="tpu_custom_call" | custom-call | flops 117440512 | bytes 1835008 | tf_op jit(solution)/shard_map/pallas_call | solution.py:33
  (35 shorter events, 13.9 us)
Async XLA Ops:
  2.2 46.6 %all-to-all-start = ((bf16[64,16,256]{2,1,0:T(8,128)(2,1)}), bf16[64,16,256]{2,1,0:T(8,128)(2,1)S(1)}, u32[]{:S(2)}, u32[]{:S(2)}) async-start(bf16[64,16,256]{2,1,0:T(8,128)(2,1)} %broadcast_in_dim.2), calls=%async_computation | async-start | bytes 1048576 | tf_op jit(solution)/shard_map/all_to_all | solution.py:214
  19.4 1.1 copy-start.6
  20.5 24.3 %copy-start = (bf16[384,3584]{1,0:T(8,128)(2,1)S(1)}, bf16[384,3584]{1,0:T(8,128)(2,1)}, u32[]{:S(2)}) copy-start(bf16[384,3584]{1,0:T(8,128)(2,1)} %grad_ref.1) | copy-start | bytes 8257540
  23.7 11.2 %collective-permute-start = (bf16[2,48,1024]{2,1,0:T(8,128)(2,1)}, bf16[2,48,1024]{2,1,0:T(8,128)(2,1)}, u32[]{:S(2)}, u32[]{:S(2)}) collective-permute-start(bf16[2,48,1024]{2,1,0:T(8,128)(2,1)} %get-tuple-element.14), channel_id=1, source_target_pairs={{0,1},{1,2},{2,3},{3,0},{4,5},{5,6},{6,7},{7,4},{8,9},{9,10},{10,1... | collective-permute-start | bytes 589832 | tf_op jit(solution)/shard_map/ppermute | solution.py:227
  26.8 10.9 %collective-permute-start.1 = (bf16[2,48,1024]{2,1,0:T(8,128)(2,1)}, bf16[2,48,1024]{2,1,0:T(8,128)(2,1)}, u32[]{:S(2)}, u32[]{:S(2)}) collective-permute-start(bf16[2,48,1024]{2,1,0:T(8,128)(2,1)} %get-tuple-element.15), channel_id=1, source_target_pairs={{0,2},{1,3},{2,0},{3,1},{4,6},{5,7},{6,4},{7,5},{8,10},{9,11},{10,... | collective-permute-start | bytes 589832 | tf_op jit(solution)/shard_map/ppermute | solution.py:227
  31.1 7.9 %collective-permute-start.2 = (bf16[2,48,1024]{2,1,0:T(8,128)(2,1)}, bf16[2,48,1024]{2,1,0:T(8,128)(2,1)}, u32[]{:S(2)}, u32[]{:S(2)}) collective-permute-start(bf16[2,48,1024]{2,1,0:T(8,128)(2,1)} %get-tuple-element.16), channel_id=1, source_target_pairs={{0,3},{1,0},{2,1},{3,2},{4,7},{5,4},{6,5},{7,6},{8,11},{9,8},{10,9... | collective-permute-start | bytes 589832 | tf_op jit(solution)/shard_map/ppermute | solution.py:227
  40.9 7.1 %collective-permute-start.3 = (bf16[4,48,1024]{2,1,0:T(8,128)(2,1)S(1)}, bf16[4,48,1024]{2,1,0:T(8,128)(2,1)S(1)}, u32[]{:S(2)}, u32[]{:S(2)}) collective-permute-start(bf16[4,48,1024]{2,1,0:T(8,128)(2,1)S(1)} %pad_maximum_fusion), channel_id=1, source_target_pairs={{0,8},{8,0},{1,9},{9,1},{2,10},{10,2},{3,11},{11,3},{4,12},{12,4},... | collective-permute-start | bytes 1179656 | tf_op jit(solution)/shard_map/ppermute | solution.py:230
  44.9 16.9 %copy-start.5 = (bf16[16,256]{1,0:T(8,128)(2,1)S(1)}, bf16[16,256]{1,0:T(8,128)(2,1)}, u32[]{:S(2)}) copy-start(bf16[16,256]{1,0:T(8,128)(2,1)} %basis_ref.1) | copy-start | bytes 24580
  46.1 24.6 %collective-permute-start.4 = (bf16[384,1792]{1,0:T(8,128)(2,1)}, bf16[384,1792]{1,0:T(8,128)(2,1)}, u32[]{:S(2)}, u32[]{:S(2)}) collective-permute-start(bf16[384,1792]{1,0:T(8,128)(2,1)} %constant_dynamic-slice_fusion), channel_id=1, source_target_pairs={{0,8},{8,0},{1,9},{9,1},{2,10},{10,2},{3,11},{11,3},{4,12},{12,4},... | collective-permute-start | bytes 4128776 | tf_op jit(solution)/shard_map/ppermute | solution.py:231
  48.0 0.7 copy-start.3
  48.8 1.0 copy-start.4
  61.8 0.8 copy-start.2
  62.6 24.7 %all-to-all-start.2 = ((bf16[16,64,256]{2,1,0:T(8,128)(2,1)}), bf16[16,64,256]{2,1,0:T(8,128)(2,1)S(1)}, u32[]{:S(2)}, u32[]{:S(2)}) async-start(bf16[16,64,256]{2,1,0:T(8,128)(2,1)} %copy-done.2), calls=%async_computation.2 | async-start | bytes 1048576 | tf_op jit(solution)/shard_map/all_to_all | solution.py:214
  90.1 0.9 copy-start.1
  91.0 10.7 %copy-start.7 = (f32[4,3584]{1,0:T(4,128)S(1)}, f32[4,3584]{1,0:T(4,128)}, u32[]{:S(2)}) copy-start(f32[4,3584]{1,0:T(4,128)} %param.8) | copy-start | bytes 172036
  91.0 10.7 %copy-start.8 = (f32[4,3584]{1,0:T(4,128)S(1)}, f32[4,3584]{1,0:T(4,128)}, u32[]{:S(2)}) copy-start(f32[4,3584]{1,0:T(4,128)} %param.9) | copy-start | bytes 172036
  91.0 33.6 %all-to-all-start.3 = ((bf16[32,8,1792]{2,1,0:T(8,128)(2,1)}), bf16[32,8,1792]{2,1,0:T(8,128)(2,1)S(1)}, u32[]{:S(2)}, u32[]{:S(2)}) async-start(bf16[32,8,1792]{2,1,0:T(8,128)(2,1)} %bitcast.10), calls=%async_computation.3 | async-start | bytes 1835008 | tf_op jit(solution)/shard_map/all_to_all | solution.py:214
  101.8 3.5 %collective-permute-start.5 = (f32[8,1792]{1,0:T(8,128)S(1)}, f32[8,1792]{1,0:T(8,128)S(1)}, u32[]{:S(2)}, u32[]{:S(2)}) collective-permute-start(f32[8,1792]{1,0:T(8,128)S(1)} %get-tuple-element.23), channel_id=1, source_target_pairs={{0,8},{8,0},{1,9},{9,1},{2,10},{10,2},{3,11},{11,3},{4,12},{12,4},... | collective-permute-start | bytes 172040 | tf_op jit(solution)/shard_map/ppermute | solution.py:233
  126.3 30.0 %all-to-all-start.4 = ((bf16[32,8,1792]{2,1,0:T(8,128)(2,1)}), bf16[32,8,1792]{2,1,0:T(8,128)(2,1)S(1)}, u32[]{:S(2)}, u32[]{:S(2)}) async-start(bf16[32,8,1792]{2,1,0:T(8,128)(2,1)} %bitcast.5), calls=%async_computation.4 | async-start | bytes 1835008 | tf_op jit(solution)/shard_map/all_to_all | solution.py:214
  133.7 4.3 %collective-permute-start.6 = (f32[8,1792]{1,0:T(8,128)S(1)}, f32[8,1792]{1,0:T(8,128)S(1)}, u32[]{:S(2)}, u32[]{:S(2)}) collective-permute-start(f32[8,1792]{1,0:T(8,128)S(1)} %get-tuple-element.19), channel_id=1, source_target_pairs={{0,8},{8,0},{1,9},{9,1},{2,10},{10,2},{3,11},{11,3},{4,12},{12,4},... | collective-permute-start | bytes 172040 | tf_op jit(solution)/shard_map/ppermute | solution.py:272
  157.7 6.6 %collective-permute-start.7 = (bf16[128,1792]{1,0:T(8,128)(2,1)S(1)}, bf16[128,1792]{1,0:T(8,128)(2,1)S(1)}, u32[]{:S(2)}, u32[]{:S(2)}) collective-permute-start(bf16[128,1792]{1,0:T(8,128)(2,1)S(1)} %get-tuple-element.20), channel_id=1, source_target_pairs={{0,8},{8,0},{1,9},{9,1},{2,10},{10,2},{3,11},{11,3},{4,12},{12,4},... | collective-permute-start | bytes 1376264 | tf_op jit(solution)/shard_map/ppermute | solution.py:285

commit v3 on v1

--- a/solution.py
+++ b/solution.py
@@ -23,13 +23,22 @@
 F32, BF16 = jnp.float32, jnp.bfloat16
 
 
-def call(body, out_shape, flops, moved):
-    return pl.pallas_call(
-        body,
-        out_shape=out_shape,
-        compiler_params=pltpu.CompilerParams(vmem_limit_bytes=VMEM_LIMIT),
-        cost_estimate=pl.CostEstimate(flops=flops, bytes_accessed=moved, transcendentals=0),
-    )
+def call(body, out_shape, flops, moved, placed=False):
+    vmem = pl.BlockSpec(memory_space=pltpu.VMEM)
+    smem = pl.BlockSpec(memory_space=pltpu.SMEM)
+
+    def run(*operands):
+        specs = [smem if placed and n == 0 else vmem for n in range(len(operands))]
+        return pl.pallas_call(
+            body,
+            out_shape=out_shape,
+            in_specs=specs,
+            out_specs=jax.tree.map(lambda _: vmem, out_shape),
+            compiler_params=pltpu.CompilerParams(vmem_limit_bytes=VMEM_LIMIT),
+            cost_estimate=pl.CostEstimate(flops=flops, bytes_accessed=moved, transcendentals=0),
+        )(*operands)
+
+    return run
 
 
 def iota(shape, axis):
@@ -40,47 +49,66 @@
     return jnp.where(condition, 1.0, 0.0).astype(BF16)
 
 
-def split_features(tokens_ref, out_ref):
+def side_block(z, y_lo, side):
+    return pl.ds(pl.multiple_of(((z * Y_LO + y_lo) * CORE + side) * 128, 128), 128)
+
+
+def take_sibling(at_ref, tokens_ref, basis_ref, out_ref, copies_ref):
+    side = 1 - at_ref[0]
+    for z in range(Z):
+        for y in range(Y_LO):
+            out_ref[:, (z * Y_LO + y) * 128 : (z * Y_LO + y + 1) * 128] = tokens_ref[
+                :, side_block(z, y, side)
+            ]
+    basis = basis_ref[...]
+    for copy in range(copies_ref.shape[0]):
+        copies_ref[copy] = basis
+
+
+def split_features(at_ref, tokens_ref, sibling_ref, *out_refs):
+    core, here = at_ref[0], at_ref[1]
     rows = tokens_ref.shape[0]
     width = Y_LO * 128
     p, q = iota((width, width), 0), iota((width, width), 1)
-    place = ((p >> 4) & 3) * 128 + (p >> 7) * 32 + ((p >> 6) & 1) * 16 + (p & 15)
-    move = one_hot(place == q)
+    steps = (((p >> 4) & 3) - here) & 3
+    move = one_hot(steps * 128 + (p >> 7) * 32 + ((p >> 6) & 1) * 16 + (p & 15) == q)
     for z in range(Z):
-        for core in range(CORE):
-            block = jnp.concatenate(
-                [
-                    tokens_ref[:, pl.ds(((z * Y_LO + y) * CORE + core) * 128, 128)]
-                    for y in range(Y_LO)
-                ],
-                axis=1,
-            )
-            moved = jnp.dot(block, move, preferred_element_type=F32).astype(BF16)
-            for x in range(X):
-                out_ref[pl.ds((core * X + x) * rows, rows), pl.ds(z * 128, 128)] = moved[
-                    :, x * 128 : (x + 1) * 128
-                ]
-
-
-def partial_coefficients(tokens_ref, basis_ref, out_ref):
-    out_ref[...] = jnp.dot(
-        tokens_ref[...], basis_ref[...], preferred_element_type=F32
-    ).astype(BF16)
+        own = jnp.concatenate(
+            [tokens_ref[:, side_block(z, y, core)] for y in range(Y_LO)], axis=1
+        )
+        other = sibling_ref[:, z * width : (z + 1) * width]
+        moved = jnp.dot(
+            jnp.concatenate([own, other], axis=0), move, preferred_element_type=F32
+        ).astype(BF16)
+        for x in range(X):
+            out_refs[x][:, z * 128 : (z + 1) * 128] = moved[:, x * 128 : (x + 1) * 128]
+
+
+def partial_coefficients(at_ref, basis_ref, *refs):
+    *token_refs, out_ref = refs
+    core, here = at_ref[0], at_ref[1]
+    rows = out_ref.shape[1]
+    tokens = jnp.concatenate([ref[...] for ref in token_refs], axis=0)
+    parts = jnp.dot(tokens, basis_ref[...], preferred_element_type=F32)
+    for step in range(X):
+        x = (here - step) & 3
+        for other in range(CORE):
+            side = core if other == 0 else 1 - core
+            start = (step * CORE + other) * rows
+            out_ref[side * X + x] = parts[start : start + rows, :]
 
 
 def sum_coefficients(parts_ref, basis_ref, out_ref):
-    rows = parts_ref.shape[0] // CLASSES
+    rows = parts_ref.shape[1]
     own = basis_ref.shape[0]
-    total = parts_ref[0:rows, :].astype(F32)
+    total = parts_ref[0]
     for part in range(1, CLASSES):
-        total += parts_ref[part * rows : (part + 1) * rows, :].astype(F32)
+        total += parts_ref[part]
     total = total.astype(BF16)
     basis = basis_ref[...]
-    count = out_ref.shape[0] // (rows + own)
-    for copy in range(count):
-        start = copy * (rows + own)
-        out_ref[start : start + rows, :] = total
-        out_ref[start + rows : start + rows + own, :] = basis
+    for copy in range(out_ref.shape[0]):
+        out_ref[copy, 0:rows, :] = total
+        out_ref[copy, rows : rows + own, :] = basis
 
 
 def rank_of(row, core):
@@ -174,93 +202,87 @@
     rows, features = tokens.shape
     own, rank = basis.shape
     group_tokens, columns = grad_gate.shape
-    half_columns = columns // 2
+    half = columns // 2
     scale = 1.0 / math.sqrt(group_tokens * Z * Y_LO * CORE)
     shape = jax.ShapeDtypeStruct
     core = lax.axis_index("core").astype(jnp.int32)
-    core_index = core.reshape(1)
+    at = jnp.stack([core, lax.axis_index("x").astype(jnp.int32)])
+    sibling_at = jnp.stack([1 - core, lax.axis_index("x").astype(jnp.int32)])
     swap = [(0, 1), (1, 0)]
-
-    basis_axes, class_axes, owner_axes = ("z", "y_lo", "y_hi"), ("core", "x"), ("z", "y_lo")
-    tensor_axes = ("y_hi", "x")
 
     def exchange(array, axes):
         return lax.all_to_all(array, axes, 0, 0, tiled=True)
 
     copies = Z * Y_LO * Y_HI
-    class_basis = exchange(
-        jnp.broadcast_to(basis[None], (copies, own, rank)).reshape(copies * own, rank), basis_axes
+    for_sibling, basis_copies = call(
+        take_sibling,
+        (shape((rows, features // CORE), BF16), shape((copies, own, rank), BF16)),
+        0,
+        2 * (rows * features + copies * own * rank),
+        True,
+    )(at, tokens, basis)
+    sibling = lax.ppermute(for_sibling, "core", swap)
+    class_basis = exchange(basis_copies, ("z", "y_lo", "y_hi")).reshape(copies * own, rank)
+    block = shape((CORE * rows, features // CLASSES), BF16)
+    blocks = call(split_features, (block,) * X, 2 * rows * features * 512, 0, True)(
+        at, tokens, sibling
     )
-    split = call(
-        split_features,
-        shape((CLASSES * rows, features // CLASSES), BF16),
-        2 * rows * features * 512,
-        4 * rows * features,
-    )(tokens)
-    class_tokens = exchange(split, class_axes)
+    held = [blocks[0]] + [
+        lax.ppermute(blocks[step], "x", [(x, (x + step) % X) for x in range(X)])
+        for step in range(1, X)
+    ]
     parts = call(
         partial_coefficients,
-        shape((CLASSES * rows, rank), BF16),
+        shape((CLASSES, rows, rank), F32),
         2 * rows * features * rank,
         2 * (rows * features + copies * own * rank),
-    )(class_tokens, class_basis)
-    parts = exchange(parts, class_axes)
+        True,
+    )(at, class_basis, *held)
+    parts = exchange(parts, ("core", "x"))
+    takers = Y_HI * X
     chunk = rows + own
-    summed = call(
-        sum_coefficients,
-        shape((8 * chunk, rank), BF16),
-        CLASSES * rows * rank,
-        4 * 8 * chunk * rank,
-    )(parts, basis)
-    gathered = exchange(summed, tensor_axes)
-
-    smem = pl.BlockSpec(memory_space=pltpu.SMEM)
-    vmem = pl.BlockSpec(memory_space=pltpu.VMEM)
+    gathered = exchange(
+        call(
+            sum_coefficients,
+            shape((takers, chunk, rank), BF16),
+            CLASSES * rows * rank,
+            4 * takers * chunk * rank,
+        )(parts, basis),
+        ("y_hi", "x"),
+    ).reshape(takers * chunk, rank)
 
     def projected(which, dtype):
-        return pl.pallas_call(
+        return call(
             functools.partial(project, scale),
-            out_shape=shape((rank, half_columns), dtype),
-            in_specs=[smem, vmem, vmem],
-            out_specs=vmem,
-            compiler_params=pltpu.CompilerParams(vmem_limit_bytes=VMEM_LIMIT),
-            cost_estimate=pl.CostEstimate(
-                flops=2 * rank * group_tokens * columns,
-                bytes_accessed=2 * group_tokens * columns + 2 * rank * columns,
-                transcendentals=0,
-            ),
+            shape((rank, half), dtype),
+            2 * rank * group_tokens * columns,
+            2 * group_tokens * columns + 2 * rank * columns,
+            True,
         )(which, gathered, grad_gate)
 
-    theirs = lax.ppermute(projected(1 - core_index, BF16), "core", swap)
-    mine = projected(core_index, F32)
-    pair = call(
-        add_halves, shape((rank, half_columns), BF16), rank * half_columns, 8 * rank * half_columns
-    )(mine, theirs)
-    owned = exchange(pair, owner_axes)
+    theirs = lax.ppermute(projected(sibling_at, BF16), "core", swap)
+    mine = projected(at, F32)
+    pair = call(add_halves, shape((rank, half), BF16), rank * half, 8 * rank * half)(mine, theirs)
+    owned = exchange(pair, ("z", "y_lo"))
     first_out, second_out, direction = call(
         adam,
         (
             shape(first_moment.shape, F32),
             shape(second_moment.shape, F32),
-            shape((rank, half_columns), BF16),
+            shape((rank, half), BF16),
         ),
-        rank * half_columns,
-        4 * rank * half_columns,
+        rank * half,
+        4 * rank * half,
     )(owned, first_moment, second_moment)
-    directions = exchange(direction, owner_axes)
+    directions = exchange(direction, ("z", "y_lo"))
     others = lax.ppermute(directions, "core", swap)
-    update = pl.pallas_call(
+    update = call(
         expand,
-        out_shape=shape((own * 8, columns), BF16),
-        in_specs=[smem, vmem, vmem, vmem],
-        out_specs=vmem,
-        compiler_params=pltpu.CompilerParams(vmem_limit_bytes=VMEM_LIMIT),
-        cost_estimate=pl.CostEstimate(
-            flops=4 * own * 8 * rank * columns,
-            bytes_accessed=4 * rank * columns,
-            transcendentals=0,
-        ),
-    )(core_index, gathered, directions, others)
+        shape((own * takers, columns), BF16),
+        4 * own * takers * rank * columns,
+        4 * rank * columns,
+        True,
+    )(at, gathered, directions, others)
     return (update, first_out, second_out)
 
 

time: 159 us -> 163 us (1.025)
  blocking collectives: 123 us -> 75.8 us
  starting transfers between devices: 12.4 us -> 47.2 us
  local copies, waits for them, and re-layouts: 1.18 us -> 8.55 us
  waiting for transfers between devices: 12.9 us -> 17.6 us
  Pallas kernels: 8.42 us -> 11.8 us
    all_to_all x5 -> x3, blocking collectives: 123 us -> 75.8 us  [exchange(): return lax.all_to_all(array, axes, 0, 0, tiled=True)]
    all_to_all x1 -> x2, starting transfers between devices: 3.41 us -> 24.3 us  [exchange(): return lax.all_to_all(array, axes, 0, 0, tiled=True)]
    ppermute x1 -> x5, starting transfers between devices: 3.9 us -> 17.8 us  [the longest x3 10.5 us: per_device(): lax.ppermute(blocks[step], 'x', [(x, (x + step) % X) for x in range(X)])]
    unnamed x10 -> x28, local copies, waits for them, and re-layouts: 1.15 us -> 8.55 us
    ppermute x1 -> x5, waiting for transfers between devices: 0.74 us -> 5.52 us  [the longest x3 3.79 us: per_device(): lax.ppermute(blocks[step], 'x', [(x, (x + step) % X) for x in range(X)])]
    pallas_call x8 -> x9, Pallas kernels: 8.42 us -> 11.8 us  [run(): pl.pallas_call(body, out_shape=out_shape, in_specs=specs, out_specs=jax.t...]
    all_to_all x1 -> x2, waiting for transfers between devices: 10.1 us -> 10 us  [exchange(): return lax.all_to_all(array, axes, 0, 0, tiled=True)]
  transfers between devices with their start and end apart: 3 -> 8, of which waited for: 3 -> 6; matrix products, arithmetic and copies ran while one was open for 0% -> 0% of each run, Pallas kernels for 1% -> 2%
where the time goes in v3:
time: 163 us; the launch traced here: 162 us
  blocking collectives  75.8 us (47%)
  starting transfers between devices  47.2 us (29%)
  waiting for transfers between devices  17.6 us (11%)
  Pallas kernels  11.8 us (7%)
  local copies, waits for them, and re-layouts  8.55 us (5%)
    all_to_all x3, blocking collectives, exchange(): return lax.all_to_all(array, axes, 0, 0, tiled=True)  75.8 us
    all_to_all x2, starting transfers between devices, exchange(): return lax.all_to_all(array, axes, 0, 0, tiled=True)  24.3 us
    pallas_call x9, Pallas kernels, run(): pl.pallas_call(body, out_shape=out_shape, in_specs=specs, out_specs=jax.t...  11.8 us
    ppermute x3, starting transfers between devices, per_device(): lax.ppermute(blocks[step], 'x', [(x, (x + step) % X) for x in range(X)])  10.5 us
    all_to_all x2, waiting for transfers between devices, exchange(): return lax.all_to_all(array, axes, 0, 0, tiled=True)  10 us
    unnamed x28, local copies, waits for them, and re-layouts  8.55 us
    ppermute x1, starting transfers between devices, per_device(): others = lax.ppermute(directions, 'core', swap)  5.13 us
    ppermute x1, starting transfers between devices, per_device(): theirs = lax.ppermute(projected(sibling_at, BF16), 'core', swap)  4.11 us
  transfers between devices with their start and end apart: 8, of which 6 were waited for; matrix products, arithmetic and copies ran while one was open for 0% of the time, Pallas kernels for 2%

profile of v3, /device:TPU:1, one launch (start us, length us, event | category | flops | bytes accessed | tf_op | source)
XLA Modules:
  0.0 161.8 jit_solution(1233961585971077002)
XLA Ops:
  0.7 1.1 copy-done.1
  2.5 1.4 shard_map.76
  4.7 17.1 %all-to-all-start = ((bf16[64,16,256]{2,1,0:T(8,128)(2,1)}), bf16[64,16,256]{2,1,0:T(8,128)(2,1)S(1)}, u32[]{:S(2)}, u32[]{:S(2)}) async-start(bf16[64,16,256]{2,1,0:T(8,128)(2,1)} %get-tuple-element.12), calls=%async_computation | async-start | bytes 1048576 | tf_op jit(solution)/shard_map/all_to_all | solution.py:214
  21.9 3.1 %collective-permute-start = (bf16[48,4096]{1,0:T(8,128)(2,1)}, bf16[48,4096]{1,0:T(8,128)(2,1)S(1)}, u32[]{:S(2)}, u32[]{:S(2)}) collective-permute-start(bf16[48,4096]{1,0:T(8,128)(2,1)} %copy-done.13), channel_id=1, source_target_pairs={{0,8},{8,0},{1,9},{9,1},{2,10},{10,2},{3,11},{11,3},{4,12},{12,4},... | collective-permute-start | bytes 1179656 | tf_op jit(solution)/shard_map/ppermute | solution.py:224
  25.0 1.5 collective-permute-done.sibling_ref
  26.6 1.1 copy-done.2
  27.7 1.5 shard_map.77
  29.2 3.1 %collective-permute-start.1 = (bf16[96,1024]{1,0:T(8,128)(2,1)S(1)}, bf16[96,1024]{1,0:T(8,128)(2,1)S(1)}, u32[]{:S(2)}, u32[]{:S(2)}) collective-permute-start(bf16[96,1024]{1,0:T(8,128)(2,1)S(1)} %get-tuple-element.15), channel_id=1, source_target_pairs={{0,1},{1,2},{2,3},{3,0},{4,5},{5,6},{6,7},{7,4},{8,9},{9,10},{10,1... | collective-permute-start | bytes 589832 | tf_op jit(solution)/shard_map/ppermute | solution.py:231
  32.3 4.4 %collective-permute-start.2 = (bf16[96,1024]{1,0:T(8,128)(2,1)S(1)}, bf16[96,1024]{1,0:T(8,128)(2,1)S(1)}, u32[]{:S(2)}, u32[]{:S(2)}) collective-permute-start(bf16[96,1024]{1,0:T(8,128)(2,1)S(1)} %get-tuple-element.16), channel_id=1, source_target_pairs={{0,2},{1,3},{2,0},{3,1},{4,6},{5,7},{6,4},{7,5},{8,10},{9,11},{10,... | collective-permute-start | bytes 589832 | tf_op jit(solution)/shard_map/ppermute | solution.py:231
  36.7 3.1 %collective-permute-start.3 = (bf16[96,1024]{1,0:T(8,128)(2,1)S(1)}, bf16[96,1024]{1,0:T(8,128)(2,1)S(1)}, u32[]{:S(2)}, u32[]{:S(2)}) collective-permute-start(bf16[96,1024]{1,0:T(8,128)(2,1)S(1)} %get-tuple-element.17), channel_id=1, source_target_pairs={{0,3},{1,0},{2,1},{3,2},{4,7},{5,4},{6,5},{7,6},{8,11},{9,8},{10,9... | collective-permute-start | bytes 589832 | tf_op jit(solution)/shard_map/ppermute | solution.py:231
  40.5 3.2 %collective-permute-done.2.refs_2_ = bf16[96,1024]{1,0:T(8,128)(2,1)S(1)} collective-permute-done((bf16[96,1024]{1,0:T(8,128)(2,1)S(1)}, bf16[96,1024]{1,0:T(8,128)(2,1)S(1)}, u32[]{:S(2)}, u32[]{:S(2)}) %collective-permute-start.2) | collective-permute-done | bytes 196640 | tf_op jit(solution)/shard_map/ppermute | solution.py:231
  45.6 0.9 copy-done.4
  47.5 0.9 copy-done.8
  49.3 13.5 %all_to_all.37.parts_ref = f32[8,48,256]{2,1,0:T(8,128)S(1)} all-to-all(f32[8,48,256]{2,1,0:T(8,128)S(1)} %shard_map.78), channel_id=1, replica_groups=mesh['z'=8,'y_lo'=4,'core'=2,'y_hi'=2,'x'=4] {'core','x'}, dimensions={0} | all-to-all | bytes 786432 | tf_op jit(solution)/shard_map/all_to_all | solution.py:214
  63.6 7.2 %all-to-all-start.2 = ((bf16[8,64,256]{2,1,0:T(8,128)(2,1)}), bf16[8,64,256]{2,1,0:T(8,128)(2,1)S(1)}, u32[]{:S(2)}, u32[]{:S(2)}) async-start(bf16[8,64,256]{2,1,0:T(8,128)(2,1)} %shard_map.79), calls=%async_computation.2 | async-start | bytes 524288 | tf_op jit(solution)/shard_map/all_to_all | solution.py:214
  70.9 10.0 %all-to-all-done.2 = bf16[8,64,256]{2,1,0:T(8,128)(2,1)S(1)} async-done(((bf16[8,64,256]{2,1,0:T(8,128)(2,1)}), bf16[8,64,256]{2,1,0:T(8,128)(2,1)S(1)}, u32[]{:S(2)}, u32[]{:S(2)}) %all-to-all-start.2) | async-done | bytes 262176 | tf_op jit(solution)/shard_map/all_to_all | solution.py:214
  80.9 1.9 %shard_map.81 = bf16[256,1792]{1,0:T(8,128)(2,1)S(1)} custom-call(s32[2]{0:T(128)S(1)} %pad_add_fusion.1.core_ref, bf16[512,256]{1,0:T(8,128)(2,1)S(1)} %bitcast.9, bf16[384,3584]{1,0:T(8,128)(2,1)S(1)} %copy-done), custom_call_target="tpu_custom_call" | custom-call | flops 704643072 | bytes 4587520 | tf_op jit(solution)/shard_map/pallas_call | solution.py:32
  82.7 4.1 %collective-permute-start.4 = (bf16[256,1792]{1,0:T(8,128)(2,1)S(1)}, bf16[256,1792]{1,0:T(8,128)(2,1)S(1)}, u32[]{:S(2)}, u32[]{:S(2)}) collective-permute-start(bf16[256,1792]{1,0:T(8,128)(2,1)S(1)} %shard_map.81), channel_id=1, source_target_pairs={{0,8},{8,0},{1,9},{9,1},{2,10},{10,2},{3,11},{11,3},{4,12},{12,4},... | collective-permute-start | bytes 2752520 | tf_op jit(solution)/shard_map/ppermute | solution.py:263
  86.9 1.9 %shard_map.80.mine_ref = f32[256,1792]{1,0:T(8,128)S(1)} custom-call(s32[2]{0:T(128)S(1)} %pad_add_fusion.at_ref.core_ref, bf16[512,256]{1,0:T(8,128)(2,1)S(1)} %bitcast.10, bf16[384,3584]{1,0:T(8,128)(2,1)S(1)} %copy-done), custom_call_target="tpu_custom_call" | custom-call | flops 704643072 | bytes 4587520 | tf_op jit(solution)/shard_map/pallas_call | solution.py:32
  89.1 32.5 %all_to_all.38 = bf16[32,8,1792]{2,1,0:T(8,128)(2,1)S(1)} all-to-all(bf16[32,8,1792]{2,1,0:T(8,128)(2,1)S(1)} %bitcast.12), channel_id=1, replica_groups=mesh['z'=8,'y_lo'=4,'core'=2,'y_hi'=2,'x'=4] {'z','y_lo'}, dimensions={0} | all-to-all | bytes 1835008 | tf_op jit(solution)/shard_map/all_to_all | solution.py:214
  122.3 29.8 %all_to_all.39 = bf16[32,8,1792]{2,1,0:T(8,128)(2,1)S(1)} all-to-all(bf16[32,8,1792]{2,1,0:T(8,128)(2,1)S(1)} %bitcast.17), channel_id=1, replica_groups=mesh['z'=8,'y_lo'=4,'core'=2,'y_hi'=2,'x'=4] {'z','y_lo'}, dimensions={0} | all-to-all | bytes 1835008 | tf_op jit(solution)/shard_map/all_to_all | solution.py:214
  152.1 5.1 %collective-permute-start.5 = (bf16[256,1792]{1,0:T(8,128)(2,1)S(1)}, bf16[256,1792]{1,0:T(8,128)(2,1)S(1)}, u32[]{:S(2)}, u32[]{:S(2)}) collective-permute-start(bf16[256,1792]{1,0:T(8,128)(2,1)S(1)} %bitcast.13), channel_id=1, source_target_pairs={{0,8},{8,0},{1,9},{9,1},{2,10},{10,2},{3,11},{11,3},{4,12},{12,4},... | collective-permute-start | bytes 2752520 | tf_op jit(solution)/shard_map/ppermute | solution.py:278
  157.3 2.1 %collective-permute-done.5.theirs_ref = bf16[256,1792]{1,0:T(8,128)(2,1)S(1)} collective-permute-done((bf16[256,1792]{1,0:T(8,128)(2,1)S(1)}, bf16[256,1792]{1,0:T(8,128)(2,1)S(1)}, u32[]{:S(2)}, u32[]{:S(2)}) %collective-permute-start.5) | collective-permute-done | bytes 917536 | tf_op jit(solution)/shard_map/ppermute | solution.py:278
  159.3 2.5 %shard_map.84 = bf16[128,3584]{1,0:T(8,128)(2,1)} custom-call(s32[2]{0:T(128)S(1)} %pad_add_fusion.at_ref.core_ref, bf16[512,256]{1,0:T(8,128)(2,1)S(1)} %bitcast.11, bf16[256,1792]{1,0:T(8,128)(2,1)S(1)} %bitcast.14, bf16[256,1792]{1,0:T(8,128)(2,1)S(1)} %collective-permute-done.5.theirs_ref), custom_call_target="tpu_custom_call" | custom-call | flops 469762048 | bytes 3670016 | tf_op jit(solution)/shard_map/pallas_call | solution.py:32
  (34 shorter events, 8.0 us)
Async XLA Ops:
  0.7 1.1 copy-start.1
  1.8 0.7 copy-start.11
  2.5 60.3 %copy-start.12 = (bf16[16,256]{1,0:T(8,128)(2,1)S(1)}, bf16[16,256]{1,0:T(8,128)(2,1)}, u32[]{:S(2)}) copy-start(bf16[16,256]{1,0:T(8,128)(2,1)} %basis_ref.3) | copy-start | bytes 24580
  4.0 0.7 copy-start.13
  4.7 40.9 %all-to-all-start = ((bf16[64,16,256]{2,1,0:T(8,128)(2,1)}), bf16[64,16,256]{2,1,0:T(8,128)(2,1)S(1)}, u32[]{:S(2)}, u32[]{:S(2)}) async-start(bf16[64,16,256]{2,1,0:T(8,128)(2,1)} %get-tuple-element.12), calls=%async_computation | async-start | bytes 1048576 | tf_op jit(solution)/shard_map/all_to_all | solution.py:214
  21.9 59.0 %copy-start = (bf16[384,3584]{1,0:T(8,128)(2,1)S(1)}, bf16[384,3584]{1,0:T(8,128)(2,1)}, u32[]{:S(2)}) copy-start(bf16[384,3584]{1,0:T(8,128)(2,1)} %grad_ref.3) | copy-start | bytes 8257540
  21.9 4.7 %collective-permute-start = (bf16[48,4096]{1,0:T(8,128)(2,1)}, bf16[48,4096]{1,0:T(8,128)(2,1)S(1)}, u32[]{:S(2)}, u32[]{:S(2)}) collective-permute-start(bf16[48,4096]{1,0:T(8,128)(2,1)} %copy-done.13), channel_id=1, source_target_pairs={{0,8},{8,0},{1,9},{9,1},{2,10},{10,2},{3,11},{11,3},{4,12},{12,4},... | collective-permute-start | bytes 1179656 | tf_op jit(solution)/shard_map/ppermute | solution.py:224
  26.6 1.1 copy-start.2
  29.2 10.6 %collective-permute-start.1 = (bf16[96,1024]{1,0:T(8,128)(2,1)S(1)}, bf16[96,1024]{1,0:T(8,128)(2,1)S(1)}, u32[]{:S(2)}, u32[]{:S(2)}) collective-permute-start(bf16[96,1024]{1,0:T(8,128)(2,1)S(1)} %get-tuple-element.15), channel_id=1, source_target_pairs={{0,1},{1,2},{2,3},{3,0},{4,5},{5,6},{6,7},{7,4},{8,9},{9,10},{10,1... | collective-permute-start | bytes 589832 | tf_op jit(solution)/shard_map/ppermute | solution.py:231
  32.3 11.3 %collective-permute-start.2 = (bf16[96,1024]{1,0:T(8,128)(2,1)S(1)}, bf16[96,1024]{1,0:T(8,128)(2,1)S(1)}, u32[]{:S(2)}, u32[]{:S(2)}) collective-permute-start(bf16[96,1024]{1,0:T(8,128)(2,1)S(1)} %get-tuple-element.16), channel_id=1, source_target_pairs={{0,2},{1,3},{2,0},{3,1},{4,6},{5,7},{6,4},{7,5},{8,10},{9,11},{10,... | collective-permute-start | bytes 589832 | tf_op jit(solution)/shard_map/ppermute | solution.py:231
  36.7 8.2 %collective-permute-start.3 = (bf16[96,1024]{1,0:T(8,128)(2,1)S(1)}, bf16[96,1024]{1,0:T(8,128)(2,1)S(1)}, u32[]{:S(2)}, u32[]{:S(2)}) collective-permute-start(bf16[96,1024]{1,0:T(8,128)(2,1)S(1)} %get-tuple-element.17), channel_id=1, source_target_pairs={{0,3},{1,0},{2,1},{3,2},{4,7},{5,4},{6,5},{7,6},{8,11},{9,8},{10,9... | collective-permute-start | bytes 589832 | tf_op jit(solution)/shard_map/ppermute | solution.py:231
  39.8 0.7 copy-start.3
  43.6 0.7 copy-start.5
  44.9 0.7 copy-start.7
  45.6 0.9 copy-start.4
  46.6 0.9 copy-start.6
  47.5 0.9 copy-start.8
  63.6 17.3 %all-to-all-start.2 = ((bf16[8,64,256]{2,1,0:T(8,128)(2,1)}), bf16[8,64,256]{2,1,0:T(8,128)(2,1)S(1)}, u32[]{:S(2)}, u32[]{:S(2)}) async-start(bf16[8,64,256]{2,1,0:T(8,128)(2,1)} %shard_map.79), calls=%async_computation.2 | async-start | bytes 524288 | tf_op jit(solution)/shard_map/all_to_all | solution.py:214
  82.7 6.2 %collective-permute-start.4 = (bf16[256,1792]{1,0:T(8,128)(2,1)S(1)}, bf16[256,1792]{1,0:T(8,128)(2,1)S(1)}, u32[]{:S(2)}, u32[]{:S(2)}) collective-permute-start(bf16[256,1792]{1,0:T(8,128)(2,1)S(1)} %shard_map.81), channel_id=1, source_target_pairs={{0,8},{8,0},{1,9},{9,1},{2,10},{10,2},{3,11},{11,3},{4,12},{12,4},... | collective-permute-start | bytes 2752520 | tf_op jit(solution)/shard_map/ppermute | solution.py:263
  88.7 32.8 %copy-start.9 = (f32[4,3584]{1,0:T(4,128)S(1)}, f32[4,3584]{1,0:T(4,128)}, u32[]{:S(2)}) copy-start(f32[4,3584]{1,0:T(4,128)} %first_ref.1) | copy-start | bytes 172036
  88.7 32.8 %copy-start.10 = (f32[4,3584]{1,0:T(4,128)S(1)}, f32[4,3584]{1,0:T(4,128)}, u32[]{:S(2)}) copy-start(f32[4,3584]{1,0:T(4,128)} %second_ref.1) | copy-start | bytes 172036
  152.1 7.2 %collective-permute-start.5 = (bf16[256,1792]{1,0:T(8,128)(2,1)S(1)}, bf16[256,1792]{1,0:T(8,128)(2,1)S(1)}, u32[]{:S(2)}, u32[]{:S(2)}) collective-permute-start(bf16[256,1792]{1,0:T(8,128)(2,1)S(1)} %bitcast.13), channel_id=1, source_target_pairs={{0,8},{8,0},{1,9},{9,1},{2,10},{10,2},{3,11},{11,3},{4,12},{12,4},... | collective-permute-start | bytes 2752520 | tf_op jit(solution)/shard_map/ppermute | solution.py:278

commit v4 on v3

--- a/solution.py
+++ b/solution.py
@@ -20,21 +20,23 @@
 CLASSES = CORE * X
 OWNERS = Z * Y_LO
 VMEM_LIMIT = 24 * 1024 * 1024
+MOST_VMEM = 58 * 1024 * 1024
 F32, BF16 = jnp.float32, jnp.bfloat16
 
 
-def call(body, out_shape, flops, moved, placed=False):
+def call(body, out_shape, flops, moved, places="", scratch=(), limit=VMEM_LIMIT):
     vmem = pl.BlockSpec(memory_space=pltpu.VMEM)
-    smem = pl.BlockSpec(memory_space=pltpu.SMEM)
+    spaces = {"s": pl.BlockSpec(memory_space=pltpu.SMEM), "h": pl.BlockSpec(memory_space=pl.ANY)}
 
     def run(*operands):
-        specs = [smem if placed and n == 0 else vmem for n in range(len(operands))]
+        where = places.ljust(len(operands), "v")
         return pl.pallas_call(
             body,
             out_shape=out_shape,
-            in_specs=specs,
+            in_specs=[spaces.get(place, vmem) for place in where],
             out_specs=jax.tree.map(lambda _: vmem, out_shape),
-            compiler_params=pltpu.CompilerParams(vmem_limit_bytes=VMEM_LIMIT),
+            scratch_shapes=scratch,
+            compiler_params=pltpu.CompilerParams(vmem_limit_bytes=limit),
             cost_estimate=pl.CostEstimate(flops=flops, bytes_accessed=moved, transcendentals=0),
         )(*operands)
 
@@ -53,49 +55,62 @@
     return pl.ds(pl.multiple_of(((z * Y_LO + y_lo) * CORE + side) * 128, 128), 128)
 
 
-def take_sibling(at_ref, tokens_ref, basis_ref, out_ref, copies_ref):
-    side = 1 - at_ref[0]
-    for z in range(Z):
-        for y in range(Y_LO):
-            out_ref[:, (z * Y_LO + y) * 128 : (z * Y_LO + y + 1) * 128] = tokens_ref[
-                :, side_block(z, y, side)
-            ]
-    basis = basis_ref[...]
-    for copy in range(copies_ref.shape[0]):
-        copies_ref[copy] = basis
-
-
-def split_features(at_ref, tokens_ref, sibling_ref, *out_refs):
+def take_side(side, tokens_ref, out_ref, sems):
+    return [
+        pltpu.make_async_copy(
+            tokens_ref.at[:, side_block(n // Y_LO, n % Y_LO, side)],
+            out_ref.at[:, n * 128 : (n + 1) * 128],
+            sems.at[n],
+        )
+        for n in range(Z * Y_LO)
+    ]
+
+
+def take_sibling(at_ref, tokens_ref, out_ref, sems):
+    copies = take_side(1 - at_ref[0], tokens_ref, out_ref, sems)
+    for copy in copies:
+        copy.start()
+    for copy in copies:
+        copy.wait()
+
+
+def split_features(at_ref, tokens_ref, sibling_ref, *refs):
+    *out_refs, own_ref, sems = refs
     core, here = at_ref[0], at_ref[1]
-    rows = tokens_ref.shape[0]
+    copies = take_side(core, tokens_ref, own_ref, sems)
+    for copy in copies:
+        copy.start()
     width = Y_LO * 128
     p, q = iota((width, width), 0), iota((width, width), 1)
     steps = (((p >> 4) & 3) - here) & 3
     move = one_hot(steps * 128 + (p >> 7) * 32 + ((p >> 6) & 1) * 16 + (p & 15) == q)
+    for copy in copies:
+        copy.wait()
     for z in range(Z):
-        own = jnp.concatenate(
-            [tokens_ref[:, side_block(z, y, core)] for y in range(Y_LO)], axis=1
-        )
-        other = sibling_ref[:, z * width : (z + 1) * width]
-        moved = jnp.dot(
-            jnp.concatenate([own, other], axis=0), move, preferred_element_type=F32
-        ).astype(BF16)
+        columns = slice(z * width, (z + 1) * width)
+        both = jnp.concatenate([own_ref[:, columns], sibling_ref[:, columns]], axis=0)
+        moved = jnp.dot(both, move, preferred_element_type=F32).astype(BF16)
         for x in range(X):
             out_refs[x][:, z * 128 : (z + 1) * 128] = moved[:, x * 128 : (x + 1) * 128]
 
 
 def partial_coefficients(at_ref, basis_ref, *refs):
-    *token_refs, out_ref = refs
+    *token_refs, out_ref, held_ref, sems = refs
     core, here = at_ref[0], at_ref[1]
     rows = out_ref.shape[1]
-    tokens = jnp.concatenate([ref[...] for ref in token_refs], axis=0)
-    parts = jnp.dot(tokens, basis_ref[...], preferred_element_type=F32)
+    copies = [
+        pltpu.make_async_copy(ref, held_ref.at[step], sems.at[step])
+        for step, ref in enumerate(token_refs)
+    ]
+    for copy in copies:
+        copy.start()
     for step in range(X):
         x = (here - step) & 3
+        copies[step].wait()
+        parts = jnp.dot(held_ref[step], basis_ref[...], preferred_element_type=F32)
         for other in range(CORE):
             side = core if other == 0 else 1 - core
-            start = (step * CORE + other) * rows
-            out_ref[side * X + x] = parts[start : start + rows, :]
+            out_ref[side * X + x] = parts[other * rows : (other + 1) * rows, :]
 
 
 def sum_coefficients(parts_ref, basis_ref, out_ref):
@@ -214,19 +229,22 @@
         return lax.all_to_all(array, axes, 0, 0, tiled=True)
 
     copies = Z * Y_LO * Y_HI
-    for_sibling, basis_copies = call(
-        take_sibling,
-        (shape((rows, features // CORE), BF16), shape((copies, own, rank), BF16)),
+    basis_copies = jnp.broadcast_to(basis[None], (copies, own, rank))
+    class_basis = exchange(basis_copies, ("z", "y_lo", "y_hi")).reshape(copies * own, rank)
+    side = shape((rows, features // CORE), BF16)
+    blocks_sem = pltpu.SemaphoreType.DMA((Z * Y_LO,))
+    for_sibling = call(take_sibling, side, 0, 2 * rows * features, "sh", [blocks_sem], MOST_VMEM)(at, tokens)
+    sibling = lax.ppermute(for_sibling, "core", swap)
+    block = shape((CORE * rows, features // CLASSES), BF16)
+    blocks = call(
+        split_features,
+        (block,) * X,
+        2 * rows * features * 512,
         0,
-        2 * (rows * features + copies * own * rank),
-        True,
-    )(at, tokens, basis)
-    sibling = lax.ppermute(for_sibling, "core", swap)
-    class_basis = exchange(basis_copies, ("z", "y_lo", "y_hi")).reshape(copies * own, rank)
-    block = shape((CORE * rows, features // CLASSES), BF16)
-    blocks = call(split_features, (block,) * X, 2 * rows * features * 512, 0, True)(
-        at, tokens, sibling
-    )
+        "sh",
+        [pltpu.VMEM(side.shape, BF16), blocks_sem],
+        MOST_VMEM,
+    )(at, tokens, sibling)
     held = [blocks[0]] + [
         lax.ppermute(blocks[step], "x", [(x, (x + step) % X) for x in range(X)])
         for step in range(1, X)
@@ -236,7 +254,9 @@
         shape((CLASSES, rows, rank), F32),
         2 * rows * features * rank,
         2 * (rows * features + copies * own * rank),
-        True,
+        "svhhhh",
+        [pltpu.VMEM((X,) + block.shape, BF16), pltpu.SemaphoreType.DMA((X,))],
+        MOST_VMEM,
     )(at, class_basis, *held)
     parts = exchange(parts, ("core", "x"))
     takers = Y_HI * X
@@ -257,7 +277,7 @@
             shape((rank, half), dtype),
             2 * rank * group_tokens * columns,
             2 * group_tokens * columns + 2 * rank * columns,
-            True,
+            "s",
         )(which, gathered, grad_gate)
 
     theirs = lax.ppermute(projected(sibling_at, BF16), "core", swap)
@@ -281,7 +301,7 @@
         shape((own * takers, columns), BF16),
         4 * own * takers * rank * columns,
         4 * rank * columns,
-        True,
+        "s",
     )(at, gathered, directions, others)
     return (update, first_out, second_out)
 

time: 163 us -> 166 us (1.018)
  Pallas kernels: 11.8 us -> 18.4 us
  local copies, waits for them, and re-layouts: 8.55 us -> 3.79 us
    pallas_call x9, Pallas kernels: 11.8 us -> 18.4 us  [run(): pl.pallas_call(body, out_shape=out_shape, in_specs=[spaces.get(place, vme...]
    unnamed x28 -> x18, local copies, waits for them, and re-layouts: 8.55 us -> 2.27 us
  transfers between devices with their start and end apart: 8 -> 8, of which waited for: 6 -> 6; matrix products, arithmetic and copies ran while one was open for 0% -> 0% of each run, Pallas kernels for 2% -> 5%
where the time goes in v4:
time: 166 us; the launch traced here: 165 us
  blocking collectives  76 us (46%)
  starting transfers between devices  47.2 us (28%)
  waiting for transfers between devices  18.6 us (11%)
  Pallas kernels  18.4 us (11%)
  local copies, waits for them, and re-layouts  3.79 us (2%)
    all_to_all x3, blocking collectives, exchange(): return lax.all_to_all(array, axes, 0, 0, tiled=True)  76 us
    all_to_all x2, starting transfers between devices, exchange(): return lax.all_to_all(array, axes, 0, 0, tiled=True)  24.3 us
    pallas_call x9, Pallas kernels, run(): pl.pallas_call(body, out_shape=out_shape, in_specs=[spaces.get(place, vme...  18.4 us
    ppermute x3, starting transfers between devices, per_device(): lax.ppermute(blocks[step], 'x', [(x, (x + step) % X) for x in range(X)])  10.5 us
    all_to_all x2, waiting for transfers between devices, exchange(): return lax.all_to_all(array, axes, 0, 0, tiled=True)  10 us
    ppermute x1, starting transfers between devices, per_device(): others = lax.ppermute(directions, 'core', swap)  5.13 us
    ppermute x3, waiting for transfers between devices, per_device(): lax.ppermute(blocks[step], 'x', [(x, (x + step) % X) for x in range(X)])  4.76 us
    ppermute x1, starting transfers between devices, per_device(): theirs = lax.ppermute(projected(sibling_at, BF16), 'core', swap)  4.11 us
  transfers between devices with their start and end apart: 8, of which 6 were waited for; matrix products, arithmetic and copies ran while one was open for 0% of the time, Pallas kernels for 5%

profile of v4, /device:TPU:1, one launch (start us, length us, event | category | flops | bytes accessed | tf_op | source)
XLA Modules:
  0.0 165.5 jit_solution(11553343212328218262)
XLA Ops:
  0.6 1.5 broadcast_in_dim.2
  2.2 17.1 %all-to-all-start = ((bf16[64,16,256]{2,1,0:T(8,128)(2,1)}), bf16[64,16,256]{2,1,0:T(8,128)(2,1)S(1)}, u32[]{:S(2)}, u32[]{:S(2)}) async-start(bf16[64,16,256]{2,1,0:T(8,128)(2,1)} %broadcast_in_dim.2), calls=%async_computation | async-start | bytes 1048576 | tf_op jit(solution)/shard_map/all_to_all | solution.py:229
  20.0 2.7 %shard_map.76 = bf16[48,4096]{1,0:T(8,128)(2,1)} custom-call(s32[2]{0:T(128)} %pad_add_fusion.at_ref.core_ref, bf16[48,8192]{1,0:T(8,128)(2,1)} %tokens_ref.3), custom_call_target="tpu_custom_call" | custom-call | bytes 786432 | tf_op jit(solution)/shard_map/pallas_call | solution.py:33
  22.7 3.1 %collective-permute-start = (bf16[48,4096]{1,0:T(8,128)(2,1)}, bf16[48,4096]{1,0:T(8,128)(2,1)S(1)}, u32[]{:S(2)}, u32[]{:S(2)}) collective-permute-start(bf16[48,4096]{1,0:T(8,128)(2,1)} %shard_map.76), channel_id=1, source_target_pairs={{0,8},{8,0},{1,9},{9,1},{2,10},{10,2},{3,11},{11,3},{4,12},{12,4},... | collective-permute-start | bytes 1179656 | tf_op jit(solution)/shard_map/ppermute | solution.py:237
  25.8 1.5 collective-permute-done.sibling_ref
  28.1 4.0 %shard_map.77 = (bf16[96,1024]{1,0:T(8,128)(2,1)}, bf16[96,1024]{1,0:T(8,128)(2,1)}, bf16[96,1024]{1,0:T(8,128)(2,1)}, bf16[96,1024]{1,0:T(8,128)(2,1)}) custom-call(s32[2]{0:T(128)} %pad_add_fusion.at_ref.core_ref, bf16[48,8192]{1,0:T(8,128)(2,1)} %tokens_ref.3, bf16[48,4096]{1,0:T(8,128)(2,1)} %copy-done.8), custom_call_target="tpu_custom_call" | custom-call | flops 402653184 | tf_op jit(solution)/shard_map/pallas_call | solution.py:33
  32.1 3.1 %collective-permute-start.1 = (bf16[96,1024]{1,0:T(8,128)(2,1)}, bf16[96,1024]{1,0:T(8,128)(2,1)S(1)}, u32[]{:S(2)}, u32[]{:S(2)}) collective-permute-start(bf16[96,1024]{1,0:T(8,128)(2,1)} %get-tuple-element.11), channel_id=1, source_target_pairs={{0,1},{1,2},{2,3},{3,0},{4,5},{5,6},{6,7},{7,4},{8,9},{9,10},{10,1... | collective-permute-start | bytes 589832 | tf_op jit(solution)/shard_map/ppermute | solution.py:249
  35.2 4.4 %collective-permute-start.2 = (bf16[96,1024]{1,0:T(8,128)(2,1)}, bf16[96,1024]{1,0:T(8,128)(2,1)S(1)}, u32[]{:S(2)}, u32[]{:S(2)}) collective-permute-start(bf16[96,1024]{1,0:T(8,128)(2,1)} %get-tuple-element.12), channel_id=1, source_target_pairs={{0,2},{1,3},{2,0},{3,1},{4,6},{5,7},{6,4},{7,5},{8,10},{9,11},{10,... | collective-permute-start | bytes 589832 | tf_op jit(solution)/shard_map/ppermute | solution.py:249
  39.6 3.1 %collective-permute-start.3 = (bf16[96,1024]{1,0:T(8,128)(2,1)}, bf16[96,1024]{1,0:T(8,128)(2,1)}, u32[]{:S(2)}, u32[]{:S(2)}) collective-permute-start(bf16[96,1024]{1,0:T(8,128)(2,1)} %get-tuple-element.13), channel_id=1, source_target_pairs={{0,3},{1,0},{2,1},{3,2},{4,7},{5,4},{6,5},{7,6},{8,11},{9,8},{10,9... | collective-permute-start | bytes 589832 | tf_op jit(solution)/shard_map/ppermute | solution.py:249
  42.7 4.0 %collective-permute-done.2.refs_2_ = bf16[96,1024]{1,0:T(8,128)(2,1)S(1)} collective-permute-done((bf16[96,1024]{1,0:T(8,128)(2,1)}, bf16[96,1024]{1,0:T(8,128)(2,1)S(1)}, u32[]{:S(2)}, u32[]{:S(2)}) %collective-permute-start.2) | collective-permute-done | bytes 196640 | tf_op jit(solution)/shard_map/ppermute | solution.py:249
  48.1 0.8 copy-done.5
  48.9 3.9 %shard_map.78 = f32[8,48,256]{2,1,0:T(8,128)} custom-call(s32[2]{0:T(128)} %pad_add_fusion.at_ref.core_ref, bf16[1024,256]{1,0:T(8,128)(2,1)} %bitcast.17, bf16[96,1024]{1,0:T(8,128)(2,1)} %get-tuple-element.10.refs_0_, bf16[96,1024]{1,0:T(8,128)(2,1)} %copy-done.6, bf16[96,1024]{1,0:T(8,128)(2,1)} %copy-done.7, bf16[96,1024]{1,0:T(8,128)(2,1)} %collective-permute-done.3.refs_3_), custom_call_target="tpu_custom_call" | custom-call | flops 201326592 | bytes 1310720 | tf_op jit(solution)/shard_map/pallas_call | solution.py:33
  52.8 13.7 %all_to_all.37.parts_ref = f32[8,48,256]{2,1,0:T(8,128)S(1)} all-to-all(f32[8,48,256]{2,1,0:T(8,128)} %shard_map.78), channel_id=1, replica_groups=mesh['z'=8,'y_lo'=4,'core'=2,'y_hi'=2,'x'=4] {'core','x'}, dimensions={0} | all-to-all | bytes 786432 | tf_op jit(solution)/shard_map/all_to_all | solution.py:229
  67.3 7.2 %all-to-all-start.2 = ((bf16[8,64,256]{2,1,0:T(8,128)(2,1)}), bf16[8,64,256]{2,1,0:T(8,128)(2,1)S(1)}, u32[]{:S(2)}, u32[]{:S(2)}) async-start(bf16[8,64,256]{2,1,0:T(8,128)(2,1)} %shard_map.79), calls=%async_computation.2 | async-start | bytes 524288 | tf_op jit(solution)/shard_map/all_to_all | solution.py:229
  74.5 10.0 %all-to-all-done.2 = bf16[8,64,256]{2,1,0:T(8,128)(2,1)S(1)} async-done(((bf16[8,64,256]{2,1,0:T(8,128)(2,1)}), bf16[8,64,256]{2,1,0:T(8,128)(2,1)S(1)}, u32[]{:S(2)}, u32[]{:S(2)}) %all-to-all-start.2) | async-done | bytes 262176 | tf_op jit(solution)/shard_map/all_to_all | solution.py:229
  84.6 1.8 %shard_map.81 = bf16[256,1792]{1,0:T(8,128)(2,1)S(1)} custom-call(s32[2]{0:T(128)S(1)} %pad_add_fusion.1.core_ref, bf16[512,256]{1,0:T(8,128)(2,1)S(1)} %bitcast.9, bf16[384,3584]{1,0:T(8,128)(2,1)S(1)} %copy-done), custom_call_target="tpu_custom_call" | custom-call | flops 704643072 | bytes 4587520 | tf_op jit(solution)/shard_map/pallas_call | solution.py:33
  86.4 4.1 %collective-permute-start.4 = (bf16[256,1792]{1,0:T(8,128)(2,1)S(1)}, bf16[256,1792]{1,0:T(8,128)(2,1)S(1)}, u32[]{:S(2)}, u32[]{:S(2)}) collective-permute-start(bf16[256,1792]{1,0:T(8,128)(2,1)S(1)} %shard_map.81), channel_id=1, source_target_pairs={{0,8},{8,0},{1,9},{9,1},{2,10},{10,2},{3,11},{11,3},{4,12},{12,4},... | collective-permute-start | bytes 2752520 | tf_op jit(solution)/shard_map/ppermute | solution.py:283
  90.5 1.8 %shard_map.80.mine_ref = f32[256,1792]{1,0:T(8,128)S(1)} custom-call(s32[2]{0:T(128)S(1)} %copy-done.4, bf16[512,256]{1,0:T(8,128)(2,1)S(1)} %bitcast.10, bf16[384,3584]{1,0:T(8,128)(2,1)S(1)} %copy-done), custom_call_target="tpu_custom_call" | custom-call | flops 704643072 | bytes 4587520 | tf_op jit(solution)/shard_map/pallas_call | solution.py:33
  92.7 32.5 %all_to_all.38 = bf16[32,8,1792]{2,1,0:T(8,128)(2,1)S(1)} all-to-all(bf16[32,8,1792]{2,1,0:T(8,128)(2,1)S(1)} %bitcast.12), channel_id=1, replica_groups=mesh['z'=8,'y_lo'=4,'core'=2,'y_hi'=2,'x'=4] {'z','y_lo'}, dimensions={0} | all-to-all | bytes 1835008 | tf_op jit(solution)/shard_map/all_to_all | solution.py:229
  125.2 0.8 shard_map.83
  126.0 29.8 %all_to_all.39 = bf16[32,8,1792]{2,1,0:T(8,128)(2,1)S(1)} all-to-all(bf16[32,8,1792]{2,1,0:T(8,128)(2,1)S(1)} %bitcast.16), channel_id=1, replica_groups=mesh['z'=8,'y_lo'=4,'core'=2,'y_hi'=2,'x'=4] {'z','y_lo'}, dimensions={0} | all-to-all | bytes 1835008 | tf_op jit(solution)/shard_map/all_to_all | solution.py:229
  155.8 5.1 %collective-permute-start.5 = (bf16[256,1792]{1,0:T(8,128)(2,1)S(1)}, bf16[256,1792]{1,0:T(8,128)(2,1)S(1)}, u32[]{:S(2)}, u32[]{:S(2)}) collective-permute-start(bf16[256,1792]{1,0:T(8,128)(2,1)S(1)} %bitcast.13), channel_id=1, source_target_pairs={{0,8},{8,0},{1,9},{9,1},{2,10},{10,2},{3,11},{11,3},{4,12},{12,4},... | collective-permute-start | bytes 2752520 | tf_op jit(solution)/shard_map/ppermute | solution.py:298
  160.9 2.1 %collective-permute-done.5.theirs_ref = bf16[256,1792]{1,0:T(8,128)(2,1)S(1)} collective-permute-done((bf16[256,1792]{1,0:T(8,128)(2,1)S(1)}, bf16[256,1792]{1,0:T(8,128)(2,1)S(1)}, u32[]{:S(2)}, u32[]{:S(2)}) %collective-permute-start.5) | collective-permute-done | bytes 917536 | tf_op jit(solution)/shard_map/ppermute | solution.py:298
  163.0 2.5 %shard_map.84 = bf16[128,3584]{1,0:T(8,128)(2,1)} custom-call(s32[2]{0:T(128)S(1)} %copy-done.4, bf16[512,256]{1,0:T(8,128)(2,1)S(1)} %bitcast.11, bf16[256,1792]{1,0:T(8,128)(2,1)S(1)} %bitcast.14, bf16[256,1792]{1,0:T(8,128)(2,1)S(1)} %collective-permute-done.5.theirs_ref), custom_call_target="tpu_custom_call" | custom-call | flops 469762048 | bytes 3670016 | tf_op jit(solution)/shard_map/pallas_call | solution.py:33
  (25 shorter events, 4.0 us)
Async XLA Ops:
  2.2 46.0 %all-to-all-start = ((bf16[64,16,256]{2,1,0:T(8,128)(2,1)}), bf16[64,16,256]{2,1,0:T(8,128)(2,1)S(1)}, u32[]{:S(2)}, u32[]{:S(2)}) async-start(bf16[64,16,256]{2,1,0:T(8,128)(2,1)} %broadcast_in_dim.2), calls=%async_computation | async-start | bytes 1048576 | tf_op jit(solution)/shard_map/all_to_all | solution.py:229
  19.3 47.2 %copy-start.3 = (bf16[16,256]{1,0:T(8,128)(2,1)S(1)}, bf16[16,256]{1,0:T(8,128)(2,1)}, u32[]{:S(2)}) copy-start(bf16[16,256]{1,0:T(8,128)(2,1)} %basis_ref.1) | copy-start | bytes 24580
  22.6 61.9 %copy-start = (bf16[384,3584]{1,0:T(8,128)(2,1)S(1)}, bf16[384,3584]{1,0:T(8,128)(2,1)}, u32[]{:S(2)}) copy-start(bf16[384,3584]{1,0:T(8,128)(2,1)} %grad_ref.3) | copy-start | bytes 8257540
  22.7 4.7 %collective-permute-start = (bf16[48,4096]{1,0:T(8,128)(2,1)}, bf16[48,4096]{1,0:T(8,128)(2,1)S(1)}, u32[]{:S(2)}, u32[]{:S(2)}) collective-permute-start(bf16[48,4096]{1,0:T(8,128)(2,1)} %shard_map.76), channel_id=1, source_target_pairs={{0,8},{8,0},{1,9},{9,1},{2,10},{10,2},{3,11},{11,3},{4,12},{12,4},... | collective-permute-start | bytes 1179656 | tf_op jit(solution)/shard_map/ppermute | solution.py:237
  27.3 0.8 copy-start.8
  32.1 10.6 %collective-permute-start.1 = (bf16[96,1024]{1,0:T(8,128)(2,1)}, bf16[96,1024]{1,0:T(8,128)(2,1)S(1)}, u32[]{:S(2)}, u32[]{:S(2)}) collective-permute-start(bf16[96,1024]{1,0:T(8,128)(2,1)} %get-tuple-element.11), channel_id=1, source_target_pairs={{0,1},{1,2},{2,3},{3,0},{4,5},{5,6},{6,7},{7,4},{8,9},{9,10},{10,1... | collective-permute-start | bytes 589832 | tf_op jit(solution)/shard_map/ppermute | solution.py:249
  35.2 11.5 %collective-permute-start.2 = (bf16[96,1024]{1,0:T(8,128)(2,1)}, bf16[96,1024]{1,0:T(8,128)(2,1)S(1)}, u32[]{:S(2)}, u32[]{:S(2)}) collective-permute-start(bf16[96,1024]{1,0:T(8,128)(2,1)} %get-tuple-element.12), channel_id=1, source_target_pairs={{0,2},{1,3},{2,0},{3,1},{4,6},{5,7},{6,4},{7,5},{8,10},{9,11},{10,... | collective-permute-start | bytes 589832 | tf_op jit(solution)/shard_map/ppermute | solution.py:249
  39.6 8.5 %collective-permute-start.3 = (bf16[96,1024]{1,0:T(8,128)(2,1)}, bf16[96,1024]{1,0:T(8,128)(2,1)}, u32[]{:S(2)}, u32[]{:S(2)}) collective-permute-start(bf16[96,1024]{1,0:T(8,128)(2,1)} %get-tuple-element.13), channel_id=1, source_target_pairs={{0,3},{1,0},{2,1},{3,2},{4,7},{5,4},{6,5},{7,6},{8,11},{9,8},{10,9... | collective-permute-start | bytes 589832 | tf_op jit(solution)/shard_map/ppermute | solution.py:249
  42.7 5.5 %copy-start.6 = (bf16[96,1024]{1,0:T(8,128)(2,1)}, bf16[96,1024]{1,0:T(8,128)(2,1)S(1)}, u32[]{:S(2)}) copy-start(bf16[96,1024]{1,0:T(8,128)(2,1)S(1)} %collective-permute-done.1.refs_1_) | copy-start | bytes 589828
  46.7 0.7 copy-start.7
  48.1 0.8 copy-start.5
  66.5 24.0 %copy-start.4 = (s32[2]{0:T(128)S(1)}, s32[2]{0:T(128)}, u32[]{:S(2)}) copy-start(s32[2]{0:T(128)} %pad_add_fusion.at_ref.core_ref) | copy-start | bytes 28
  67.3 17.3 %all-to-all-start.2 = ((bf16[8,64,256]{2,1,0:T(8,128)(2,1)}), bf16[8,64,256]{2,1,0:T(8,128)(2,1)S(1)}, u32[]{:S(2)}, u32[]{:S(2)}) async-start(bf16[8,64,256]{2,1,0:T(8,128)(2,1)} %shard_map.79), calls=%async_computation.2 | async-start | bytes 524288 | tf_op jit(solution)/shard_map/all_to_all | solution.py:229
  86.4 6.2 %collective-permute-start.4 = (bf16[256,1792]{1,0:T(8,128)(2,1)S(1)}, bf16[256,1792]{1,0:T(8,128)(2,1)S(1)}, u32[]{:S(2)}, u32[]{:S(2)}) collective-permute-start(bf16[256,1792]{1,0:T(8,128)(2,1)S(1)} %shard_map.81), channel_id=1, source_target_pairs={{0,8},{8,0},{1,9},{9,1},{2,10},{10,2},{3,11},{11,3},{4,12},{12,4},... | collective-permute-start | bytes 2752520 | tf_op jit(solution)/shard_map/ppermute | solution.py:283
  92.4 32.8 %copy-start.1 = (f32[4,3584]{1,0:T(4,128)S(1)}, f32[4,3584]{1,0:T(4,128)}, u32[]{:S(2)}) copy-start(f32[4,3584]{1,0:T(4,128)} %first_ref.1) | copy-start | bytes 172036
  92.4 32.8 %copy-start.2 = (f32[4,3584]{1,0:T(4,128)S(1)}, f32[4,3584]{1,0:T(4,128)}, u32[]{:S(2)}) copy-start(f32[4,3584]{1,0:T(4,128)} %second_ref.1) | copy-start | bytes 172036
  155.8 7.2 %collective-permute-start.5 = (bf16[256,1792]{1,0:T(8,128)(2,1)S(1)}, bf16[256,1792]{1,0:T(8,128)(2,1)S(1)}, u32[]{:S(2)}, u32[]{:S(2)}) collective-permute-start(bf16[256,1792]{1,0:T(8,128)(2,1)S(1)} %bitcast.13), channel_id=1, source_target_pairs={{0,8},{8,0},{1,9},{9,1},{2,10},{10,2},{3,11},{11,3},{4,12},{12,4},... | collective-permute-start | bytes 2752520 | tf_op jit(solution)/shard_map/ppermute | solution.py:298

commit v5 on v3

--- a/solution.py
+++ b/solution.py
@@ -17,7 +17,6 @@
 EPS = 1e-08
 
 Z, Y_LO, CORE, Y_HI, X = 8, 4, 2, 2, 4
-CLASSES = CORE * X
 OWNERS = Z * Y_LO
 VMEM_LIMIT = 24 * 1024 * 1024
 F32, BF16 = jnp.float32, jnp.bfloat16
@@ -49,61 +48,55 @@
     return jnp.where(condition, 1.0, 0.0).astype(BF16)
 
 
-def side_block(z, y_lo, side):
-    return pl.ds(pl.multiple_of(((z * Y_LO + y_lo) * CORE + side) * 128, 128), 128)
-
-
-def take_sibling(at_ref, tokens_ref, basis_ref, out_ref, copies_ref):
-    side = 1 - at_ref[0]
-    for z in range(Z):
-        for y in range(Y_LO):
-            out_ref[:, (z * Y_LO + y) * 128 : (z * Y_LO + y + 1) * 128] = tokens_ref[
-                :, side_block(z, y, side)
-            ]
-    basis = basis_ref[...]
-    for copy in range(copies_ref.shape[0]):
-        copies_ref[copy] = basis
-
-
-def split_features(at_ref, tokens_ref, sibling_ref, *out_refs):
-    core, here = at_ref[0], at_ref[1]
-    rows = tokens_ref.shape[0]
+def split_features(at_ref, tokens_ref, *out_refs):
+    here = at_ref[1]
     width = Y_LO * 128
     p, q = iota((width, width), 0), iota((width, width), 1)
     steps = (((p >> 4) & 3) - here) & 3
     move = one_hot(steps * 128 + (p >> 7) * 32 + ((p >> 6) & 1) * 16 + (p & 15) == q)
     for z in range(Z):
-        own = jnp.concatenate(
-            [tokens_ref[:, side_block(z, y, core)] for y in range(Y_LO)], axis=1
-        )
-        other = sibling_ref[:, z * width : (z + 1) * width]
-        moved = jnp.dot(
-            jnp.concatenate([own, other], axis=0), move, preferred_element_type=F32
-        ).astype(BF16)
-        for x in range(X):
-            out_refs[x][:, z * 128 : (z + 1) * 128] = moved[:, x * 128 : (x + 1) * 128]
+        for side in range(CORE):
+            block = jnp.concatenate(
+                [
+                    tokens_ref[:, ((z * Y_LO + y) * CORE + side) * 128 :][:, :128]
+                    for y in range(Y_LO)
+                ],
+                axis=1,
+            )
+            moved = jnp.dot(block, move, preferred_element_type=F32).astype(BF16)
+            start = (side * Z + z) * 128
+            for x in range(X):
+                out_refs[x][:, start : start + 128] = moved[:, x * 128 : (x + 1) * 128]
+
+
+def class_part(token_refs, basis_ref, side):
+    width = basis_ref.shape[0]
+    columns = pl.ds(pl.multiple_of(side * width, 128), width)
+    tokens = jnp.concatenate([ref[:, columns] for ref in token_refs], axis=0)
+    return jnp.dot(tokens, basis_ref[...], preferred_element_type=F32)
 
 
 def partial_coefficients(at_ref, basis_ref, *refs):
     *token_refs, out_ref = refs
-    core, here = at_ref[0], at_ref[1]
-    rows = out_ref.shape[1]
-    tokens = jnp.concatenate([ref[...] for ref in token_refs], axis=0)
-    parts = jnp.dot(tokens, basis_ref[...], preferred_element_type=F32)
+    here, rows = at_ref[1], out_ref.shape[1]
+    parts = class_part(token_refs, basis_ref, at_ref[0])
     for step in range(X):
-        x = (here - step) & 3
-        for other in range(CORE):
-            side = core if other == 0 else 1 - core
-            start = (step * CORE + other) * rows
-            out_ref[side * X + x] = parts[start : start + rows, :]
+        out_ref[(here - step) & 3] = parts[step * rows : (step + 1) * rows, :]
+
+
+def whole_coefficients(at_ref, basis_ref, part_ref, *refs):
+    *token_refs, out_ref = refs
+    here, rows = at_ref[1], out_ref.shape[1]
+    parts = class_part(token_refs, basis_ref, 1 - at_ref[0])
+    for step in range(X):
+        place = (here - step) & 3
+        out_ref[place] = part_ref[place] + parts[step * rows : (step + 1) * rows, :]
 
 
 def sum_coefficients(parts_ref, basis_ref, out_ref):
     rows = parts_ref.shape[1]
     own = basis_ref.shape[0]
-    total = parts_ref[0]
-    for part in range(1, CLASSES):
-        total += parts_ref[part]
+    total = (parts_ref[0] + parts_ref[1]) + (parts_ref[2] + parts_ref[3])
     total = total.astype(BF16)
     basis = basis_ref[...]
     for copy in range(out_ref.shape[0]):
@@ -214,38 +207,30 @@
         return lax.all_to_all(array, axes, 0, 0, tiled=True)
 
     copies = Z * Y_LO * Y_HI
-    for_sibling, basis_copies = call(
-        take_sibling,
-        (shape((rows, features // CORE), BF16), shape((copies, own, rank), BF16)),
-        0,
-        2 * (rows * features + copies * own * rank),
-        True,
-    )(at, tokens, basis)
-    sibling = lax.ppermute(for_sibling, "core", swap)
+    basis_copies = jnp.broadcast_to(basis[None], (copies, own, rank))
     class_basis = exchange(basis_copies, ("z", "y_lo", "y_hi")).reshape(copies * own, rank)
-    block = shape((CORE * rows, features // CLASSES), BF16)
-    blocks = call(split_features, (block,) * X, 2 * rows * features * 512, 0, True)(
-        at, tokens, sibling
-    )
+    block = shape((rows, features // X), BF16)
+    blocks = call(split_features, (block,) * X, 2 * rows * features * 512, 0, True)(at, tokens)
     held = [blocks[0]] + [
         lax.ppermute(blocks[step], "x", [(x, (x + step) % X) for x in range(X)])
         for step in range(1, X)
     ]
-    parts = call(
-        partial_coefficients,
-        shape((CLASSES, rows, rank), F32),
-        2 * rows * features * rank,
-        2 * (rows * features + copies * own * rank),
-        True,
-    )(at, class_basis, *held)
-    parts = exchange(parts, ("core", "x"))
+    class_basis, *held = lax.optimization_barrier((class_basis, *held))
+    sibling_basis = lax.ppermute(class_basis, "core", swap)
+    part_shape = shape((X, rows, rank), F32)
+    part_cost = (rows * features * rank, rows * features + copies * own * rank)
+    part = call(partial_coefficients, part_shape, *part_cost, True)(at, class_basis, *held)
+    parts = call(whole_coefficients, part_shape, *part_cost, True)(
+        at, sibling_basis, part, *held
+    )
+    parts = exchange(parts, "x")
     takers = Y_HI * X
     chunk = rows + own
     gathered = exchange(
         call(
             sum_coefficients,
             shape((takers, chunk, rank), BF16),
-            CLASSES * rows * rank,
+            X * rows * rank,
             4 * takers * chunk * rank,
         )(parts, basis),
         ("y_hi", "x"),

time: 163 us -> 155 us (0.951)
  blocking collectives: 75.8 us -> 70.6 us
  waiting for transfers between devices: 17.6 us -> 15.6 us
    all_to_all x3, blocking collectives: 75.8 us -> 70.6 us  [exchange(): return lax.all_to_all(array, axes, 0, 0, tiled=True)]
    unnamed x28 -> x22, local copies, waits for them, and re-layouts: 8.55 us -> 5.94 us
  transfers between devices with their start and end apart: 8 -> 8, of which waited for: 6 -> 6; matrix products, arithmetic and copies ran while one was open for 0% -> 0% of each run, Pallas kernels for 2% -> 3%
where the time goes in v5:
time: 155 us
  blocking collectives  70.6 us (46%)
  starting transfers between devices  48.1 us (31%)
  waiting for transfers between devices  15.6 us (10%)
  Pallas kernels  11.8 us (8%)
  local copies, waits for them, and re-layouts  7.47 us (5%)
    all_to_all x3, blocking collectives, exchange(): return lax.all_to_all(array, axes, 0, 0, tiled=True)  70.6 us
    all_to_all x2, starting transfers between devices, exchange(): return lax.all_to_all(array, axes, 0, 0, tiled=True)  23.3 us
    pallas_call x9, Pallas kernels, run(): pl.pallas_call(body, out_shape=out_shape, in_specs=specs, out_specs=jax.t...  11.8 us
    ppermute x3, starting transfers between devices, per_device(): lax.ppermute(blocks[step], 'x', [(x, (x + step) % X) for x in range(X)])  10.5 us
    all_to_all x2, waiting for transfers between devices, exchange(): return lax.all_to_all(array, axes, 0, 0, tiled=True)  10.1 us
    unnamed x22, local copies, waits for them, and re-layouts  5.94 us
    ppermute x1, starting transfers between devices, per_device(): others = lax.ppermute(directions, 'core', swap)  5.13 us
    ppermute x1, starting transfers between devices, per_device(): theirs = lax.ppermute(projected(sibling_at, BF16), 'core', swap)  4.84 us
  transfers between devices with their start and end apart: 8, of which 6 were waited for; matrix products, arithmetic and copies ran while one was open for 0% of the time, Pallas kernels for 3%

profile of v5, /device:TPU:1, one launch (start us, length us, event | category | flops | bytes accessed | tf_op | source)
XLA Modules:
  0.0 154.6 jit_solution(13903276269239489183)
XLA Ops:
  0.6 1.5 broadcast_in_dim.2
  2.2 17.1 %all-to-all-start = ((bf16[64,16,256]{2,1,0:T(8,128)(2,1)}), bf16[64,16,256]{2,1,0:T(8,128)(2,1)S(1)}, u32[]{:S(2)}, u32[]{:S(2)}) async-start(bf16[64,16,256]{2,1,0:T(8,128)(2,1)} %broadcast_in_dim.2), calls=%async_computation | async-start | bytes 1048576 | tf_op jit(solution)/shard_map/all_to_all | solution.py:207
  19.4 1.1 copy-done.10
  20.5 2.3 %shard_map.76 = (bf16[48,2048]{1,0:T(8,128)(2,1)S(1)}, bf16[48,2048]{1,0:T(8,128)(2,1)S(1)}, bf16[48,2048]{1,0:T(8,128)(2,1)S(1)}, bf16[48,2048]{1,0:T(8,128)(2,1)S(1)}) custom-call(s32[2]{0:T(128)S(1)} %pad_add_fusion.at_ref.core_ref, bf16[48,8192]{1,0:T(8,128)(2,1)S(1)} %copy-done.10), custom_call_target="tpu_custom_call" | custom-call | flops 402653184 | tf_op jit(solution)/shard_map/pallas_call | solution.py:31
  22.8 3.1 %collective-permute-start = (bf16[48,2048]{1,0:T(8,128)(2,1)S(1)}, bf16[48,2048]{1,0:T(8,128)(2,1)S(1)}, u32[]{:S(2)}, u32[]{:S(2)}) collective-permute-start(bf16[48,2048]{1,0:T(8,128)(2,1)S(1)} %get-tuple-element.16), channel_id=1, source_target_pairs={{0,1},{1,2},{2,3},{3,0},{4,5},{5,6},{6,7},{7,4},{8,9},{9,10},{10,1... | collective-permute-start | bytes 589832 | tf_op jit(solution)/shard_map/ppermute | solution.py:215
  25.9 4.4 %collective-permute-start.1 = (bf16[48,2048]{1,0:T(8,128)(2,1)S(1)}, bf16[48,2048]{1,0:T(8,128)(2,1)S(1)}, u32[]{:S(2)}, u32[]{:S(2)}) collective-permute-start(bf16[48,2048]{1,0:T(8,128)(2,1)S(1)} %get-tuple-element.17), channel_id=1, source_target_pairs={{0,2},{1,3},{2,0},{3,1},{4,6},{5,7},{6,4},{7,5},{8,10},{9,11},{10,... | collective-permute-start | bytes 589832 | tf_op jit(solution)/shard_map/ppermute | solution.py:215
  30.3 3.1 %collective-permute-start.2 = (bf16[48,2048]{1,0:T(8,128)(2,1)S(1)}, bf16[48,2048]{1,0:T(8,128)(2,1)S(1)}, u32[]{:S(2)}, u32[]{:S(2)}) collective-permute-start(bf16[48,2048]{1,0:T(8,128)(2,1)S(1)} %get-tuple-element.18), channel_id=1, source_target_pairs={{0,3},{1,0},{2,1},{3,2},{4,7},{5,4},{6,5},{7,6},{8,11},{9,8},{10,9... | collective-permute-start | bytes 589832 | tf_op jit(solution)/shard_map/ppermute | solution.py:215
  34.0 2.5 %collective-permute-done.1.refs_2_ = bf16[48,2048]{1,0:T(8,128)(2,1)S(1)} collective-permute-done((bf16[48,2048]{1,0:T(8,128)(2,1)S(1)}, bf16[48,2048]{1,0:T(8,128)(2,1)S(1)}, u32[]{:S(2)}, u32[]{:S(2)}) %collective-permute-start.1) | collective-permute-done | bytes 196640 | tf_op jit(solution)/shard_map/ppermute | solution.py:215
  38.8 4.3 %collective-permute-start.3 = (bf16[1024,256]{1,0:T(8,128)(2,1)S(1)}, bf16[1024,256]{1,0:T(8,128)(2,1)S(1)}, u32[]{:S(2)}, u32[]{:S(2)}) collective-permute-start(bf16[1024,256]{1,0:T(8,128)(2,1)S(1)} %bitcast.16), channel_id=1, source_target_pairs={{0,8},{8,0},{1,9},{9,1},{2,10},{10,2},{3,11},{11,3},{4,12},{12,4},... | collective-permute-start | bytes 1572872 | tf_op jit(solution)/shard_map/ppermute | solution.py:219
  43.1 0.9 copy-done.2
  44.1 0.9 copy-done.4
  45.0 0.9 copy-done.6
  46.7 0.8 shard_map.78
  47.6 9.3 %all_to_all.37.parts_ref = f32[4,48,256]{2,1,0:T(8,128)S(1)} all-to-all(f32[4,48,256]{2,1,0:T(8,128)S(1)} %shard_map.78), channel_id=1, replica_groups=mesh['z'=8,'y_lo'=4,'core'=2,'y_hi'=2,'x'=4] {'x'}, dimensions={0} | all-to-all | bytes 393216 | tf_op jit(solution)/shard_map/all_to_all | solution.py:207
  57.6 6.2 %all-to-all-start.2 = ((bf16[8,64,256]{2,1,0:T(8,128)(2,1)}), bf16[8,64,256]{2,1,0:T(8,128)(2,1)S(1)}, u32[]{:S(2)}, u32[]{:S(2)}) async-start(bf16[8,64,256]{2,1,0:T(8,128)(2,1)} %shard_map.79), calls=%async_computation.2 | async-start | bytes 524288 | tf_op jit(solution)/shard_map/all_to_all | solution.py:207
  63.9 9.9 %all-to-all-done.2 = bf16[8,64,256]{2,1,0:T(8,128)(2,1)S(1)} async-done(((bf16[8,64,256]{2,1,0:T(8,128)(2,1)}), bf16[8,64,256]{2,1,0:T(8,128)(2,1)S(1)}, u32[]{:S(2)}, u32[]{:S(2)}) %all-to-all-start.2) | async-done | bytes 262176 | tf_op jit(solution)/shard_map/all_to_all | solution.py:207
  73.8 1.8 %shard_map.81 = bf16[256,1792]{1,0:T(8,128)(2,1)S(1)} custom-call(s32[2]{0:T(128)S(1)} %pad_add_fusion.1.core_ref, bf16[512,256]{1,0:T(8,128)(2,1)S(1)} %bitcast.9, bf16[384,3584]{1,0:T(8,128)(2,1)S(1)} %copy-done), custom_call_target="tpu_custom_call" | custom-call | flops 704643072 | bytes 4587520 | tf_op jit(solution)/shard_map/pallas_call | solution.py:31
  75.6 4.8 %collective-permute-start.4 = (bf16[256,1792]{1,0:T(8,128)(2,1)S(1)}, bf16[256,1792]{1,0:T(8,128)(2,1)S(1)}, u32[]{:S(2)}, u32[]{:S(2)}) collective-permute-start(bf16[256,1792]{1,0:T(8,128)(2,1)S(1)} %shard_map.81), channel_id=1, source_target_pairs={{0,8},{8,0},{1,9},{9,1},{2,10},{10,2},{3,11},{11,3},{4,12},{12,4},... | collective-permute-start | bytes 2752520 | tf_op jit(solution)/shard_map/ppermute | solution.py:248
  80.5 1.8 %shard_map.80.mine_ref = f32[256,1792]{1,0:T(8,128)S(1)} custom-call(s32[2]{0:T(128)S(1)} %pad_add_fusion.at_ref.core_ref, bf16[512,256]{1,0:T(8,128)(2,1)S(1)} %bitcast.10, bf16[384,3584]{1,0:T(8,128)(2,1)S(1)} %copy-done), custom_call_target="tpu_custom_call" | custom-call | flops 704643072 | bytes 4587520 | tf_op jit(solution)/shard_map/pallas_call | solution.py:31
  82.8 31.5 %all_to_all.38 = bf16[32,8,1792]{2,1,0:T(8,128)(2,1)S(1)} all-to-all(bf16[32,8,1792]{2,1,0:T(8,128)(2,1)S(1)} %bitcast.12), channel_id=1, replica_groups=mesh['z'=8,'y_lo'=4,'core'=2,'y_hi'=2,'x'=4] {'z','y_lo'}, dimensions={0} | all-to-all | bytes 1835008 | tf_op jit(solution)/shard_map/all_to_all | solution.py:207
  115.1 29.8 %all_to_all.39 = bf16[32,8,1792]{2,1,0:T(8,128)(2,1)S(1)} all-to-all(bf16[32,8,1792]{2,1,0:T(8,128)(2,1)S(1)} %bitcast.18), channel_id=1, replica_groups=mesh['z'=8,'y_lo'=4,'core'=2,'y_hi'=2,'x'=4] {'z','y_lo'}, dimensions={0} | all-to-all | bytes 1835008 | tf_op jit(solution)/shard_map/all_to_all | solution.py:207
  144.9 5.1 %collective-permute-start.5 = (bf16[256,1792]{1,0:T(8,128)(2,1)S(1)}, bf16[256,1792]{1,0:T(8,128)(2,1)S(1)}, u32[]{:S(2)}, u32[]{:S(2)}) collective-permute-start(bf16[256,1792]{1,0:T(8,128)(2,1)S(1)} %bitcast.13), channel_id=1, source_target_pairs={{0,8},{8,0},{1,9},{9,1},{2,10},{10,2},{3,11},{11,3},{4,12},{12,4},... | collective-permute-start | bytes 2752520 | tf_op jit(solution)/shard_map/ppermute | solution.py:263
  150.1 2.1 %collective-permute-done.5.theirs_ref = bf16[256,1792]{1,0:T(8,128)(2,1)S(1)} collective-permute-done((bf16[256,1792]{1,0:T(8,128)(2,1)S(1)}, bf16[256,1792]{1,0:T(8,128)(2,1)S(1)}, u32[]{:S(2)}, u32[]{:S(2)}) %collective-permute-start.5) | collective-permute-done | bytes 917536 | tf_op jit(solution)/shard_map/ppermute | solution.py:263
  152.1 2.5 %shard_map.84 = bf16[128,3584]{1,0:T(8,128)(2,1)} custom-call(s32[2]{0:T(128)S(1)} %pad_add_fusion.at_ref.core_ref, bf16[512,256]{1,0:T(8,128)(2,1)S(1)} %bitcast.11, bf16[256,1792]{1,0:T(8,128)(2,1)S(1)} %bitcast.14, bf16[256,1792]{1,0:T(8,128)(2,1)S(1)} %collective-permute-done.5.theirs_ref), custom_call_target="tpu_custom_call" | custom-call | flops 469762048 | bytes 3670016 | tf_op jit(solution)/shard_map/pallas_call | solution.py:31
  (29 shorter events, 5.9 us)
Async XLA Ops:
  2.2 36.6 %all-to-all-start = ((bf16[64,16,256]{2,1,0:T(8,128)(2,1)}), bf16[64,16,256]{2,1,0:T(8,128)(2,1)S(1)}, u32[]{:S(2)}, u32[]{:S(2)}) async-start(bf16[64,16,256]{2,1,0:T(8,128)(2,1)} %broadcast_in_dim.2), calls=%async_computation | async-start | bytes 1048576 | tf_op jit(solution)/shard_map/all_to_all | solution.py:207
  19.3 37.6 %copy-start.9 = (bf16[16,256]{1,0:T(8,128)(2,1)S(1)}, bf16[16,256]{1,0:T(8,128)(2,1)}, u32[]{:S(2)}) copy-start(bf16[16,256]{1,0:T(8,128)(2,1)} %basis_ref.1) | copy-start | bytes 24580
  19.4 1.1 copy-start.10
  20.5 53.3 %copy-start = (bf16[384,3584]{1,0:T(8,128)(2,1)S(1)}, bf16[384,3584]{1,0:T(8,128)(2,1)}, u32[]{:S(2)}) copy-start(bf16[384,3584]{1,0:T(8,128)(2,1)} %grad_ref.3) | copy-start | bytes 8257540
  22.8 10.6 %collective-permute-start = (bf16[48,2048]{1,0:T(8,128)(2,1)S(1)}, bf16[48,2048]{1,0:T(8,128)(2,1)S(1)}, u32[]{:S(2)}, u32[]{:S(2)}) collective-permute-start(bf16[48,2048]{1,0:T(8,128)(2,1)S(1)} %get-tuple-element.16), channel_id=1, source_target_pairs={{0,1},{1,2},{2,3},{3,0},{4,5},{5,6},{6,7},{7,4},{8,9},{9,10},{10,1... | collective-permute-start | bytes 589832 | tf_op jit(solution)/shard_map/ppermute | solution.py:215
  25.9 10.6 %collective-permute-start.1 = (bf16[48,2048]{1,0:T(8,128)(2,1)S(1)}, bf16[48,2048]{1,0:T(8,128)(2,1)S(1)}, u32[]{:S(2)}, u32[]{:S(2)}) collective-permute-start(bf16[48,2048]{1,0:T(8,128)(2,1)S(1)} %get-tuple-element.17), channel_id=1, source_target_pairs={{0,2},{1,3},{2,0},{3,1},{4,6},{5,7},{6,4},{7,5},{8,10},{9,11},{10,... | collective-permute-start | bytes 589832 | tf_op jit(solution)/shard_map/ppermute | solution.py:215
  30.3 7.6 %collective-permute-start.2 = (bf16[48,2048]{1,0:T(8,128)(2,1)S(1)}, bf16[48,2048]{1,0:T(8,128)(2,1)S(1)}, u32[]{:S(2)}, u32[]{:S(2)}) collective-permute-start(bf16[48,2048]{1,0:T(8,128)(2,1)S(1)} %get-tuple-element.18), channel_id=1, source_target_pairs={{0,3},{1,0},{2,1},{3,2},{4,7},{5,4},{6,5},{7,6},{8,11},{9,8},{10,9... | collective-permute-start | bytes 589832 | tf_op jit(solution)/shard_map/ppermute | solution.py:215
  33.4 0.7 copy-start.1
  36.5 0.7 copy-start.3
  37.9 0.7 copy-start.5
  38.8 7.9 %collective-permute-start.3 = (bf16[1024,256]{1,0:T(8,128)(2,1)S(1)}, bf16[1024,256]{1,0:T(8,128)(2,1)S(1)}, u32[]{:S(2)}, u32[]{:S(2)}) collective-permute-start(bf16[1024,256]{1,0:T(8,128)(2,1)S(1)} %bitcast.16), channel_id=1, source_target_pairs={{0,8},{8,0},{1,9},{9,1},{2,10},{10,2},{3,11},{11,3},{4,12},{12,4},... | collective-permute-start | bytes 1572872 | tf_op jit(solution)/shard_map/ppermute | solution.py:219
  43.1 0.9 copy-start.2
  44.1 0.9 copy-start.4
  45.0 0.9 copy-start.6
  57.6 16.1 %all-to-all-start.2 = ((bf16[8,64,256]{2,1,0:T(8,128)(2,1)}), bf16[8,64,256]{2,1,0:T(8,128)(2,1)S(1)}, u32[]{:S(2)}, u32[]{:S(2)}) async-start(bf16[8,64,256]{2,1,0:T(8,128)(2,1)} %shard_map.79), calls=%async_computation.2 | async-start | bytes 524288 | tf_op jit(solution)/shard_map/all_to_all | solution.py:207
  75.6 6.9 %collective-permute-start.4 = (bf16[256,1792]{1,0:T(8,128)(2,1)S(1)}, bf16[256,1792]{1,0:T(8,128)(2,1)S(1)}, u32[]{:S(2)}, u32[]{:S(2)}) collective-permute-start(bf16[256,1792]{1,0:T(8,128)(2,1)S(1)} %shard_map.81), channel_id=1, source_target_pairs={{0,8},{8,0},{1,9},{9,1},{2,10},{10,2},{3,11},{11,3},{4,12},{12,4},... | collective-permute-start | bytes 2752520 | tf_op jit(solution)/shard_map/ppermute | solution.py:248
  82.3 32.0 %copy-start.7 = (f32[4,3584]{1,0:T(4,128)S(1)}, f32[4,3584]{1,0:T(4,128)}, u32[]{:S(2)}) copy-start(f32[4,3584]{1,0:T(4,128)} %first_ref.1) | copy-start | bytes 172036
  82.3 32.0 %copy-start.8 = (f32[4,3584]{1,0:T(4,128)S(1)}, f32[4,3584]{1,0:T(4,128)}, u32[]{:S(2)}) copy-start(f32[4,3584]{1,0:T(4,128)} %second_ref.1) | copy-start | bytes 172036
  144.9 7.2 %collective-permute-start.5 = (bf16[256,1792]{1,0:T(8,128)(2,1)S(1)}, bf16[256,1792]{1,0:T(8,128)(2,1)S(1)}, u32[]{:S(2)}, u32[]{:S(2)}) collective-permute-start(bf16[256,1792]{1,0:T(8,128)(2,1)S(1)} %bitcast.13), channel_id=1, source_target_pairs={{0,8},{8,0},{1,9},{9,1},{2,10},{10,2},{3,11},{11,3},{4,12},{12,4},... | collective-permute-start | bytes 2752520 | tf_op jit(solution)/shard_map/ppermute | solution.py:263

commit v6 on v5

--- a/solution.py
+++ b/solution.py
@@ -22,22 +22,13 @@
 F32, BF16 = jnp.float32, jnp.bfloat16
 
 
-def call(body, out_shape, flops, moved, placed=False):
-    vmem = pl.BlockSpec(memory_space=pltpu.VMEM)
-    smem = pl.BlockSpec(memory_space=pltpu.SMEM)
-
-    def run(*operands):
-        specs = [smem if placed and n == 0 else vmem for n in range(len(operands))]
-        return pl.pallas_call(
-            body,
-            out_shape=out_shape,
-            in_specs=specs,
-            out_specs=jax.tree.map(lambda _: vmem, out_shape),
-            compiler_params=pltpu.CompilerParams(vmem_limit_bytes=VMEM_LIMIT),
-            cost_estimate=pl.CostEstimate(flops=flops, bytes_accessed=moved, transcendentals=0),
-        )(*operands)
-
-    return run
+def call(body, out_shape, flops, moved):
+    return pl.pallas_call(
+        body,
+        out_shape=out_shape,
+        compiler_params=pltpu.CompilerParams(vmem_limit_bytes=VMEM_LIMIT),
+        cost_estimate=pl.CostEstimate(flops=flops, bytes_accessed=moved, transcendentals=0),
+    )
 
 
 def iota(shape, axis):
@@ -48,8 +39,8 @@
     return jnp.where(condition, 1.0, 0.0).astype(BF16)
 
 
-def split_features(at_ref, tokens_ref, *out_refs):
-    here = at_ref[1]
+def split_features(tokens_ref, *out_refs):
+    here = lax.axis_index("x")
     width = Y_LO * 128
     p, q = iota((width, width), 0), iota((width, width), 1)
     steps = (((p >> 4) & 3) - here) & 3
@@ -58,7 +49,7 @@
         for side in range(CORE):
             block = jnp.concatenate(
                 [
-                    tokens_ref[:, ((z * Y_LO + y) * CORE + side) * 128 :][:, :128]
+                    tokens_ref[:, pl.ds(((z * Y_LO + y) * CORE + side) * 128, 128)]
                     for y in range(Y_LO)
                 ],
                 axis=1,
@@ -76,18 +67,18 @@
     return jnp.dot(tokens, basis_ref[...], preferred_element_type=F32)
 
 
-def partial_coefficients(at_ref, basis_ref, *refs):
+def partial_coefficients(basis_ref, *refs):
     *token_refs, out_ref = refs
-    here, rows = at_ref[1], out_ref.shape[1]
-    parts = class_part(token_refs, basis_ref, at_ref[0])
+    here, rows = lax.axis_index("x"), out_ref.shape[1]
+    parts = class_part(token_refs, basis_ref, lax.axis_index("core"))
     for step in range(X):
         out_ref[(here - step) & 3] = parts[step * rows : (step + 1) * rows, :]
 
 
-def whole_coefficients(at_ref, basis_ref, part_ref, *refs):
+def whole_coefficients(basis_ref, part_ref, *refs):
     *token_refs, out_ref = refs
-    here, rows = at_ref[1], out_ref.shape[1]
-    parts = class_part(token_refs, basis_ref, 1 - at_ref[0])
+    here, rows = lax.axis_index("x"), out_ref.shape[1]
+    parts = class_part(token_refs, basis_ref, 1 - lax.axis_index("core"))
     for step in range(X):
         place = (here - step) & 3
         out_ref[place] = part_ref[place] + parts[step * rows : (step + 1) * rows, :]
@@ -108,8 +99,9 @@
     return (row >> 3) * 8 + core * 4 + (row & 3)
 
 
-def project(scale, core_ref, gathered_ref, grad_ref, out_ref):
-    core = core_ref[0]
+def project(scale, own, gathered_ref, grad_ref, out_ref):
+    core = lax.axis_index("core")
+    core = core if own else 1 - core
     width = out_ref.shape[1]
     chunk = gathered_ref.shape[0] // 8
     tokens = chunk - 16
@@ -164,8 +156,8 @@
         out_ref[part * 16 : (part + 1) * 16, :] = block
 
 
-def expand(core_ref, gathered_ref, mine_ref, theirs_ref, out_ref):
-    core = core_ref[0]
+def expand(gathered_ref, mine_ref, theirs_ref, out_ref):
+    core = lax.axis_index("core")
     chunk = gathered_ref.shape[0] // 8
     basis = jnp.concatenate(
         [gathered_ref[t * chunk + chunk - 16 : (t + 1) * chunk, :] for t in range(8)], axis=0
@@ -198,9 +190,6 @@
     half = columns // 2
     scale = 1.0 / math.sqrt(group_tokens * Z * Y_LO * CORE)
     shape = jax.ShapeDtypeStruct
-    core = lax.axis_index("core").astype(jnp.int32)
-    at = jnp.stack([core, lax.axis_index("x").astype(jnp.int32)])
-    sibling_at = jnp.stack([1 - core, lax.axis_index("x").astype(jnp.int32)])
     swap = [(0, 1), (1, 0)]
 
     def exchange(array, axes):
@@ -210,7 +199,7 @@
     basis_copies = jnp.broadcast_to(basis[None], (copies, own, rank))
     class_basis = exchange(basis_copies, ("z", "y_lo", "y_hi")).reshape(copies * own, rank)
     block = shape((rows, features // X), BF16)
-    blocks = call(split_features, (block,) * X, 2 * rows * features * 512, 0, True)(at, tokens)
+    blocks = call(split_features, (block,) * X, 2 * rows * features * 512, 0)(tokens)
     held = [blocks[0]] + [
         lax.ppermute(blocks[step], "x", [(x, (x + step) % X) for x in range(X)])
         for step in range(1, X)
@@ -219,9 +208,9 @@
     sibling_basis = lax.ppermute(class_basis, "core", swap)
     part_shape = shape((X, rows, rank), F32)
     part_cost = (rows * features * rank, rows * features + copies * own * rank)
-    part = call(partial_coefficients, part_shape, *part_cost, True)(at, class_basis, *held)
-    parts = call(whole_coefficients, part_shape, *part_cost, True)(
-        at, sibling_basis, part, *held
+    part = call(partial_coefficients, part_shape, *part_cost)(class_basis, *held)
+    parts = call(whole_coefficients, part_shape, *part_cost)(
+        sibling_basis, part, *held
     )
     parts = exchange(parts, "x")
     takers = Y_HI * X
@@ -236,17 +225,16 @@
         ("y_hi", "x"),
     ).reshape(takers * chunk, rank)
 
-    def projected(which, dtype):
+    def projected(own_half, dtype):
         return call(
-            functools.partial(project, scale),
+            functools.partial(project, scale, own_half),
             shape((rank, half), dtype),
             2 * rank * group_tokens * columns,
             2 * group_tokens * columns + 2 * rank * columns,
-            True,
-        )(which, gathered, grad_gate)
-
-    theirs = lax.ppermute(projected(sibling_at, BF16), "core", swap)
-    mine = projected(at, F32)
+            )(gathered, grad_gate)
+
+    theirs = lax.ppermute(projected(False, BF16), "core", swap)
+    mine = projected(True, F32)
     pair = call(add_halves, shape((rank, half), BF16), rank * half, 8 * rank * half)(mine, theirs)
     owned = exchange(pair, ("z", "y_lo"))
     first_out, second_out, direction = call(
@@ -266,8 +254,7 @@
         shape((own * takers, columns), BF16),
         4 * own * takers * rank * columns,
         4 * rank * columns,
-        True,
-    )(at, gathered, directions, others)
+    )(gathered, directions, others)
     return (update, first_out, second_out)
 
 

time: 155 us -> 152 us (0.981)
  blocking collectives: 70.6 us -> 86 us
  waiting for transfers between devices: 15.6 us -> 6.85 us
  starting transfers between devices: 48.1 us -> 42.1 us
  Pallas kernels: 11.8 us -> 7.78 us
    all_to_all x3 -> x4, blocking collectives: 70.6 us -> 86 us  [exchange(): return lax.all_to_all(array, axes, 0, 0, tiled=True)]
    all_to_all x2 -> x1, waiting for transfers between devices: 10.1 us -> 0.84 us  [exchange(): return lax.all_to_all(array, axes, 0, 0, tiled=True)]
    all_to_all x2 -> x1, starting transfers between devices: 23.3 us -> 17.3 us  [exchange(): return lax.all_to_all(array, axes, 0, 0, tiled=True)]
    pallas_call x9, Pallas kernels: 11.8 us -> 7.78 us  [the longest x2 2.61 us: projected(): call(functools.partial(project, scale, own_half), shape((rank, half), dty...]
  transfers between devices with their start and end apart: 8 -> 7, of which waited for: 6 -> 5; matrix products, arithmetic and copies ran while one was open for 0% -> 0% of each run, Pallas kernels for 3% -> 2%
where the time goes in v6:
time: 152 us; the launch traced here: 151 us
  blocking collectives  86 us (57%)
  starting transfers between devices  42.1 us (28%)
  Pallas kernels  7.78 us (5%)
  local copies, waits for them, and re-layouts  7.46 us (5%)
  waiting for transfers between devices  6.85 us (5%)
    all_to_all x4, blocking collectives, exchange(): return lax.all_to_all(array, axes, 0, 0, tiled=True)  86 us
    all_to_all x1, starting transfers between devices, exchange(): return lax.all_to_all(array, axes, 0, 0, tiled=True)  17.3 us
    ppermute x3, starting transfers between devices, per_device(): lax.ppermute(blocks[step], 'x', [(x, (x + step) % X) for x in range(X)])  10.5 us
    unnamed x22, local copies, waits for them, and re-layouts  5.94 us
    ppermute x1, starting transfers between devices, per_device(): others = lax.ppermute(directions, 'core', swap)  5.13 us
    ppermute x1, starting transfers between devices, per_device(): theirs = lax.ppermute(projected(False, BF16), 'core', swap)  4.84 us
    ppermute x1, starting transfers between devices, per_device(): sibling_basis = lax.ppermute(class_basis, 'core', swap)  4.32 us
    ppermute x3, waiting for transfers between devices, per_device(): lax.ppermute(blocks[step], 'x', [(x, (x + step) % X) for x in range(X)])  3.19 us
  transfers between devices with their start and end apart: 7, of which 5 were waited for; matrix products, arithmetic and copies ran while one was open for 0% of the time, Pallas kernels for 2%

profile of v6, /device:TPU:1, one launch (start us, length us, event | category | flops | bytes accessed | tf_op | source)
XLA Modules:
  0.0 151.0 jit_solution(17796340285718598234)
XLA Ops:
  0.6 1.5 %broadcast_in_dim.2 = bf16[64,16,256]{2,1,0:T(8,128)(2,1)} broadcast(bf16[16,256]{1,0:T(8,128)(2,1)} %basis_ref.1), dimensions={1,2} | broadcast | bytes 532480 | tf_op jit(solution)/shard_map/broadcast_in_dim | solution.py:199
  2.2 17.3 %all-to-all-start = ((bf16[64,16,256]{2,1,0:T(8,128)(2,1)}), bf16[64,16,256]{2,1,0:T(8,128)(2,1)S(1)}, u32[]{:S(2)}, u32[]{:S(2)}) async-start(bf16[64,16,256]{2,1,0:T(8,128)(2,1)} %broadcast_in_dim.2), calls=%async_computation | async-start | bytes 1048576 | tf_op jit(solution)/shard_map/all_to_all | solution.py:196
  19.4 1.1 copy-done.10
  20.6 1.7 %shard_map.76 = (bf16[48,2048]{1,0:T(8,128)(2,1)S(1)}, bf16[48,2048]{1,0:T(8,128)(2,1)S(1)}, bf16[48,2048]{1,0:T(8,128)(2,1)S(1)}, bf16[48,2048]{1,0:T(8,128)(2,1)S(1)}) custom-call(bf16[48,8192]{1,0:T(8,128)(2,1)S(1)} %copy-done.10), custom_call_target="tpu_custom_call" | custom-call | flops 402653184 | tf_op jit(solution)/shard_map/pallas_call | solution.py:202
  22.3 3.1 %collective-permute-start = (bf16[48,2048]{1,0:T(8,128)(2,1)S(1)}, bf16[48,2048]{1,0:T(8,128)(2,1)S(1)}, u32[]{:S(2)}, u32[]{:S(2)}) collective-permute-start(bf16[48,2048]{1,0:T(8,128)(2,1)S(1)} %get-tuple-element.16), channel_id=1, source_target_pairs={{0,1},{1,2},{2,3},{3,0},{4,5},{5,6},{6,7},{7,4},{8,9},{9,10},{10,1... | collective-permute-start | bytes 589832 | tf_op jit(solution)/shard_map/ppermute | solution.py:204
  25.4 4.4 %collective-permute-start.1 = (bf16[48,2048]{1,0:T(8,128)(2,1)S(1)}, bf16[48,2048]{1,0:T(8,128)(2,1)S(1)}, u32[]{:S(2)}, u32[]{:S(2)}) collective-permute-start(bf16[48,2048]{1,0:T(8,128)(2,1)S(1)} %get-tuple-element.17), channel_id=1, source_target_pairs={{0,2},{1,3},{2,0},{3,1},{4,6},{5,7},{6,4},{7,5},{8,10},{9,11},{10,... | collective-permute-start | bytes 589832 | tf_op jit(solution)/shard_map/ppermute | solution.py:204
  29.8 3.1 %collective-permute-start.2 = (bf16[48,2048]{1,0:T(8,128)(2,1)S(1)}, bf16[48,2048]{1,0:T(8,128)(2,1)S(1)}, u32[]{:S(2)}, u32[]{:S(2)}) collective-permute-start(bf16[48,2048]{1,0:T(8,128)(2,1)S(1)} %get-tuple-element.18), channel_id=1, source_target_pairs={{0,3},{1,0},{2,1},{3,2},{4,7},{5,4},{6,5},{7,6},{8,11},{9,8},{10,9... | collective-permute-start | bytes 589832 | tf_op jit(solution)/shard_map/ppermute | solution.py:204
  33.6 2.5 %collective-permute-done.1.refs_2_ = bf16[48,2048]{1,0:T(8,128)(2,1)S(1)} collective-permute-done((bf16[48,2048]{1,0:T(8,128)(2,1)S(1)}, bf16[48,2048]{1,0:T(8,128)(2,1)S(1)}, u32[]{:S(2)}, u32[]{:S(2)}) %collective-permute-start.1) | collective-permute-done | bytes 196640 | tf_op jit(solution)/shard_map/ppermute | solution.py:204
  38.1 0.8 all-to-all-done
  38.9 4.3 %collective-permute-start.3 = (bf16[1024,256]{1,0:T(8,128)(2,1)S(1)}, bf16[1024,256]{1,0:T(8,128)(2,1)S(1)}, u32[]{:S(2)}, u32[]{:S(2)}) collective-permute-start(bf16[1024,256]{1,0:T(8,128)(2,1)S(1)} %bitcast.13), channel_id=1, source_target_pairs={{0,8},{8,0},{1,9},{9,1},{2,10},{10,2},{3,11},{11,3},{4,12},{12,4},... | collective-permute-start | bytes 1572872 | tf_op jit(solution)/shard_map/ppermute | solution.py:208
  43.3 0.9 copy-done.2
  44.2 0.9 copy-done.4
  45.1 0.9 copy-done.6
  46.6 9.3 %all_to_all.37.parts_ref = f32[4,48,256]{2,1,0:T(8,128)S(1)} all-to-all(f32[4,48,256]{2,1,0:T(8,128)S(1)} %shard_map.78), channel_id=1, replica_groups=mesh['z'=8,'y_lo'=4,'core'=2,'y_hi'=2,'x'=4] {'x'}, dimensions={0} | all-to-all | bytes 393216 | tf_op jit(solution)/shard_map/all_to_all | solution.py:196
  56.0 15.3 %all_to_all.38 = bf16[8,64,256]{2,1,0:T(8,128)(2,1)S(1)} all-to-all(bf16[8,64,256]{2,1,0:T(8,128)(2,1)S(1)} %shard_map.79), channel_id=1, replica_groups=mesh['z'=8,'y_lo'=4,'core'=2,'y_hi'=2,'x'=4] {'y_hi','x'}, dimensions={0} | all-to-all | bytes 524288 | tf_op jit(solution)/shard_map/all_to_all | solution.py:196
  71.3 1.3 shard_map.81
  72.6 4.8 %collective-permute-start.4 = (bf16[256,1792]{1,0:T(8,128)(2,1)S(1)}, bf16[256,1792]{1,0:T(8,128)(2,1)S(1)}, u32[]{:S(2)}, u32[]{:S(2)}) collective-permute-start(bf16[256,1792]{1,0:T(8,128)(2,1)S(1)} %shard_map.81), channel_id=1, source_target_pairs={{0,8},{8,0},{1,9},{9,1},{2,10},{10,2},{3,11},{11,3},{4,12},{12,4},... | collective-permute-start | bytes 2752520 | tf_op jit(solution)/shard_map/ppermute | solution.py:236
  77.5 1.3 shard_map.80.mine_ref
  79.7 31.5 %all_to_all.39 = bf16[32,8,1792]{2,1,0:T(8,128)(2,1)S(1)} all-to-all(bf16[32,8,1792]{2,1,0:T(8,128)(2,1)S(1)} %bitcast.9), channel_id=1, replica_groups=mesh['z'=8,'y_lo'=4,'core'=2,'y_hi'=2,'x'=4] {'z','y_lo'}, dimensions={0} | all-to-all | bytes 1835008 | tf_op jit(solution)/shard_map/all_to_all | solution.py:196
  111.2 0.8 shard_map.83
  112.0 29.8 %all_to_all.40 = bf16[32,8,1792]{2,1,0:T(8,128)(2,1)S(1)} all-to-all(bf16[32,8,1792]{2,1,0:T(8,128)(2,1)S(1)} %bitcast.15), channel_id=1, replica_groups=mesh['z'=8,'y_lo'=4,'core'=2,'y_hi'=2,'x'=4] {'z','y_lo'}, dimensions={0} | all-to-all | bytes 1835008 | tf_op jit(solution)/shard_map/all_to_all | solution.py:196
  141.8 5.1 %collective-permute-start.5 = (bf16[256,1792]{1,0:T(8,128)(2,1)S(1)}, bf16[256,1792]{1,0:T(8,128)(2,1)S(1)}, u32[]{:S(2)}, u32[]{:S(2)}) collective-permute-start(bf16[256,1792]{1,0:T(8,128)(2,1)S(1)} %bitcast.10), channel_id=1, source_target_pairs={{0,8},{8,0},{1,9},{9,1},{2,10},{10,2},{3,11},{11,3},{4,12},{12,4},... | collective-permute-start | bytes 2752520 | tf_op jit(solution)/shard_map/ppermute | solution.py:251
  146.9 2.1 %collective-permute-done.5.theirs_ref = bf16[256,1792]{1,0:T(8,128)(2,1)S(1)} collective-permute-done((bf16[256,1792]{1,0:T(8,128)(2,1)S(1)}, bf16[256,1792]{1,0:T(8,128)(2,1)S(1)}, u32[]{:S(2)}, u32[]{:S(2)}) %collective-permute-start.5) | collective-permute-done | bytes 917536 | tf_op jit(solution)/shard_map/ppermute | solution.py:251
  149.0 2.0 %shard_map.84 = bf16[128,3584]{1,0:T(8,128)(2,1)} custom-call(bf16[512,256]{1,0:T(8,128)(2,1)S(1)} %bitcast.8, bf16[256,1792]{1,0:T(8,128)(2,1)S(1)} %bitcast.11, bf16[256,1792]{1,0:T(8,128)(2,1)S(1)} %collective-permute-done.5.theirs_ref), custom_call_target="tpu_custom_call" | custom-call | flops 469762048 | bytes 3670016 | tf_op jit(solution)/shard_map/pallas_call | solution.py:252
  (26 shorter events, 4.2 us)
Async XLA Ops:
  2.2 53.8 %copy-start.9 = (bf16[16,256]{1,0:T(8,128)(2,1)S(1)}, bf16[16,256]{1,0:T(8,128)(2,1)}, u32[]{:S(2)}) copy-start(bf16[16,256]{1,0:T(8,128)(2,1)} %basis_ref.1) | copy-start | bytes 24580
  2.2 36.8 %all-to-all-start = ((bf16[64,16,256]{2,1,0:T(8,128)(2,1)}), bf16[64,16,256]{2,1,0:T(8,128)(2,1)S(1)}, u32[]{:S(2)}, u32[]{:S(2)}) async-start(bf16[64,16,256]{2,1,0:T(8,128)(2,1)} %broadcast_in_dim.2), calls=%async_computation | async-start | bytes 1048576 | tf_op jit(solution)/shard_map/all_to_all | solution.py:196
  19.4 1.1 copy-start.10
  20.6 50.8 %copy-start = (bf16[384,3584]{1,0:T(8,128)(2,1)S(1)}, bf16[384,3584]{1,0:T(8,128)(2,1)}, u32[]{:S(2)}) copy-start(bf16[384,3584]{1,0:T(8,128)(2,1)} %grad_ref.3) | copy-start | bytes 8257540
  22.3 10.6 %collective-permute-start = (bf16[48,2048]{1,0:T(8,128)(2,1)S(1)}, bf16[48,2048]{1,0:T(8,128)(2,1)S(1)}, u32[]{:S(2)}, u32[]{:S(2)}) collective-permute-start(bf16[48,2048]{1,0:T(8,128)(2,1)S(1)} %get-tuple-element.16), channel_id=1, source_target_pairs={{0,1},{1,2},{2,3},{3,0},{4,5},{5,6},{6,7},{7,4},{8,9},{9,10},{10,1... | collective-permute-start | bytes 589832 | tf_op jit(solution)/shard_map/ppermute | solution.py:204
  25.4 10.6 %collective-permute-start.1 = (bf16[48,2048]{1,0:T(8,128)(2,1)S(1)}, bf16[48,2048]{1,0:T(8,128)(2,1)S(1)}, u32[]{:S(2)}, u32[]{:S(2)}) collective-permute-start(bf16[48,2048]{1,0:T(8,128)(2,1)S(1)} %get-tuple-element.17), channel_id=1, source_target_pairs={{0,2},{1,3},{2,0},{3,1},{4,6},{5,7},{6,4},{7,5},{8,10},{9,11},{10,... | collective-permute-start | bytes 589832 | tf_op jit(solution)/shard_map/ppermute | solution.py:204
  29.8 7.6 %collective-permute-start.2 = (bf16[48,2048]{1,0:T(8,128)(2,1)S(1)}, bf16[48,2048]{1,0:T(8,128)(2,1)S(1)}, u32[]{:S(2)}, u32[]{:S(2)}) collective-permute-start(bf16[48,2048]{1,0:T(8,128)(2,1)S(1)} %get-tuple-element.18), channel_id=1, source_target_pairs={{0,3},{1,0},{2,1},{3,2},{4,7},{5,4},{6,5},{7,6},{8,11},{9,8},{10,9... | collective-permute-start | bytes 589832 | tf_op jit(solution)/shard_map/ppermute | solution.py:204
  32.9 0.7 copy-start.1
  36.1 0.7 copy-start.3
  37.4 0.7 copy-start.5
  38.9 7.4 %collective-permute-start.3 = (bf16[1024,256]{1,0:T(8,128)(2,1)S(1)}, bf16[1024,256]{1,0:T(8,128)(2,1)S(1)}, u32[]{:S(2)}, u32[]{:S(2)}) collective-permute-start(bf16[1024,256]{1,0:T(8,128)(2,1)S(1)} %bitcast.13), channel_id=1, source_target_pairs={{0,8},{8,0},{1,9},{9,1},{2,10},{10,2},{3,11},{11,3},{4,12},{12,4},... | collective-permute-start | bytes 1572872 | tf_op jit(solution)/shard_map/ppermute | solution.py:208
  43.3 0.9 copy-start.2
  44.2 0.9 copy-start.4
  45.1 0.9 copy-start.6
  72.6 6.9 %collective-permute-start.4 = (bf16[256,1792]{1,0:T(8,128)(2,1)S(1)}, bf16[256,1792]{1,0:T(8,128)(2,1)S(1)}, u32[]{:S(2)}, u32[]{:S(2)}) collective-permute-start(bf16[256,1792]{1,0:T(8,128)(2,1)S(1)} %shard_map.81), channel_id=1, source_target_pairs={{0,8},{8,0},{1,9},{9,1},{2,10},{10,2},{3,11},{11,3},{4,12},{12,4},... | collective-permute-start | bytes 2752520 | tf_op jit(solution)/shard_map/ppermute | solution.py:236
  78.8 32.5 %copy-start.7 = (f32[4,3584]{1,0:T(4,128)S(1)}, f32[4,3584]{1,0:T(4,128)}, u32[]{:S(2)}) copy-start(f32[4,3584]{1,0:T(4,128)} %first_ref.1) | copy-start | bytes 172036
  78.8 32.4 %copy-start.8 = (f32[4,3584]{1,0:T(4,128)S(1)}, f32[4,3584]{1,0:T(4,128)}, u32[]{:S(2)}) copy-start(f32[4,3584]{1,0:T(4,128)} %second_ref.1) | copy-start | bytes 172036
  141.8 7.2 %collective-permute-start.5 = (bf16[256,1792]{1,0:T(8,128)(2,1)S(1)}, bf16[256,1792]{1,0:T(8,128)(2,1)S(1)}, u32[]{:S(2)}, u32[]{:S(2)}) collective-permute-start(bf16[256,1792]{1,0:T(8,128)(2,1)S(1)} %bitcast.10), channel_id=1, source_target_pairs={{0,8},{8,0},{1,9},{9,1},{2,10},{10,2},{3,11},{11,3},{4,12},{12,4},... | collective-permute-start | bytes 2752520 | tf_op jit(solution)/shard_map/ppermute | solution.py:251

commit v7 on v6

--- a/solution.py
+++ b/solution.py
@@ -60,25 +60,29 @@
                 out_refs[x][:, start : start + 128] = moved[:, x * 128 : (x + 1) * 128]
 
 
-def class_part(token_refs, basis_ref, side):
+def stack(*refs):
+    *block_refs, out_ref = refs
+    rows = block_refs[0].shape[0]
+    for step, ref in enumerate(block_refs):
+        out_ref[step * rows : (step + 1) * rows, :] = ref[...]
+
+
+def class_part(tokens_ref, basis_ref, side):
     width = basis_ref.shape[0]
     columns = pl.ds(pl.multiple_of(side * width, 128), width)
-    tokens = jnp.concatenate([ref[:, columns] for ref in token_refs], axis=0)
-    return jnp.dot(tokens, basis_ref[...], preferred_element_type=F32)
-
-
-def partial_coefficients(basis_ref, *refs):
-    *token_refs, out_ref = refs
+    return jnp.dot(tokens_ref[:, columns], basis_ref[...], preferred_element_type=F32)
+
+
+def partial_coefficients(basis_ref, tokens_ref, out_ref):
     here, rows = lax.axis_index("x"), out_ref.shape[1]
-    parts = class_part(token_refs, basis_ref, lax.axis_index("core"))
+    parts = class_part(tokens_ref, basis_ref, lax.axis_index("core"))
     for step in range(X):
         out_ref[(here - step) & 3] = parts[step * rows : (step + 1) * rows, :]
 
 
-def whole_coefficients(basis_ref, part_ref, *refs):
-    *token_refs, out_ref = refs
+def whole_coefficients(basis_ref, part_ref, tokens_ref, out_ref):
     here, rows = lax.axis_index("x"), out_ref.shape[1]
-    parts = class_part(token_refs, basis_ref, 1 - lax.axis_index("core"))
+    parts = class_part(tokens_ref, basis_ref, 1 - lax.axis_index("core"))
     for step in range(X):
         place = (here - step) & 3
         out_ref[place] = part_ref[place] + parts[step * rows : (step + 1) * rows, :]
@@ -156,29 +160,45 @@
         out_ref[part * 16 : (part + 1) * 16, :] = block
 
 
-def expand(gathered_ref, mine_ref, theirs_ref, out_ref):
+def arrange_basis(gathered_ref, out_ref):
     core = lax.axis_index("core")
     chunk = gathered_ref.shape[0] // 8
     basis = jnp.concatenate(
         [gathered_ref[t * chunk + chunk - 16 : (t + 1) * chunk, :] for t in range(8)], axis=0
     )
     rank = basis.shape[1]
-    width = mine_ref.shape[1]
     r, place = iota((rank, rank), 0), iota((rank, rank), 1)
+    for which in range(CORE):
+        side = core if which == 0 else 1 - core
+        for half in range(2):
+            move = one_hot((r == rank_of(place, side)) & (((place >> 2) & 1) == half))
+            out_ref[2 * which + half] = jnp.dot(
+                basis, move, preferred_element_type=F32
+            ).astype(BF16)
+
+
+def expand_own(basis_ref, directions_ref, out_ref):
+    width = directions_ref.shape[1]
+    tile = 256
     for half in range(2):
-        in_half = ((place >> 2) & 1) == half
-        own = one_hot((r == rank_of(place, core)) & in_half)
-        other = one_hot((r == rank_of(place, 1 - core)) & in_half)
-        own_basis = jnp.dot(basis, own, preferred_element_type=F32).astype(BF16)
-        other_basis = jnp.dot(basis, other, preferred_element_type=F32).astype(BF16)
-        tile = 256
+        basis = basis_ref[half]
         for start in range(0, width, tile):
-            out_ref[:, half * width + start : half * width + start + tile] = (
-                jnp.dot(
-                    own_basis, mine_ref[:, start : start + tile], preferred_element_type=F32
-                )
+            out_ref[:, half * width + start : half * width + start + tile] = jnp.dot(
+                basis, directions_ref[:, start : start + tile], preferred_element_type=F32
+            )
+
+
+def expand(basis_ref, part_ref, directions_ref, out_ref):
+    width = directions_ref.shape[1]
+    tile = 256
+    for half in range(2):
+        basis = basis_ref[2 + half]
+        for start in range(0, width, tile):
+            columns = slice(half * width + start, half * width + start + tile)
+            out_ref[:, columns] = (
+                part_ref[:, columns]
                 + jnp.dot(
-                    other_basis, theirs_ref[:, start : start + tile], preferred_element_type=F32
+                    basis, directions_ref[:, start : start + tile], preferred_element_type=F32
                 )
             ).astype(BF16)
 
@@ -204,13 +224,16 @@
         lax.ppermute(blocks[step], "x", [(x, (x + step) % X) for x in range(X)])
         for step in range(1, X)
     ]
-    class_basis, *held = lax.optimization_barrier((class_basis, *held))
+    stacked = call(
+        stack, shape((X * rows, features // X), BF16), rows * features, 4 * rows * features
+    )(*held)
+    class_basis, stacked = lax.optimization_barrier((class_basis, stacked))
     sibling_basis = lax.ppermute(class_basis, "core", swap)
     part_shape = shape((X, rows, rank), F32)
     part_cost = (rows * features * rank, rows * features + copies * own * rank)
-    part = call(partial_coefficients, part_shape, *part_cost)(class_basis, *held)
+    part = call(partial_coefficients, part_shape, *part_cost)(class_basis, stacked)
     parts = call(whole_coefficients, part_shape, *part_cost)(
-        sibling_basis, part, *held
+        sibling_basis, part, stacked
     )
     parts = exchange(parts, "x")
     takers = Y_HI * X
@@ -249,12 +272,13 @@
     )(owned, first_moment, second_moment)
     directions = exchange(direction, ("z", "y_lo"))
     others = lax.ppermute(directions, "core", swap)
-    update = call(
-        expand,
-        shape((own * takers, columns), BF16),
-        4 * own * takers * rank * columns,
-        4 * rank * columns,
-    )(gathered, directions, others)
+    update_rows = own * takers
+    bases = call(
+        arrange_basis, shape((4, update_rows, rank), BF16), 8 * update_rows * rank * rank, 0
+    )(gathered)
+    cost = (4 * update_rows * rank * half, 4 * update_rows * columns)
+    part = call(expand_own, shape((update_rows, columns), F32), *cost)(bases, directions)
+    update = call(expand, shape((update_rows, columns), BF16), *cost)(bases, part, others)
     return (update, first_out, second_out)
 
 

time: 152 us -> 149 us (0.980)
  local copies, waits for them, and re-layouts: 7.46 us -> 2.68 us
  waiting for transfers between devices: 6.85 us -> 9.38 us
    unnamed x22 -> x10, local copies, waits for them, and re-layouts: 5.94 us -> 1.15 us
  transfers between devices with their start and end apart: 7 -> 7, of which waited for: 5 -> 6; matrix products, arithmetic and copies ran while one was open for 0% -> 0% of each run, Pallas kernels for 2% -> 3%
where the time goes in v7:
time: 149 us; the launch traced here: 148 us
  blocking collectives  85.1 us (57%)
  starting transfers between devices  42.3 us (28%)
  waiting for transfers between devices  9.38 us (6%)
  Pallas kernels  7.88 us (5%)
  local copies, waits for them, and re-layouts  2.68 us (2%)
    all_to_all x4, blocking collectives, exchange(): return lax.all_to_all(array, axes, 0, 0, tiled=True)  85.1 us
    all_to_all x1, starting transfers between devices, exchange(): return lax.all_to_all(array, axes, 0, 0, tiled=True)  17.1 us
    ppermute x3, starting transfers between devices, per_device(): lax.ppermute(blocks[step], 'x', [(x, (x + step) % X) for x in range(X)])  10.5 us
    ppermute x1, starting transfers between devices, per_device(): others = lax.ppermute(directions, 'core', swap)  5.13 us
    ppermute x1, starting transfers between devices, per_device(): theirs = lax.ppermute(projected(False, BF16), 'core', swap)  5.12 us
    ppermute x3, waiting for transfers between devices, per_device(): lax.ppermute(blocks[step], 'x', [(x, (x + step) % X) for x in range(X)])  4.53 us
    ppermute x1, starting transfers between devices, per_device(): sibling_basis = lax.ppermute(class_basis, 'core', swap)  4.32 us
  transfers between devices with their start and end apart: 7, of which 6 were waited for; matrix products, arithmetic and copies ran while one was open for 0% of the time, Pallas kernels for 3%

profile of v7, /device:TPU:1, one launch (start us, length us, event | category | flops | bytes accessed | tf_op | source)
XLA Modules:
  0.0 148.1 jit_solution(17952114923134679244)
XLA Ops:
  0.6 1.5 %broadcast_in_dim.2 = bf16[64,16,256]{2,1,0:T(8,128)(2,1)} broadcast(bf16[16,256]{1,0:T(8,128)(2,1)} %basis_ref.1), dimensions={1,2} | broadcast | bytes 532480 | tf_op jit(solution)/shard_map/broadcast_in_dim | solution.py:219
  2.2 17.1 %all-to-all-start = ((bf16[64,16,256]{2,1,0:T(8,128)(2,1)}), bf16[64,16,256]{2,1,0:T(8,128)(2,1)S(1)}, u32[]{:S(2)}, u32[]{:S(2)}) async-start(bf16[64,16,256]{2,1,0:T(8,128)(2,1)} %broadcast_in_dim.2), calls=%async_computation | async-start | bytes 1048576 | tf_op jit(solution)/shard_map/all_to_all | solution.py:216
  19.3 1.1 copy-done.4
  20.4 1.7 %shard_map.76 = (bf16[48,2048]{1,0:T(8,128)(2,1)S(1)}, bf16[48,2048]{1,0:T(8,128)(2,1)S(1)}, bf16[48,2048]{1,0:T(8,128)(2,1)S(1)}, bf16[48,2048]{1,0:T(8,128)(2,1)S(1)}) custom-call(bf16[48,8192]{1,0:T(8,128)(2,1)S(1)} %copy-done.4), custom_call_target="tpu_custom_call" | custom-call | flops 402653184 | tf_op jit(solution)/shard_map/pallas_call | solution.py:222
  22.2 3.1 %collective-permute-start = (bf16[48,2048]{1,0:T(8,128)(2,1)S(1)}, bf16[48,2048]{1,0:T(8,128)(2,1)S(1)}, u32[]{:S(2)}, u32[]{:S(2)}) collective-permute-start(bf16[48,2048]{1,0:T(8,128)(2,1)S(1)} %get-tuple-element.13), channel_id=1, source_target_pairs={{0,1},{1,2},{2,3},{3,0},{4,5},{5,6},{6,7},{7,4},{8,9},{9,10},{10,1... | collective-permute-start | bytes 589832 | tf_op jit(solution)/shard_map/ppermute | solution.py:224
  25.3 4.4 %collective-permute-start.1 = (bf16[48,2048]{1,0:T(8,128)(2,1)S(1)}, bf16[48,2048]{1,0:T(8,128)(2,1)S(1)}, u32[]{:S(2)}, u32[]{:S(2)}) collective-permute-start(bf16[48,2048]{1,0:T(8,128)(2,1)S(1)} %get-tuple-element.14), channel_id=1, source_target_pairs={{0,2},{1,3},{2,0},{3,1},{4,6},{5,7},{6,4},{7,5},{8,10},{9,11},{10,... | collective-permute-start | bytes 589832 | tf_op jit(solution)/shard_map/ppermute | solution.py:224
  29.7 3.1 %collective-permute-start.2 = (bf16[48,2048]{1,0:T(8,128)(2,1)S(1)}, bf16[48,2048]{1,0:T(8,128)(2,1)S(1)}, u32[]{:S(2)}, u32[]{:S(2)}) collective-permute-start(bf16[48,2048]{1,0:T(8,128)(2,1)S(1)} %get-tuple-element.15), channel_id=1, source_target_pairs={{0,3},{1,0},{2,1},{3,2},{4,7},{5,4},{6,5},{7,6},{8,11},{9,8},{10,9... | collective-permute-start | bytes 589832 | tf_op jit(solution)/shard_map/ppermute | solution.py:224
  32.8 3.2 %collective-permute-done.1.refs_2_ = bf16[48,2048]{1,0:T(8,128)(2,1)S(1)} collective-permute-done((bf16[48,2048]{1,0:T(8,128)(2,1)S(1)}, bf16[48,2048]{1,0:T(8,128)(2,1)S(1)}, u32[]{:S(2)}, u32[]{:S(2)}) %collective-permute-start.1) | collective-permute-done | bytes 196640 | tf_op jit(solution)/shard_map/ppermute | solution.py:224
  35.9 1.4 collective-permute-done.2.refs_3_
  37.4 1.5 all-to-all-done
  38.8 4.3 %collective-permute-start.3 = (bf16[1024,256]{1,0:T(8,128)(2,1)S(1)}, bf16[1024,256]{1,0:T(8,128)(2,1)S(1)}, u32[]{:S(2)}, u32[]{:S(2)}) collective-permute-start(bf16[1024,256]{1,0:T(8,128)(2,1)S(1)} %bitcast.13), channel_id=1, source_target_pairs={{0,8},{8,0},{1,9},{9,1},{2,10},{10,2},{3,11},{11,3},{4,12},{12,4},... | collective-permute-start | bytes 1572872 | tf_op jit(solution)/shard_map/ppermute | solution.py:231
  43.4 1.2 collective-permute-done.3.basis_ref
  44.9 9.1 %all_to_all.37.parts_ref = f32[4,48,256]{2,1,0:T(8,128)S(1)} all-to-all(f32[4,48,256]{2,1,0:T(8,128)S(1)} %shard_map.79), channel_id=1, replica_groups=mesh['z'=8,'y_lo'=4,'core'=2,'y_hi'=2,'x'=4] {'x'}, dimensions={0} | all-to-all | bytes 393216 | tf_op jit(solution)/shard_map/all_to_all | solution.py:216
  54.1 14.8 %all_to_all.38 = bf16[8,64,256]{2,1,0:T(8,128)(2,1)S(1)} all-to-all(bf16[8,64,256]{2,1,0:T(8,128)(2,1)S(1)} %shard_map.80), channel_id=1, replica_groups=mesh['z'=8,'y_lo'=4,'core'=2,'y_hi'=2,'x'=4] {'y_hi','x'}, dimensions={0} | all-to-all | bytes 524288 | tf_op jit(solution)/shard_map/all_to_all | solution.py:216
  68.8 1.3 shard_map.83
  70.1 5.1 %collective-permute-start.4 = (bf16[256,1792]{1,0:T(8,128)(2,1)S(1)}, bf16[256,1792]{1,0:T(8,128)(2,1)S(1)}, u32[]{:S(2)}, u32[]{:S(2)}) collective-permute-start(bf16[256,1792]{1,0:T(8,128)(2,1)S(1)} %shard_map.83), channel_id=1, source_target_pairs={{0,8},{8,0},{1,9},{9,1},{2,10},{10,2},{3,11},{11,3},{4,12},{12,4},... | collective-permute-start | bytes 2752520 | tf_op jit(solution)/shard_map/ppermute | solution.py:259
  75.3 1.3 shard_map.82.mine_ref
  76.6 0.8 collective-permute-done.4.theirs_ref
  77.5 31.5 %all_to_all.39 = bf16[32,8,1792]{2,1,0:T(8,128)(2,1)S(1)} all-to-all(bf16[32,8,1792]{2,1,0:T(8,128)(2,1)S(1)} %bitcast.9), channel_id=1, replica_groups=mesh['z'=8,'y_lo'=4,'core'=2,'y_hi'=2,'x'=4] {'z','y_lo'}, dimensions={0} | all-to-all | bytes 1835008 | tf_op jit(solution)/shard_map/all_to_all | solution.py:216
  109.0 0.8 shard_map.85
  109.8 29.8 %all_to_all.40 = bf16[32,8,1792]{2,1,0:T(8,128)(2,1)S(1)} all-to-all(bf16[32,8,1792]{2,1,0:T(8,128)(2,1)S(1)} %bitcast.15), channel_id=1, replica_groups=mesh['z'=8,'y_lo'=4,'core'=2,'y_hi'=2,'x'=4] {'z','y_lo'}, dimensions={0} | all-to-all | bytes 1835008 | tf_op jit(solution)/shard_map/all_to_all | solution.py:216
  139.6 5.1 %collective-permute-start.5 = (bf16[256,1792]{1,0:T(8,128)(2,1)S(1)}, bf16[256,1792]{1,0:T(8,128)(2,1)S(1)}, u32[]{:S(2)}, u32[]{:S(2)}) collective-permute-start(bf16[256,1792]{1,0:T(8,128)(2,1)S(1)} %bitcast.10), channel_id=1, source_target_pairs={{0,8},{8,0},{1,9},{9,1},{2,10},{10,2},{3,11},{11,3},{4,12},{12,4},... | collective-permute-start | bytes 2752520 | tf_op jit(solution)/shard_map/ppermute | solution.py:274
  145.4 1.4 collective-permute-done.5.directions_ref
  146.8 1.3 shard_map.87
  (17 shorter events, 1.5 us)
Async XLA Ops:
  2.2 36.6 %all-to-all-start = ((bf16[64,16,256]{2,1,0:T(8,128)(2,1)}), bf16[64,16,256]{2,1,0:T(8,128)(2,1)S(1)}, u32[]{:S(2)}, u32[]{:S(2)}) async-start(bf16[64,16,256]{2,1,0:T(8,128)(2,1)} %broadcast_in_dim.2), calls=%async_computation | async-start | bytes 1048576 | tf_op jit(solution)/shard_map/all_to_all | solution.py:216
  19.3 1.1 copy-start.4
  22.2 10.6 %collective-permute-start = (bf16[48,2048]{1,0:T(8,128)(2,1)S(1)}, bf16[48,2048]{1,0:T(8,128)(2,1)S(1)}, u32[]{:S(2)}, u32[]{:S(2)}) collective-permute-start(bf16[48,2048]{1,0:T(8,128)(2,1)S(1)} %get-tuple-element.13), channel_id=1, source_target_pairs={{0,1},{1,2},{2,3},{3,0},{4,5},{5,6},{6,7},{7,4},{8,9},{9,10},{10,1... | collective-permute-start | bytes 589832 | tf_op jit(solution)/shard_map/ppermute | solution.py:224
  25.3 10.6 %collective-permute-start.1 = (bf16[48,2048]{1,0:T(8,128)(2,1)S(1)}, bf16[48,2048]{1,0:T(8,128)(2,1)S(1)}, u32[]{:S(2)}, u32[]{:S(2)}) collective-permute-start(bf16[48,2048]{1,0:T(8,128)(2,1)S(1)} %get-tuple-element.14), channel_id=1, source_target_pairs={{0,2},{1,3},{2,0},{3,1},{4,6},{5,7},{6,4},{7,5},{8,10},{9,11},{10,... | collective-permute-start | bytes 589832 | tf_op jit(solution)/shard_map/ppermute | solution.py:224
  29.7 7.6 %collective-permute-start.2 = (bf16[48,2048]{1,0:T(8,128)(2,1)S(1)}, bf16[48,2048]{1,0:T(8,128)(2,1)S(1)}, u32[]{:S(2)}, u32[]{:S(2)}) collective-permute-start(bf16[48,2048]{1,0:T(8,128)(2,1)S(1)} %get-tuple-element.15), channel_id=1, source_target_pairs={{0,3},{1,0},{2,1},{3,2},{4,7},{5,4},{6,5},{7,6},{8,11},{9,8},{10,9... | collective-permute-start | bytes 589832 | tf_op jit(solution)/shard_map/ppermute | solution.py:224
  37.3 16.7 %copy-start.3 = (bf16[16,256]{1,0:T(8,128)(2,1)S(1)}, bf16[16,256]{1,0:T(8,128)(2,1)}, u32[]{:S(2)}) copy-start(bf16[16,256]{1,0:T(8,128)(2,1)} %basis_ref.1) | copy-start | bytes 24580
  38.8 5.8 %collective-permute-start.3 = (bf16[1024,256]{1,0:T(8,128)(2,1)S(1)}, bf16[1024,256]{1,0:T(8,128)(2,1)S(1)}, u32[]{:S(2)}, u32[]{:S(2)}) collective-permute-start(bf16[1024,256]{1,0:T(8,128)(2,1)S(1)} %bitcast.13), channel_id=1, source_target_pairs={{0,8},{8,0},{1,9},{9,1},{2,10},{10,2},{3,11},{11,3},{4,12},{12,4},... | collective-permute-start | bytes 1572872 | tf_op jit(solution)/shard_map/ppermute | solution.py:231
  43.4 25.4 %copy-start = (bf16[384,3584]{1,0:T(8,128)(2,1)S(1)}, bf16[384,3584]{1,0:T(8,128)(2,1)}, u32[]{:S(2)}) copy-start(bf16[384,3584]{1,0:T(8,128)(2,1)} %grad_ref.3) | copy-start | bytes 8257540
  70.1 7.2 %collective-permute-start.4 = (bf16[256,1792]{1,0:T(8,128)(2,1)S(1)}, bf16[256,1792]{1,0:T(8,128)(2,1)S(1)}, u32[]{:S(2)}, u32[]{:S(2)}) collective-permute-start(bf16[256,1792]{1,0:T(8,128)(2,1)S(1)} %shard_map.83), channel_id=1, source_target_pairs={{0,8},{8,0},{1,9},{9,1},{2,10},{10,2},{3,11},{11,3},{4,12},{12,4},... | collective-permute-start | bytes 2752520 | tf_op jit(solution)/shard_map/ppermute | solution.py:259
  77.5 31.5 %copy-start.1 = (f32[4,3584]{1,0:T(4,128)S(1)}, f32[4,3584]{1,0:T(4,128)}, u32[]{:S(2)}) copy-start(f32[4,3584]{1,0:T(4,128)} %first_ref.1) | copy-start | bytes 172036
  77.5 31.5 %copy-start.2 = (f32[4,3584]{1,0:T(4,128)S(1)}, f32[4,3584]{1,0:T(4,128)}, u32[]{:S(2)}) copy-start(f32[4,3584]{1,0:T(4,128)} %second_ref.1) | copy-start | bytes 172036
  139.6 7.2 %collective-permute-start.5 = (bf16[256,1792]{1,0:T(8,128)(2,1)S(1)}, bf16[256,1792]{1,0:T(8,128)(2,1)S(1)}, u32[]{:S(2)}, u32[]{:S(2)}) collective-permute-start(bf16[256,1792]{1,0:T(8,128)(2,1)S(1)} %bitcast.10), channel_id=1, source_target_pairs={{0,8},{8,0},{1,9},{9,1},{2,10},{10,2},{3,11},{11,3},{4,12},{12,4},... | collective-permute-start | bytes 2752520 | tf_op jit(solution)/shard_map/ppermute | solution.py:274

commit v8 on v7

--- a/solution.py
+++ b/solution.py
@@ -138,6 +138,19 @@
     out_ref[...] = (mine_ref[...] + theirs_ref[...].astype(F32)).astype(BF16)
 
 
+def sum_planes(parts_ref, out_ref):
+    total = parts_ref[0].astype(F32)
+    for part in range(1, parts_ref.shape[0]):
+        total += parts_ref[part].astype(F32)
+    out_ref[...] = total.astype(BF16)
+
+
+def repeat(block_ref, out_ref):
+    block = block_ref[...]
+    for copy in range(out_ref.shape[0]):
+        out_ref[copy] = block
+
+
 def adam(parts_ref, first_ref, second_ref, first_out_ref, second_out_ref, out_ref):
     rows, width = 4, parts_ref.shape[1]
     total = parts_ref[0:16, :].astype(F32)
@@ -259,18 +272,23 @@
     theirs = lax.ppermute(projected(False, BF16), "core", swap)
     mine = projected(True, F32)
     pair = call(add_halves, shape((rank, half), BF16), rank * half, 8 * rank * half)(mine, theirs)
-    owned = exchange(pair, ("z", "y_lo"))
+    plane = rank // Z
+    planes = exchange(pair.reshape(Z, plane, half), "z")
+    summed = call(sum_planes, shape((plane, half), BF16), rank * half, 2 * rank * half)(planes)
+    owned = exchange(summed, "y_lo")
     first_out, second_out, direction = call(
         adam,
         (
             shape(first_moment.shape, F32),
             shape(second_moment.shape, F32),
-            shape((rank, half), BF16),
+            shape((plane, half), BF16),
         ),
         rank * half,
         4 * rank * half,
     )(owned, first_moment, second_moment)
-    directions = exchange(direction, ("z", "y_lo"))
+    line = exchange(direction, "y_lo")
+    planes = call(repeat, shape((Z, plane, half), BF16), 0, 2 * rank * half)(line)
+    directions = exchange(planes, "z").reshape(rank, half)
     others = lax.ppermute(directions, "core", swap)
     update_rows = own * takers
     bases = call(

time: 149 us -> 160 us (1.074)
  blocking collectives: 85.1 us -> 94 us
  starting transfers between devices: 42.3 us -> 44.5 us
    all_to_all x4 -> x6, blocking collectives: 85.1 us -> 94 us  [exchange(): return lax.all_to_all(array, axes, 0, 0, tiled=True)]
    ppermute x1, starting transfers between devices: 5.13 us -> 7.37 us  [per_device(): others = lax.ppermute(directions, 'core', swap)]
where the time goes in v8:
time: 160 us; the launch traced here: 159 us
  blocking collectives  94 us (59%)
  starting transfers between devices  44.5 us (28%)
  waiting for transfers between devices  9.38 us (6%)
  Pallas kernels  7.96 us (5%)
  local copies, waits for them, and re-layouts  2.68 us (2%)
    all_to_all x6, blocking collectives, exchange(): return lax.all_to_all(array, axes, 0, 0, tiled=True)  94 us
    all_to_all x1, starting transfers between devices, exchange(): return lax.all_to_all(array, axes, 0, 0, tiled=True)  17.1 us
    ppermute x3, starting transfers between devices, per_device(): lax.ppermute(blocks[step], 'x', [(x, (x + step) % X) for x in range(X)])  10.5 us
    ppermute x1, starting transfers between devices, per_device(): others = lax.ppermute(directions, 'core', swap)  7.37 us
    ppermute x1, starting transfers between devices, per_device(): theirs = lax.ppermute(projected(False, BF16), 'core', swap)  5.12 us
    ppermute x3, waiting for transfers between devices, per_device(): lax.ppermute(blocks[step], 'x', [(x, (x + step) % X) for x in range(X)])  4.53 us
    ppermute x1, starting transfers between devices, per_device(): sibling_basis = lax.ppermute(class_basis, 'core', swap)  4.32 us
  transfers between devices with their start and end apart: 7, of which 6 were waited for; matrix products, arithmetic and copies ran while one was open for 0% of the time, Pallas kernels for 3%

profile of v8, /device:TPU:1, one launch (start us, length us, event | category | flops | bytes accessed | tf_op | source)
XLA Modules:
  0.0 159.4 jit_solution(3794156333732624694)
XLA Ops:
  0.6 1.5 broadcast_in_dim.2
  2.2 17.1 %all-to-all-start = ((bf16[64,16,256]{2,1,0:T(8,128)(2,1)}), bf16[64,16,256]{2,1,0:T(8,128)(2,1)S(1)}, u32[]{:S(2)}, u32[]{:S(2)}) async-start(bf16[64,16,256]{2,1,0:T(8,128)(2,1)} %broadcast_in_dim.2), calls=%async_computation | async-start | bytes 1048576 | tf_op jit(solution)/shard_map/all_to_all | solution.py:229
  19.3 1.1 copy-done.4
  20.4 1.7 %shard_map.76 = (bf16[48,2048]{1,0:T(8,128)(2,1)S(1)}, bf16[48,2048]{1,0:T(8,128)(2,1)S(1)}, bf16[48,2048]{1,0:T(8,128)(2,1)S(1)}, bf16[48,2048]{1,0:T(8,128)(2,1)S(1)}) custom-call(bf16[48,8192]{1,0:T(8,128)(2,1)S(1)} %copy-done.4), custom_call_target="tpu_custom_call" | custom-call | flops 402653184 | tf_op jit(solution)/shard_map/pallas_call | solution.py:235
  22.2 3.1 %collective-permute-start = (bf16[48,2048]{1,0:T(8,128)(2,1)S(1)}, bf16[48,2048]{1,0:T(8,128)(2,1)S(1)}, u32[]{:S(2)}, u32[]{:S(2)}) collective-permute-start(bf16[48,2048]{1,0:T(8,128)(2,1)S(1)} %get-tuple-element.13), channel_id=1, source_target_pairs={{0,1},{1,2},{2,3},{3,0},{4,5},{5,6},{6,7},{7,4},{8,9},{9,10},{10,1... | collective-permute-start | bytes 589832 | tf_op jit(solution)/shard_map/ppermute | solution.py:237
  25.3 4.4 %collective-permute-start.1 = (bf16[48,2048]{1,0:T(8,128)(2,1)S(1)}, bf16[48,2048]{1,0:T(8,128)(2,1)S(1)}, u32[]{:S(2)}, u32[]{:S(2)}) collective-permute-start(bf16[48,2048]{1,0:T(8,128)(2,1)S(1)} %get-tuple-element.14), channel_id=1, source_target_pairs={{0,2},{1,3},{2,0},{3,1},{4,6},{5,7},{6,4},{7,5},{8,10},{9,11},{10,... | collective-permute-start | bytes 589832 | tf_op jit(solution)/shard_map/ppermute | solution.py:237
  29.7 3.1 %collective-permute-start.2 = (bf16[48,2048]{1,0:T(8,128)(2,1)S(1)}, bf16[48,2048]{1,0:T(8,128)(2,1)S(1)}, u32[]{:S(2)}, u32[]{:S(2)}) collective-permute-start(bf16[48,2048]{1,0:T(8,128)(2,1)S(1)} %get-tuple-element.15), channel_id=1, source_target_pairs={{0,3},{1,0},{2,1},{3,2},{4,7},{5,4},{6,5},{7,6},{8,11},{9,8},{10,9... | collective-permute-start | bytes 589832 | tf_op jit(solution)/shard_map/ppermute | solution.py:237
  32.8 3.2 %collective-permute-done.1.refs_2_ = bf16[48,2048]{1,0:T(8,128)(2,1)S(1)} collective-permute-done((bf16[48,2048]{1,0:T(8,128)(2,1)S(1)}, bf16[48,2048]{1,0:T(8,128)(2,1)S(1)}, u32[]{:S(2)}, u32[]{:S(2)}) %collective-permute-start.1) | collective-permute-done | bytes 196640 | tf_op jit(solution)/shard_map/ppermute | solution.py:237
  35.9 1.4 collective-permute-done.2.refs_3_
  37.4 1.5 all-to-all-done
  38.8 4.3 %collective-permute-start.3 = (bf16[1024,256]{1,0:T(8,128)(2,1)S(1)}, bf16[1024,256]{1,0:T(8,128)(2,1)S(1)}, u32[]{:S(2)}, u32[]{:S(2)}) collective-permute-start(bf16[1024,256]{1,0:T(8,128)(2,1)S(1)} %bitcast.14), channel_id=1, source_target_pairs={{0,8},{8,0},{1,9},{9,1},{2,10},{10,2},{3,11},{11,3},{4,12},{12,4},... | collective-permute-start | bytes 1572872 | tf_op jit(solution)/shard_map/ppermute | solution.py:244
  43.4 1.2 collective-permute-done.3.basis_ref
  44.9 9.1 %all_to_all.47.parts_ref = f32[4,48,256]{2,1,0:T(8,128)S(1)} all-to-all(f32[4,48,256]{2,1,0:T(8,128)S(1)} %shard_map.79), channel_id=1, replica_groups=mesh['z'=8,'y_lo'=4,'core'=2,'y_hi'=2,'x'=4] {'x'}, dimensions={0} | all-to-all | bytes 393216 | tf_op jit(solution)/shard_map/all_to_all | solution.py:229
  54.1 14.8 %all_to_all.48 = bf16[8,64,256]{2,1,0:T(8,128)(2,1)S(1)} all-to-all(bf16[8,64,256]{2,1,0:T(8,128)(2,1)S(1)} %shard_map.80), channel_id=1, replica_groups=mesh['z'=8,'y_lo'=4,'core'=2,'y_hi'=2,'x'=4] {'y_hi','x'}, dimensions={0} | all-to-all | bytes 524288 | tf_op jit(solution)/shard_map/all_to_all | solution.py:229
  68.8 1.3 shard_map.83
  70.1 5.1 %collective-permute-start.4 = (bf16[256,1792]{1,0:T(8,128)(2,1)S(1)}, bf16[256,1792]{1,0:T(8,128)(2,1)S(1)}, u32[]{:S(2)}, u32[]{:S(2)}) collective-permute-start(bf16[256,1792]{1,0:T(8,128)(2,1)S(1)} %shard_map.83), channel_id=1, source_target_pairs={{0,8},{8,0},{1,9},{9,1},{2,10},{10,2},{3,11},{11,3},{4,12},{12,4},... | collective-permute-start | bytes 2752520 | tf_op jit(solution)/shard_map/ppermute | solution.py:272
  75.3 1.3 shard_map.82.mine_ref
  77.5 31.5 %all_to_all.49.parts_ref = bf16[8,32,1792]{2,1,0:T(8,128)(2,1)S(1)} all-to-all(bf16[8,32,1792]{2,1,0:T(8,128)(2,1)S(1)} %bitcast.11), channel_id=1, replica_groups=mesh['z'=8,'y_lo'=4,'core'=2,'y_hi'=2,'x'=4] {'z'}, dimensions={0} | all-to-all | bytes 1835008 | tf_op jit(solution)/shard_map/all_to_all | solution.py:229
  109.1 7.8 %all_to_all.50 = bf16[4,8,1792]{2,1,0:T(8,128)(2,1)S(1)} all-to-all(bf16[4,8,1792]{2,1,0:T(8,128)(2,1)S(1)} %bitcast.17), channel_id=1, replica_groups=mesh['z'=8,'y_lo'=4,'core'=2,'y_hi'=2,'x'=4] {'y_lo'}, dimensions={0} | all-to-all | bytes 229376 | tf_op jit(solution)/shard_map/all_to_all | solution.py:229
  117.6 7.1 %all_to_all.51 = bf16[4,8,1792]{2,1,0:T(8,128)(2,1)S(1)} all-to-all(bf16[4,8,1792]{2,1,0:T(8,128)(2,1)S(1)} %bitcast.19), channel_id=1, replica_groups=mesh['z'=8,'y_lo'=4,'core'=2,'y_hi'=2,'x'=4] {'y_lo'}, dimensions={0} | all-to-all | bytes 229376 | tf_op jit(solution)/shard_map/all_to_all | solution.py:229
  124.8 23.8 %all_to_all.52 = bf16[8,32,1792]{2,1,0:T(8,128)(2,1)S(1)} all-to-all(bf16[8,32,1792]{2,1,0:T(8,128)(2,1)S(1)} %shard_map.87), channel_id=1, replica_groups=mesh['z'=8,'y_lo'=4,'core'=2,'y_hi'=2,'x'=4] {'z'}, dimensions={0} | all-to-all | bytes 1835008 | tf_op jit(solution)/shard_map/all_to_all | solution.py:229
  148.6 7.4 %collective-permute-start.5 = (bf16[256,1792]{1,0:T(8,128)(2,1)S(1)}, bf16[256,1792]{1,0:T(8,128)(2,1)S(1)}, u32[]{:S(2)}, u32[]{:S(2)}) collective-permute-start(bf16[256,1792]{1,0:T(8,128)(2,1)S(1)} %bitcast.12), channel_id=1, source_target_pairs={{0,8},{8,0},{1,9},{9,1},{2,10},{10,2},{3,11},{11,3},{4,12},{12,4},... | collective-permute-start | bytes 2752520 | tf_op jit(solution)/shard_map/ppermute | solution.py:292
  156.6 1.4 collective-permute-done.5.directions_ref
  158.0 1.3 shard_map.89
  (21 shorter events, 3.1 us)
Async XLA Ops:
  2.2 36.6 %all-to-all-start = ((bf16[64,16,256]{2,1,0:T(8,128)(2,1)}), bf16[64,16,256]{2,1,0:T(8,128)(2,1)S(1)}, u32[]{:S(2)}, u32[]{:S(2)}) async-start(bf16[64,16,256]{2,1,0:T(8,128)(2,1)} %broadcast_in_dim.2), calls=%async_computation | async-start | bytes 1048576 | tf_op jit(solution)/shard_map/all_to_all | solution.py:229
  19.3 1.1 copy-start.4
  22.2 10.6 %collective-permute-start = (bf16[48,2048]{1,0:T(8,128)(2,1)S(1)}, bf16[48,2048]{1,0:T(8,128)(2,1)S(1)}, u32[]{:S(2)}, u32[]{:S(2)}) collective-permute-start(bf16[48,2048]{1,0:T(8,128)(2,1)S(1)} %get-tuple-element.13), channel_id=1, source_target_pairs={{0,1},{1,2},{2,3},{3,0},{4,5},{5,6},{6,7},{7,4},{8,9},{9,10},{10,1... | collective-permute-start | bytes 589832 | tf_op jit(solution)/shard_map/ppermute | solution.py:237
  25.3 10.6 %collective-permute-start.1 = (bf16[48,2048]{1,0:T(8,128)(2,1)S(1)}, bf16[48,2048]{1,0:T(8,128)(2,1)S(1)}, u32[]{:S(2)}, u32[]{:S(2)}) collective-permute-start(bf16[48,2048]{1,0:T(8,128)(2,1)S(1)} %get-tuple-element.14), channel_id=1, source_target_pairs={{0,2},{1,3},{2,0},{3,1},{4,6},{5,7},{6,4},{7,5},{8,10},{9,11},{10,... | collective-permute-start | bytes 589832 | tf_op jit(solution)/shard_map/ppermute | solution.py:237
  29.7 7.6 %collective-permute-start.2 = (bf16[48,2048]{1,0:T(8,128)(2,1)S(1)}, bf16[48,2048]{1,0:T(8,128)(2,1)S(1)}, u32[]{:S(2)}, u32[]{:S(2)}) collective-permute-start(bf16[48,2048]{1,0:T(8,128)(2,1)S(1)} %get-tuple-element.15), channel_id=1, source_target_pairs={{0,3},{1,0},{2,1},{3,2},{4,7},{5,4},{6,5},{7,6},{8,11},{9,8},{10,9... | collective-permute-start | bytes 589832 | tf_op jit(solution)/shard_map/ppermute | solution.py:237
  37.3 16.7 %copy-start.3 = (bf16[16,256]{1,0:T(8,128)(2,1)S(1)}, bf16[16,256]{1,0:T(8,128)(2,1)}, u32[]{:S(2)}) copy-start(bf16[16,256]{1,0:T(8,128)(2,1)} %basis_ref.1) | copy-start | bytes 24580
  38.8 5.8 %collective-permute-start.3 = (bf16[1024,256]{1,0:T(8,128)(2,1)S(1)}, bf16[1024,256]{1,0:T(8,128)(2,1)S(1)}, u32[]{:S(2)}, u32[]{:S(2)}) collective-permute-start(bf16[1024,256]{1,0:T(8,128)(2,1)S(1)} %bitcast.14), channel_id=1, source_target_pairs={{0,8},{8,0},{1,9},{9,1},{2,10},{10,2},{3,11},{11,3},{4,12},{12,4},... | collective-permute-start | bytes 1572872 | tf_op jit(solution)/shard_map/ppermute | solution.py:244
  43.4 25.4 %copy-start = (bf16[384,3584]{1,0:T(8,128)(2,1)S(1)}, bf16[384,3584]{1,0:T(8,128)(2,1)}, u32[]{:S(2)}) copy-start(bf16[384,3584]{1,0:T(8,128)(2,1)} %grad_ref.3) | copy-start | bytes 8257540
  70.1 7.2 %collective-permute-start.4 = (bf16[256,1792]{1,0:T(8,128)(2,1)S(1)}, bf16[256,1792]{1,0:T(8,128)(2,1)S(1)}, u32[]{:S(2)}, u32[]{:S(2)}) collective-permute-start(bf16[256,1792]{1,0:T(8,128)(2,1)S(1)} %shard_map.83), channel_id=1, source_target_pairs={{0,8},{8,0},{1,9},{9,1},{2,10},{10,2},{3,11},{11,3},{4,12},{12,4},... | collective-permute-start | bytes 2752520 | tf_op jit(solution)/shard_map/ppermute | solution.py:272
  77.5 39.4 %copy-start.1 = (f32[4,3584]{1,0:T(4,128)S(1)}, f32[4,3584]{1,0:T(4,128)}, u32[]{:S(2)}) copy-start(f32[4,3584]{1,0:T(4,128)} %first_ref.1) | copy-start | bytes 172036
  77.5 39.4 %copy-start.2 = (f32[4,3584]{1,0:T(4,128)S(1)}, f32[4,3584]{1,0:T(4,128)}, u32[]{:S(2)}) copy-start(f32[4,3584]{1,0:T(4,128)} %second_ref.1) | copy-start | bytes 172036
  148.6 9.5 %collective-permute-start.5 = (bf16[256,1792]{1,0:T(8,128)(2,1)S(1)}, bf16[256,1792]{1,0:T(8,128)(2,1)S(1)}, u32[]{:S(2)}, u32[]{:S(2)}) collective-permute-start(bf16[256,1792]{1,0:T(8,128)(2,1)S(1)} %bitcast.12), channel_id=1, source_target_pairs={{0,8},{8,0},{1,9},{9,1},{2,10},{10,2},{3,11},{11,3},{4,12},{12,4},... | collective-permute-start | bytes 2752520 | tf_op jit(solution)/shard_map/ppermute | solution.py:292

commit v9 on v7

--- a/solution.py
+++ b/solution.py
@@ -100,7 +100,7 @@
 
 
 def rank_of(row, core):
-    return (row >> 3) * 8 + core * 4 + (row & 3)
+    return ((row >> 3) & 7) * 32 + (row >> 6) * 8 + core * 4 + (row & 3)
 
 
 def project(scale, own, gathered_ref, grad_ref, out_ref):
@@ -259,7 +259,7 @@
     theirs = lax.ppermute(projected(False, BF16), "core", swap)
     mine = projected(True, F32)
     pair = call(add_halves, shape((rank, half), BF16), rank * half, 8 * rank * half)(mine, theirs)
-    owned = exchange(pair, ("z", "y_lo"))
+    owned = exchange(pair, ("y_lo", "z"))
     first_out, second_out, direction = call(
         adam,
         (
@@ -270,7 +270,7 @@
         rank * half,
         4 * rank * half,
     )(owned, first_moment, second_moment)
-    directions = exchange(direction, ("z", "y_lo"))
+    directions = exchange(direction, ("y_lo", "z"))
     others = lax.ppermute(directions, "core", swap)
     update_rows = own * takers
     bases = call(

time: 149 us -> 149 us (level)
  no operation moved by 1% of the time
where the time goes in v9:
time: 149 us; the launch traced here: 148 us
  blocking collectives  85.7 us (58%)
  starting transfers between devices  41.9 us (28%)
  waiting for transfers between devices  9.38 us (6%)
  Pallas kernels  7.88 us (5%)
  local copies, waits for them, and re-layouts  2.68 us (2%)
    all_to_all x4, blocking collectives, exchange(): return lax.all_to_all(array, axes, 0, 0, tiled=True)  85.7 us
    all_to_all x1, starting transfers between devices, exchange(): return lax.all_to_all(array, axes, 0, 0, tiled=True)  17.1 us
    ppermute x3, starting transfers between devices, per_device(): lax.ppermute(blocks[step], 'x', [(x, (x + step) % X) for x in range(X)])  10.5 us
    ppermute x1, starting transfers between devices, per_device(): theirs = lax.ppermute(projected(False, BF16), 'core', swap)  5.12 us
    ppermute x1, starting transfers between devices, per_device(): others = lax.ppermute(directions, 'core', swap)  4.74 us
    ppermute x3, waiting for transfers between devices, per_device(): lax.ppermute(blocks[step], 'x', [(x, (x + step) % X) for x in range(X)])  4.53 us
    ppermute x1, starting transfers between devices, per_device(): sibling_basis = lax.ppermute(class_basis, 'core', swap)  4.32 us
  transfers between devices with their start and end apart: 7, of which 6 were waited for; matrix products, arithmetic and copies ran while one was open for 0% of the time, Pallas kernels for 3%

profile of v9, /device:TPU:1, one launch (start us, length us, event | category | flops | bytes accessed | tf_op | source)
XLA Modules:
  0.0 148.3 jit_solution(13853282574853725715)
XLA Ops:
  0.6 1.5 %broadcast_in_dim.2 = bf16[64,16,256]{2,1,0:T(8,128)(2,1)} broadcast(bf16[16,256]{1,0:T(8,128)(2,1)} %basis_ref.1), dimensions={1,2} | broadcast | bytes 532480 | tf_op jit(solution)/shard_map/broadcast_in_dim | solution.py:219
  2.2 17.1 %all-to-all-start = ((bf16[64,16,256]{2,1,0:T(8,128)(2,1)}), bf16[64,16,256]{2,1,0:T(8,128)(2,1)S(1)}, u32[]{:S(2)}, u32[]{:S(2)}) async-start(bf16[64,16,256]{2,1,0:T(8,128)(2,1)} %broadcast_in_dim.2), calls=%async_computation | async-start | bytes 1048576 | tf_op jit(solution)/shard_map/all_to_all | solution.py:216
  19.3 1.1 copy-done.4
  20.4 1.7 %shard_map.76 = (bf16[48,2048]{1,0:T(8,128)(2,1)S(1)}, bf16[48,2048]{1,0:T(8,128)(2,1)S(1)}, bf16[48,2048]{1,0:T(8,128)(2,1)S(1)}, bf16[48,2048]{1,0:T(8,128)(2,1)S(1)}) custom-call(bf16[48,8192]{1,0:T(8,128)(2,1)S(1)} %copy-done.4), custom_call_target="tpu_custom_call" | custom-call | flops 402653184 | tf_op jit(solution)/shard_map/pallas_call | solution.py:222
  22.2 3.1 %collective-permute-start = (bf16[48,2048]{1,0:T(8,128)(2,1)S(1)}, bf16[48,2048]{1,0:T(8,128)(2,1)S(1)}, u32[]{:S(2)}, u32[]{:S(2)}) collective-permute-start(bf16[48,2048]{1,0:T(8,128)(2,1)S(1)} %get-tuple-element.13), channel_id=1, source_target_pairs={{0,1},{1,2},{2,3},{3,0},{4,5},{5,6},{6,7},{7,4},{8,9},{9,10},{10,1... | collective-permute-start | bytes 589832 | tf_op jit(solution)/shard_map/ppermute | solution.py:224
  25.3 4.4 %collective-permute-start.1 = (bf16[48,2048]{1,0:T(8,128)(2,1)S(1)}, bf16[48,2048]{1,0:T(8,128)(2,1)S(1)}, u32[]{:S(2)}, u32[]{:S(2)}) collective-permute-start(bf16[48,2048]{1,0:T(8,128)(2,1)S(1)} %get-tuple-element.14), channel_id=1, source_target_pairs={{0,2},{1,3},{2,0},{3,1},{4,6},{5,7},{6,4},{7,5},{8,10},{9,11},{10,... | collective-permute-start | bytes 589832 | tf_op jit(solution)/shard_map/ppermute | solution.py:224
  29.7 3.1 %collective-permute-start.2 = (bf16[48,2048]{1,0:T(8,128)(2,1)S(1)}, bf16[48,2048]{1,0:T(8,128)(2,1)S(1)}, u32[]{:S(2)}, u32[]{:S(2)}) collective-permute-start(bf16[48,2048]{1,0:T(8,128)(2,1)S(1)} %get-tuple-element.15), channel_id=1, source_target_pairs={{0,3},{1,0},{2,1},{3,2},{4,7},{5,4},{6,5},{7,6},{8,11},{9,8},{10,9... | collective-permute-start | bytes 589832 | tf_op jit(solution)/shard_map/ppermute | solution.py:224
  32.8 3.2 %collective-permute-done.1.refs_2_ = bf16[48,2048]{1,0:T(8,128)(2,1)S(1)} collective-permute-done((bf16[48,2048]{1,0:T(8,128)(2,1)S(1)}, bf16[48,2048]{1,0:T(8,128)(2,1)S(1)}, u32[]{:S(2)}, u32[]{:S(2)}) %collective-permute-start.1) | collective-permute-done | bytes 196640 | tf_op jit(solution)/shard_map/ppermute | solution.py:224
  35.9 1.4 collective-permute-done.2.refs_3_
  37.4 1.5 all-to-all-done
  38.8 4.3 %collective-permute-start.3 = (bf16[1024,256]{1,0:T(8,128)(2,1)S(1)}, bf16[1024,256]{1,0:T(8,128)(2,1)S(1)}, u32[]{:S(2)}, u32[]{:S(2)}) collective-permute-start(bf16[1024,256]{1,0:T(8,128)(2,1)S(1)} %bitcast.13), channel_id=1, source_target_pairs={{0,8},{8,0},{1,9},{9,1},{2,10},{10,2},{3,11},{11,3},{4,12},{12,4},... | collective-permute-start | bytes 1572872 | tf_op jit(solution)/shard_map/ppermute | solution.py:231
  43.4 1.2 collective-permute-done.3.basis_ref
  44.9 9.1 %all_to_all.37.parts_ref = f32[4,48,256]{2,1,0:T(8,128)S(1)} all-to-all(f32[4,48,256]{2,1,0:T(8,128)S(1)} %shard_map.79), channel_id=1, replica_groups=mesh['z'=8,'y_lo'=4,'core'=2,'y_hi'=2,'x'=4] {'x'}, dimensions={0} | all-to-all | bytes 393216 | tf_op jit(solution)/shard_map/all_to_all | solution.py:216
  54.1 14.8 %all_to_all.38 = bf16[8,64,256]{2,1,0:T(8,128)(2,1)S(1)} all-to-all(bf16[8,64,256]{2,1,0:T(8,128)(2,1)S(1)} %shard_map.80), channel_id=1, replica_groups=mesh['z'=8,'y_lo'=4,'core'=2,'y_hi'=2,'x'=4] {'y_hi','x'}, dimensions={0} | all-to-all | bytes 524288 | tf_op jit(solution)/shard_map/all_to_all | solution.py:216
  68.8 1.3 shard_map.83
  70.1 5.1 %collective-permute-start.4 = (bf16[256,1792]{1,0:T(8,128)(2,1)S(1)}, bf16[256,1792]{1,0:T(8,128)(2,1)S(1)}, u32[]{:S(2)}, u32[]{:S(2)}) collective-permute-start(bf16[256,1792]{1,0:T(8,128)(2,1)S(1)} %shard_map.83), channel_id=1, source_target_pairs={{0,8},{8,0},{1,9},{9,1},{2,10},{10,2},{3,11},{11,3},{4,12},{12,4},... | collective-permute-start | bytes 2752520 | tf_op jit(solution)/shard_map/ppermute | solution.py:259
  75.3 1.3 shard_map.82.mine_ref
  76.6 0.8 collective-permute-done.4.theirs_ref
  77.5 31.5 %all_to_all.39 = bf16[32,8,1792]{2,1,0:T(8,128)(2,1)S(1)} all-to-all(bf16[32,8,1792]{2,1,0:T(8,128)(2,1)S(1)} %bitcast.9), channel_id=1, replica_groups=mesh['z'=8,'y_lo'=4,'core'=2,'y_hi'=2,'x'=4] {'y_lo','z'}, dimensions={0} | all-to-all | bytes 1835008 | tf_op jit(solution)/shard_map/all_to_all | solution.py:216
  109.0 0.8 shard_map.85
  109.8 30.3 %all_to_all.40 = bf16[32,8,1792]{2,1,0:T(8,128)(2,1)S(1)} all-to-all(bf16[32,8,1792]{2,1,0:T(8,128)(2,1)S(1)} %bitcast.15), channel_id=1, replica_groups=mesh['z'=8,'y_lo'=4,'core'=2,'y_hi'=2,'x'=4] {'y_lo','z'}, dimensions={0} | all-to-all | bytes 1835008 | tf_op jit(solution)/shard_map/all_to_all | solution.py:216
  140.1 4.7 %collective-permute-start.5 = (bf16[256,1792]{1,0:T(8,128)(2,1)S(1)}, bf16[256,1792]{1,0:T(8,128)(2,1)S(1)}, u32[]{:S(2)}, u32[]{:S(2)}) collective-permute-start(bf16[256,1792]{1,0:T(8,128)(2,1)S(1)} %bitcast.10), channel_id=1, source_target_pairs={{0,8},{8,0},{1,9},{9,1},{2,10},{10,2},{3,11},{11,3},{4,12},{12,4},... | collective-permute-start | bytes 2752520 | tf_op jit(solution)/shard_map/ppermute | solution.py:274
  145.6 1.4 collective-permute-done.5.directions_ref
  147.0 1.3 shard_map.87
  (17 shorter events, 1.5 us)
Async XLA Ops:
  2.2 36.6 %all-to-all-start = ((bf16[64,16,256]{2,1,0:T(8,128)(2,1)}), bf16[64,16,256]{2,1,0:T(8,128)(2,1)S(1)}, u32[]{:S(2)}, u32[]{:S(2)}) async-start(bf16[64,16,256]{2,1,0:T(8,128)(2,1)} %broadcast_in_dim.2), calls=%async_computation | async-start | bytes 1048576 | tf_op jit(solution)/shard_map/all_to_all | solution.py:216
  19.3 1.1 copy-start.4
  22.2 10.6 %collective-permute-start = (bf16[48,2048]{1,0:T(8,128)(2,1)S(1)}, bf16[48,2048]{1,0:T(8,128)(2,1)S(1)}, u32[]{:S(2)}, u32[]{:S(2)}) collective-permute-start(bf16[48,2048]{1,0:T(8,128)(2,1)S(1)} %get-tuple-element.13), channel_id=1, source_target_pairs={{0,1},{1,2},{2,3},{3,0},{4,5},{5,6},{6,7},{7,4},{8,9},{9,10},{10,1... | collective-permute-start | bytes 589832 | tf_op jit(solution)/shard_map/ppermute | solution.py:224
  25.3 10.6 %collective-permute-start.1 = (bf16[48,2048]{1,0:T(8,128)(2,1)S(1)}, bf16[48,2048]{1,0:T(8,128)(2,1)S(1)}, u32[]{:S(2)}, u32[]{:S(2)}) collective-permute-start(bf16[48,2048]{1,0:T(8,128)(2,1)S(1)} %get-tuple-element.14), channel_id=1, source_target_pairs={{0,2},{1,3},{2,0},{3,1},{4,6},{5,7},{6,4},{7,5},{8,10},{9,11},{10,... | collective-permute-start | bytes 589832 | tf_op jit(solution)/shard_map/ppermute | solution.py:224
  29.7 7.6 %collective-permute-start.2 = (bf16[48,2048]{1,0:T(8,128)(2,1)S(1)}, bf16[48,2048]{1,0:T(8,128)(2,1)S(1)}, u32[]{:S(2)}, u32[]{:S(2)}) collective-permute-start(bf16[48,2048]{1,0:T(8,128)(2,1)S(1)} %get-tuple-element.15), channel_id=1, source_target_pairs={{0,3},{1,0},{2,1},{3,2},{4,7},{5,4},{6,5},{7,6},{8,11},{9,8},{10,9... | collective-permute-start | bytes 589832 | tf_op jit(solution)/shard_map/ppermute | solution.py:224
  37.3 16.7 %copy-start.3 = (bf16[16,256]{1,0:T(8,128)(2,1)S(1)}, bf16[16,256]{1,0:T(8,128)(2,1)}, u32[]{:S(2)}) copy-start(bf16[16,256]{1,0:T(8,128)(2,1)} %basis_ref.1) | copy-start | bytes 24580
  38.8 5.8 %collective-permute-start.3 = (bf16[1024,256]{1,0:T(8,128)(2,1)S(1)}, bf16[1024,256]{1,0:T(8,128)(2,1)S(1)}, u32[]{:S(2)}, u32[]{:S(2)}) collective-permute-start(bf16[1024,256]{1,0:T(8,128)(2,1)S(1)} %bitcast.13), channel_id=1, source_target_pairs={{0,8},{8,0},{1,9},{9,1},{2,10},{10,2},{3,11},{11,3},{4,12},{12,4},... | collective-permute-start | bytes 1572872 | tf_op jit(solution)/shard_map/ppermute | solution.py:231
  43.4 25.4 %copy-start = (bf16[384,3584]{1,0:T(8,128)(2,1)S(1)}, bf16[384,3584]{1,0:T(8,128)(2,1)}, u32[]{:S(2)}) copy-start(bf16[384,3584]{1,0:T(8,128)(2,1)} %grad_ref.3) | copy-start | bytes 8257540
  70.1 7.2 %collective-permute-start.4 = (bf16[256,1792]{1,0:T(8,128)(2,1)S(1)}, bf16[256,1792]{1,0:T(8,128)(2,1)S(1)}, u32[]{:S(2)}, u32[]{:S(2)}) collective-permute-start(bf16[256,1792]{1,0:T(8,128)(2,1)S(1)} %shard_map.83), channel_id=1, source_target_pairs={{0,8},{8,0},{1,9},{9,1},{2,10},{10,2},{3,11},{11,3},{4,12},{12,4},... | collective-permute-start | bytes 2752520 | tf_op jit(solution)/shard_map/ppermute | solution.py:259
  77.5 31.5 %copy-start.1 = (f32[4,3584]{1,0:T(4,128)S(1)}, f32[4,3584]{1,0:T(4,128)}, u32[]{:S(2)}) copy-start(f32[4,3584]{1,0:T(4,128)} %first_ref.1) | copy-start | bytes 172036
  77.5 31.5 %copy-start.2 = (f32[4,3584]{1,0:T(4,128)S(1)}, f32[4,3584]{1,0:T(4,128)}, u32[]{:S(2)}) copy-start(f32[4,3584]{1,0:T(4,128)} %second_ref.1) | copy-start | bytes 172036
  140.1 6.8 %collective-permute-start.5 = (bf16[256,1792]{1,0:T(8,128)(2,1)S(1)}, bf16[256,1792]{1,0:T(8,128)(2,1)S(1)}, u32[]{:S(2)}, u32[]{:S(2)}) collective-permute-start(bf16[256,1792]{1,0:T(8,128)(2,1)S(1)} %bitcast.10), channel_id=1, source_target_pairs={{0,8},{8,0},{1,9},{9,1},{2,10},{10,2},{3,11},{11,3},{4,12},{12,4},... | collective-permute-start | bytes 2752520 | tf_op jit(solution)/shard_map/ppermute | solution.py:274

commit v10 on v7

--- a/solution.py
+++ b/solution.py
@@ -16,6 +16,7 @@
 BETA_TWO = 0.95
 EPS = 1e-08
 
+Z_HI, Z_LO = 4, 2
 Z, Y_LO, CORE, Y_HI, X = 8, 4, 2, 2, 4
 OWNERS = Z * Y_LO
 VMEM_LIMIT = 24 * 1024 * 1024
@@ -161,45 +162,49 @@
 
 
 def arrange_basis(gathered_ref, out_ref):
-    core = lax.axis_index("core")
+    core, parity = lax.axis_index("core"), lax.axis_index("z_lo")
     chunk = gathered_ref.shape[0] // 8
     basis = jnp.concatenate(
         [gathered_ref[t * chunk + chunk - 16 : (t + 1) * chunk, :] for t in range(8)], axis=0
     )
     rank = basis.shape[1]
     r, place = iota((rank, rank), 0), iota((rank, rank), 1)
-    for which in range(CORE):
-        side = core if which == 0 else 1 - core
+    side = jnp.where(place < rank // 2, core, 1 - core)
+    owner = (place & (rank // 2 - 1)) >> 3
+    for which in range(Z_LO):
+        z = (owner >> 2) * 2 + (parity if which == 0 else 1 - parity)
+        held = (z * Y_LO + (owner & 3)) * 8 + side * 4 + (place & 3)
         for half in range(2):
-            move = one_hot((r == rank_of(place, side)) & (((place >> 2) & 1) == half))
+            move = one_hot((r == held) & (((place >> 2) & 1) == half))
             out_ref[2 * which + half] = jnp.dot(
                 basis, move, preferred_element_type=F32
             ).astype(BF16)
 
 
-def expand_own(basis_ref, directions_ref, out_ref):
-    width = directions_ref.shape[1]
+def expand_own(basis_ref, own_ref, sibling_ref, out_ref):
+    width = own_ref.shape[1]
     tile = 256
-    for half in range(2):
-        basis = basis_ref[half]
-        for start in range(0, width, tile):
+    for start in range(0, width, tile):
+        columns = slice(start, start + tile)
+        directions = jnp.concatenate([own_ref[:, columns], sibling_ref[:, columns]], axis=0)
+        for half in range(2):
             out_ref[:, half * width + start : half * width + start + tile] = jnp.dot(
-                basis, directions_ref[:, start : start + tile], preferred_element_type=F32
+                basis_ref[half], directions, preferred_element_type=F32
             )
 
 
-def expand(basis_ref, part_ref, directions_ref, out_ref):
-    width = directions_ref.shape[1]
+def expand(basis_ref, part_ref, *refs):
+    *block_refs, out_ref = refs
+    width = block_refs[0].shape[1]
     tile = 256
-    for half in range(2):
-        basis = basis_ref[2 + half]
-        for start in range(0, width, tile):
-            columns = slice(half * width + start, half * width + start + tile)
-            out_ref[:, columns] = (
-                part_ref[:, columns]
-                + jnp.dot(
-                    basis, directions_ref[:, start : start + tile], preferred_element_type=F32
-                )
+    for start in range(0, width, tile):
+        columns = slice(start, start + tile)
+        directions = jnp.concatenate([ref[:, columns] for ref in block_refs], axis=0)
+        for half in range(2):
+            there = slice(half * width + start, half * width + start + tile)
+            out_ref[:, there] = (
+                part_ref[:, there]
+                + jnp.dot(basis_ref[2 + half], directions, preferred_element_type=F32)
             ).astype(BF16)
 
 
@@ -217,7 +222,7 @@
 
     copies = Z * Y_LO * Y_HI
     basis_copies = jnp.broadcast_to(basis[None], (copies, own, rank))
-    class_basis = exchange(basis_copies, ("z", "y_lo", "y_hi")).reshape(copies * own, rank)
+    class_basis = exchange(basis_copies, ("z_hi", "z_lo", "y_lo", "y_hi")).reshape(copies * own, rank)
     block = shape((rows, features // X), BF16)
     blocks = call(split_features, (block,) * X, 2 * rows * features * 512, 0)(tokens)
     held = [blocks[0]] + [
@@ -259,33 +264,43 @@
     theirs = lax.ppermute(projected(False, BF16), "core", swap)
     mine = projected(True, F32)
     pair = call(add_halves, shape((rank, half), BF16), rank * half, 8 * rank * half)(mine, theirs)
-    owned = exchange(pair, ("z", "y_lo"))
+    owned = exchange(pair, ("z_hi", "z_lo", "y_lo"))
     first_out, second_out, direction = call(
         adam,
         (
             shape(first_moment.shape, F32),
             shape(second_moment.shape, F32),
-            shape((rank, half), BF16),
+            shape((rank // Z_LO, half), BF16),
         ),
         rank * half,
         4 * rank * half,
     )(owned, first_moment, second_moment)
-    directions = exchange(direction, ("z", "y_lo"))
-    others = lax.ppermute(directions, "core", swap)
+    same = exchange(direction, ("z_hi", "y_lo"))
+    middle = same.shape[0] // 2
+
+    def along_z(array, step):
+        return lax.ppermute(array, ("z_hi", "z_lo"), [(z, (z + step) % Z) for z in range(Z)])
+
+    upper, lower = along_z(same[:middle], 1), along_z(same[middle:], -1)
+    sibling_same = lax.ppermute(same, "core", swap)
+    sibling_upper = lax.ppermute(upper, "core", swap)
+    sibling_lower = lax.ppermute(lower, "core", swap)
     update_rows = own * takers
     bases = call(
         arrange_basis, shape((4, update_rows, rank), BF16), 8 * update_rows * rank * rank, 0
     )(gathered)
     cost = (4 * update_rows * rank * half, 4 * update_rows * columns)
-    part = call(expand_own, shape((update_rows, columns), F32), *cost)(bases, directions)
-    update = call(expand, shape((update_rows, columns), BF16), *cost)(bases, part, others)
+    part = call(expand_own, shape((update_rows, columns), F32), *cost)(bases, same, sibling_same)
+    update = call(expand, shape((update_rows, columns), BF16), *cost)(
+        bases, part, upper, lower, sibling_upper, sibling_lower
+    )
     return (update, first_out, second_out)
 
 
 def solution(mesh):
-    names = ("z", "y_lo", "core", "y_hi", "x")
-    fine = Mesh(mesh.devices.reshape(Z, Y_LO, CORE, Y_HI, X), names)
-    data, tensor = names[:3], names[3:]
+    names = ("z_hi", "z_lo", "y_lo", "core", "y_hi", "x")
+    fine = Mesh(mesh.devices.reshape(Z_HI, Z_LO, Y_LO, CORE, Y_HI, X), names)
+    data, tensor = names[:4], names[4:]
     placed = (P(names, None), P(data, tensor), P(names, None), P(data, tensor), P(data, tensor))
     return jax.shard_map(
         per_device,

time: 149 us -> 155 us (1.040)
  starting transfers between devices: 42.3 us -> 51.6 us
  blocking collectives: 85.1 us -> 77.6 us
  waiting for transfers between devices: 9.38 us -> 13.4 us
    ppermute x1 -> x5, starting transfers between devices: 5.13 us -> 14.5 us  [the longest x2 5.28 us: along_z(): lax.ppermute(array, ('z_hi', 'z_lo'), [(z, (z + step) % Z) for z in range...]
    all_to_all x4, blocking collectives: 85.1 us -> 77.6 us  [exchange(): return lax.all_to_all(array, axes, 0, 0, tiled=True)]
    ppermute x1 -> x5, waiting for transfers between devices: 1.39 us -> 5.43 us  [the longest x2 5.03 us: along_z(): lax.ppermute(array, ('z_hi', 'z_lo'), [(z, (z + step) % Z) for z in range...]
  transfers between devices with their start and end apart: 7 -> 11, of which waited for: 6 -> 8; matrix products, arithmetic and copies ran while one was open for 0% -> 0% of each run, Pallas kernels for 3% -> 3%
where the time goes in v10:
time: 155 us; the launch traced here: 154 us
  blocking collectives  77.6 us (50%)
  starting transfers between devices  51.6 us (33%)
  waiting for transfers between devices  13.4 us (9%)
  Pallas kernels  7.88 us (5%)
  local copies, waits for them, and re-layouts  2.71 us (2%)
    all_to_all x4, blocking collectives, exchange(): return lax.all_to_all(array, axes, 0, 0, tiled=True)  77.6 us
    all_to_all x1, starting transfers between devices, exchange(): return lax.all_to_all(array, axes, 0, 0, tiled=True)  17.1 us
    ppermute x3, starting transfers between devices, per_device(): lax.ppermute(blocks[step], 'x', [(x, (x + step) % X) for x in range(X)])  10.5 us
    ppermute x2, starting transfers between devices, along_z(): lax.ppermute(array, ('z_hi', 'z_lo'), [(z, (z + step) % Z) for z in range...  5.28 us
    ppermute x1, starting transfers between devices, per_device(): theirs = lax.ppermute(projected(False, BF16), 'core', swap)  5.12 us
    ppermute x2, waiting for transfers between devices, along_z(): lax.ppermute(array, ('z_hi', 'z_lo'), [(z, (z + step) % Z) for z in range...  5.03 us
    ppermute x3, waiting for transfers between devices, per_device(): lax.ppermute(blocks[step], 'x', [(x, (x + step) % X) for x in range(X)])  4.53 us
    ppermute x1, starting transfers between devices, per_device(): sibling_basis = lax.ppermute(class_basis, 'core', swap)  4.32 us
  transfers between devices with their start and end apart: 11, of which 8 were waited for; matrix products, arithmetic and copies ran while one was open for 0% of the time, Pallas kernels for 3%

profile of v10, /device:TPU:1, one launch (start us, length us, event | category | flops | bytes accessed | tf_op | source)
XLA Modules:
  0.0 154.1 jit_solution(9123156482643664464)
XLA Ops:
  0.6 1.5 broadcast_in_dim.2
  2.2 17.1 %all-to-all-start = ((bf16[64,16,256]{2,1,0:T(8,128)(2,1)}), bf16[64,16,256]{2,1,0:T(8,128)(2,1)S(1)}, u32[]{:S(2)}, u32[]{:S(2)}) async-start(bf16[64,16,256]{2,1,0:T(8,128)(2,1)} %broadcast_in_dim.2), calls=%async_computation | async-start | bytes 1048576 | tf_op jit(solution)/shard_map/all_to_all | solution.py:221
  20.4 1.7 %shard_map.76 = (bf16[48,2048]{1,0:T(8,128)(2,1)S(1)}, bf16[48,2048]{1,0:T(8,128)(2,1)S(1)}, bf16[48,2048]{1,0:T(8,128)(2,1)S(1)}, bf16[48,2048]{1,0:T(8,128)(2,1)S(1)}) custom-call(bf16[48,8192]{1,0:T(8,128)(2,1)S(1)} %copy-done.4), custom_call_target="tpu_custom_call" | custom-call | flops 402653184 | tf_op jit(solution)/shard_map/pallas_call | solution.py:227
  22.2 3.1 %collective-permute-start = (bf16[48,2048]{1,0:T(8,128)(2,1)S(1)}, bf16[48,2048]{1,0:T(8,128)(2,1)S(1)}, u32[]{:S(2)}, u32[]{:S(2)}) collective-permute-start(bf16[48,2048]{1,0:T(8,128)(2,1)S(1)} %get-tuple-element.13), channel_id=1, source_target_pairs={{0,1},{1,2},{2,3},{3,0},{4,5},{5,6},{6,7},{7,4},{8,9},{9,10},{10,1... | collective-permute-start | bytes 589832 | tf_op jit(solution)/shard_map/ppermute | solution.py:229
  25.3 4.4 %collective-permute-start.1 = (bf16[48,2048]{1,0:T(8,128)(2,1)S(1)}, bf16[48,2048]{1,0:T(8,128)(2,1)S(1)}, u32[]{:S(2)}, u32[]{:S(2)}) collective-permute-start(bf16[48,2048]{1,0:T(8,128)(2,1)S(1)} %get-tuple-element.14), channel_id=1, source_target_pairs={{0,2},{1,3},{2,0},{3,1},{4,6},{5,7},{6,4},{7,5},{8,10},{9,11},{10,... | collective-permute-start | bytes 589832 | tf_op jit(solution)/shard_map/ppermute | solution.py:229
  29.7 3.1 %collective-permute-start.2 = (bf16[48,2048]{1,0:T(8,128)(2,1)S(1)}, bf16[48,2048]{1,0:T(8,128)(2,1)S(1)}, u32[]{:S(2)}, u32[]{:S(2)}) collective-permute-start(bf16[48,2048]{1,0:T(8,128)(2,1)S(1)} %get-tuple-element.15), channel_id=1, source_target_pairs={{0,3},{1,0},{2,1},{3,2},{4,7},{5,4},{6,5},{7,6},{8,11},{9,8},{10,9... | collective-permute-start | bytes 589832 | tf_op jit(solution)/shard_map/ppermute | solution.py:229
  32.8 3.2 %collective-permute-done.1.refs_2_ = bf16[48,2048]{1,0:T(8,128)(2,1)S(1)} collective-permute-done((bf16[48,2048]{1,0:T(8,128)(2,1)S(1)}, bf16[48,2048]{1,0:T(8,128)(2,1)S(1)}, u32[]{:S(2)}, u32[]{:S(2)}) %collective-permute-start.1) | collective-permute-done | bytes 196640 | tf_op jit(solution)/shard_map/ppermute | solution.py:229
  35.9 1.4 collective-permute-done.2.refs_3_
  37.4 1.5 all-to-all-done
  38.8 4.3 %collective-permute-start.3 = (bf16[1024,256]{1,0:T(8,128)(2,1)S(1)}, bf16[1024,256]{1,0:T(8,128)(2,1)S(1)}, u32[]{:S(2)}, u32[]{:S(2)}) collective-permute-start(bf16[1024,256]{1,0:T(8,128)(2,1)S(1)} %bitcast.17), channel_id=1, source_target_pairs={{0,8},{8,0},{1,9},{9,1},{2,10},{10,2},{3,11},{11,3},{4,12},{12,4},... | collective-permute-start | bytes 1572872 | tf_op jit(solution)/shard_map/ppermute | solution.py:236
  44.9 9.1 %all_to_all.37.parts_ref = f32[4,48,256]{2,1,0:T(8,128)S(1)} all-to-all(f32[4,48,256]{2,1,0:T(8,128)S(1)} %shard_map.79), channel_id=1, replica_groups=mesh['z_hi'=4,'z_lo'=2,'y_lo'=4,'core'=2,'y_hi'=2,'x'=4] {'x'}, dimensions={0} | all-to-all | bytes 393216 | tf_op jit(solution)/shard_map/all_to_all | solution.py:221
  54.1 14.8 %all_to_all.38 = bf16[8,64,256]{2,1,0:T(8,128)(2,1)S(1)} all-to-all(bf16[8,64,256]{2,1,0:T(8,128)(2,1)S(1)} %shard_map.80), channel_id=1, replica_groups=mesh['z_hi'=4,'z_lo'=2,'y_lo'=4,'core'=2,'y_hi'=2,'x'=4] {'y_hi','x'}, dimensions={0} | all-to-all | bytes 524288 | tf_op jit(solution)/shard_map/all_to_all | solution.py:221
  68.8 1.3 shard_map.83
  70.1 5.1 %collective-permute-start.4 = (bf16[256,1792]{1,0:T(8,128)(2,1)S(1)}, bf16[256,1792]{1,0:T(8,128)(2,1)S(1)}, u32[]{:S(2)}, u32[]{:S(2)}) collective-permute-start(bf16[256,1792]{1,0:T(8,128)(2,1)S(1)} %shard_map.83), channel_id=1, source_target_pairs={{0,8},{8,0},{1,9},{9,1},{2,10},{10,2},{3,11},{11,3},{4,12},{12,4},... | collective-permute-start | bytes 2752520 | tf_op jit(solution)/shard_map/ppermute | solution.py:264
  75.3 1.3 shard_map.82.mine_ref
  77.5 31.5 %all_to_all.39 = bf16[32,8,1792]{2,1,0:T(8,128)(2,1)S(1)} all-to-all(bf16[32,8,1792]{2,1,0:T(8,128)(2,1)S(1)} %bitcast.15), channel_id=1, replica_groups=mesh['z_hi'=4,'z_lo'=2,'y_lo'=4,'core'=2,'y_hi'=2,'x'=4] {'z_hi','z_lo',..., dimensions={0} | all-to-all | bytes 1835008 | tf_op jit(solution)/shard_map/all_to_all | solution.py:221
  109.8 22.3 %all_to_all.40 = bf16[16,8,1792]{2,1,0:T(8,128)(2,1)S(1)} all-to-all(bf16[16,8,1792]{2,1,0:T(8,128)(2,1)S(1)} %bitcast.19), channel_id=1, replica_groups=mesh['z_hi'=4,'z_lo'=2,'y_lo'=4,'core'=2,'y_hi'=2,'x'=4] {'z_hi','y_lo'}, dimensions={0} | all-to-all | bytes 917504 | tf_op jit(solution)/shard_map/all_to_all | solution.py:221
  132.0 3.5 %collective-permute-start.5 = (bf16[128,1792]{1,0:T(8,128)(2,1)S(1)}, bf16[128,1792]{1,0:T(8,128)(2,1)S(1)}, u32[]{:S(2)}, u32[]{:S(2)}) collective-permute-start(bf16[128,1792]{1,0:T(8,128)(2,1)S(1)} %bitcast.13), channel_id=1, source_target_pairs={{0,8},{8,0},{1,9},{9,1},{2,10},{10,2},{3,11},{11,3},{4,12},{12,4},... | collective-permute-start | bytes 1376264 | tf_op jit(solution)/shard_map/ppermute | solution.py:285
  135.6 3.0 %collective-permute-start.7 = (bf16[64,1792]{1,0:T(8,128)(2,1)S(1)}, bf16[64,1792]{1,0:T(8,128)(2,1)S(1)}, u32[]{:S(2)}, u32[]{:S(2)}) collective-permute-start(bf16[64,1792]{1,0:T(8,128)(2,1)S(1)} %get-tuple-element.21), channel_id=1, source_target_pairs={{0,448},{64,0},{128,64},{192,128},{256,192},{320,256},{384,320},{4... | collective-permute-start | bytes 688136 | tf_op jit(solution)/shard_map/ppermute | solution.py:282
  138.6 2.3 %collective-permute-start.6 = (bf16[64,1792]{1,0:T(8,128)(2,1)S(1)}, bf16[64,1792]{1,0:T(8,128)(2,1)S(1)}, u32[]{:S(2)}, u32[]{:S(2)}) collective-permute-start(bf16[64,1792]{1,0:T(8,128)(2,1)S(1)} %get-tuple-element.22), channel_id=1, source_target_pairs={{0,64},{64,128},{128,192},{192,256},{256,320},{320,384},{384,448},... | collective-permute-start | bytes 688136 | tf_op jit(solution)/shard_map/ppermute | solution.py:282
  140.9 3.8 %collective-permute-done.7.refs_1_ = bf16[64,1792]{1,0:T(8,128)(2,1)S(1)} collective-permute-done((bf16[64,1792]{1,0:T(8,128)(2,1)S(1)}, bf16[64,1792]{1,0:T(8,128)(2,1)S(1)}, u32[]{:S(2)}, u32[]{:S(2)}) %collective-permute-start.7) | collective-permute-done | bytes 229408 | tf_op jit(solution)/shard_map/ppermute | solution.py:282
  144.7 2.7 %collective-permute-start.9 = (bf16[64,1792]{1,0:T(8,128)(2,1)S(1)}, bf16[64,1792]{1,0:T(8,128)(2,1)S(1)}, u32[]{:S(2)}, u32[]{:S(2)}) collective-permute-start(bf16[64,1792]{1,0:T(8,128)(2,1)S(1)} %collective-permute-done.7.refs_1_), channel_id=1, source_target_pairs={{0,8},{8,0},{1,9},{9,1},{2,10},{10,2},{3,11},{11,3},{4,12},{12,4},... | collective-permute-start | bytes 688136 | tf_op jit(solution)/shard_map/ppermute | solution.py:287
  148.6 3.0 %collective-permute-start.8 = (bf16[64,1792]{1,0:T(8,128)(2,1)S(1)}, bf16[64,1792]{1,0:T(8,128)(2,1)S(1)}, u32[]{:S(2)}, u32[]{:S(2)}) collective-permute-start(bf16[64,1792]{1,0:T(8,128)(2,1)S(1)} %collective-permute-done.6.refs_0_), channel_id=1, source_target_pairs={{0,8},{8,0},{1,9},{9,1},{2,10},{10,2},{3,11},{11,3},{4,12},{12,4},... | collective-permute-start | bytes 688136 | tf_op jit(solution)/shard_map/ppermute | solution.py:286
  152.7 1.3 shard_map.87
  (26 shorter events, 7.0 us)
Async XLA Ops:
  2.2 36.6 %all-to-all-start = ((bf16[64,16,256]{2,1,0:T(8,128)(2,1)}), bf16[64,16,256]{2,1,0:T(8,128)(2,1)S(1)}, u32[]{:S(2)}, u32[]{:S(2)}) async-start(bf16[64,16,256]{2,1,0:T(8,128)(2,1)} %broadcast_in_dim.2), calls=%async_computation | async-start | bytes 1048576 | tf_op jit(solution)/shard_map/all_to_all | solution.py:221
  19.3 1.1 copy-start.4
  22.2 10.6 %collective-permute-start = (bf16[48,2048]{1,0:T(8,128)(2,1)S(1)}, bf16[48,2048]{1,0:T(8,128)(2,1)S(1)}, u32[]{:S(2)}, u32[]{:S(2)}) collective-permute-start(bf16[48,2048]{1,0:T(8,128)(2,1)S(1)} %get-tuple-element.13), channel_id=1, source_target_pairs={{0,1},{1,2},{2,3},{3,0},{4,5},{5,6},{6,7},{7,4},{8,9},{9,10},{10,1... | collective-permute-start | bytes 589832 | tf_op jit(solution)/shard_map/ppermute | solution.py:229
  25.3 10.6 %collective-permute-start.1 = (bf16[48,2048]{1,0:T(8,128)(2,1)S(1)}, bf16[48,2048]{1,0:T(8,128)(2,1)S(1)}, u32[]{:S(2)}, u32[]{:S(2)}) collective-permute-start(bf16[48,2048]{1,0:T(8,128)(2,1)S(1)} %get-tuple-element.14), channel_id=1, source_target_pairs={{0,2},{1,3},{2,0},{3,1},{4,6},{5,7},{6,4},{7,5},{8,10},{9,11},{10,... | collective-permute-start | bytes 589832 | tf_op jit(solution)/shard_map/ppermute | solution.py:229
  29.7 7.6 %collective-permute-start.2 = (bf16[48,2048]{1,0:T(8,128)(2,1)S(1)}, bf16[48,2048]{1,0:T(8,128)(2,1)S(1)}, u32[]{:S(2)}, u32[]{:S(2)}) collective-permute-start(bf16[48,2048]{1,0:T(8,128)(2,1)S(1)} %get-tuple-element.15), channel_id=1, source_target_pairs={{0,3},{1,0},{2,1},{3,2},{4,7},{5,4},{6,5},{7,6},{8,11},{9,8},{10,9... | collective-permute-start | bytes 589832 | tf_op jit(solution)/shard_map/ppermute | solution.py:229
  37.3 16.7 %copy-start.3 = (bf16[16,256]{1,0:T(8,128)(2,1)S(1)}, bf16[16,256]{1,0:T(8,128)(2,1)}, u32[]{:S(2)}) copy-start(bf16[16,256]{1,0:T(8,128)(2,1)} %basis_ref.1) | copy-start | bytes 24580
  38.8 5.8 %collective-permute-start.3 = (bf16[1024,256]{1,0:T(8,128)(2,1)S(1)}, bf16[1024,256]{1,0:T(8,128)(2,1)S(1)}, u32[]{:S(2)}, u32[]{:S(2)}) collective-permute-start(bf16[1024,256]{1,0:T(8,128)(2,1)S(1)} %bitcast.17), channel_id=1, source_target_pairs={{0,8},{8,0},{1,9},{9,1},{2,10},{10,2},{3,11},{11,3},{4,12},{12,4},... | collective-permute-start | bytes 1572872 | tf_op jit(solution)/shard_map/ppermute | solution.py:236
  43.4 25.4 %copy-start = (bf16[384,3584]{1,0:T(8,128)(2,1)S(1)}, bf16[384,3584]{1,0:T(8,128)(2,1)}, u32[]{:S(2)}) copy-start(bf16[384,3584]{1,0:T(8,128)(2,1)} %grad_ref.3) | copy-start | bytes 8257540
  70.1 7.2 %collective-permute-start.4 = (bf16[256,1792]{1,0:T(8,128)(2,1)S(1)}, bf16[256,1792]{1,0:T(8,128)(2,1)S(1)}, u32[]{:S(2)}, u32[]{:S(2)}) collective-permute-start(bf16[256,1792]{1,0:T(8,128)(2,1)S(1)} %shard_map.83), channel_id=1, source_target_pairs={{0,8},{8,0},{1,9},{9,1},{2,10},{10,2},{3,11},{11,3},{4,12},{12,4},... | collective-permute-start | bytes 2752520 | tf_op jit(solution)/shard_map/ppermute | solution.py:264
  77.5 31.5 %copy-start.1 = (f32[4,3584]{1,0:T(4,128)S(1)}, f32[4,3584]{1,0:T(4,128)}, u32[]{:S(2)}) copy-start(f32[4,3584]{1,0:T(4,128)} %first_ref.1) | copy-start | bytes 172036
  77.5 31.5 %copy-start.2 = (f32[4,3584]{1,0:T(4,128)S(1)}, f32[4,3584]{1,0:T(4,128)}, u32[]{:S(2)}) copy-start(f32[4,3584]{1,0:T(4,128)} %second_ref.1) | copy-start | bytes 172036
  132.0 19.9 %collective-permute-start.5 = (bf16[128,1792]{1,0:T(8,128)(2,1)S(1)}, bf16[128,1792]{1,0:T(8,128)(2,1)S(1)}, u32[]{:S(2)}, u32[]{:S(2)}) collective-permute-start(bf16[128,1792]{1,0:T(8,128)(2,1)S(1)} %bitcast.13), channel_id=1, source_target_pairs={{0,8},{8,0},{1,9},{9,1},{2,10},{10,2},{3,11},{11,3},{4,12},{12,4},... | collective-permute-start | bytes 1376264 | tf_op jit(solution)/shard_map/ppermute | solution.py:285
  135.6 9.1 %collective-permute-start.7 = (bf16[64,1792]{1,0:T(8,128)(2,1)S(1)}, bf16[64,1792]{1,0:T(8,128)(2,1)S(1)}, u32[]{:S(2)}, u32[]{:S(2)}) collective-permute-start(bf16[64,1792]{1,0:T(8,128)(2,1)S(1)} %get-tuple-element.21), channel_id=1, source_target_pairs={{0,448},{64,0},{128,64},{192,128},{256,192},{320,256},{384,320},{4... | collective-permute-start | bytes 688136 | tf_op jit(solution)/shard_map/ppermute | solution.py:282
  138.6 10.0 %collective-permute-start.6 = (bf16[64,1792]{1,0:T(8,128)(2,1)S(1)}, bf16[64,1792]{1,0:T(8,128)(2,1)S(1)}, u32[]{:S(2)}, u32[]{:S(2)}) collective-permute-start(bf16[64,1792]{1,0:T(8,128)(2,1)S(1)} %get-tuple-element.22), channel_id=1, source_target_pairs={{0,64},{64,128},{128,192},{192,256},{256,320},{320,384},{384,448},... | collective-permute-start | bytes 688136 | tf_op jit(solution)/shard_map/ppermute | solution.py:282
  144.7 7.6 %collective-permute-start.9 = (bf16[64,1792]{1,0:T(8,128)(2,1)S(1)}, bf16[64,1792]{1,0:T(8,128)(2,1)S(1)}, u32[]{:S(2)}, u32[]{:S(2)}) collective-permute-start(bf16[64,1792]{1,0:T(8,128)(2,1)S(1)} %collective-permute-done.7.refs_1_), channel_id=1, source_target_pairs={{0,8},{8,0},{1,9},{9,1},{2,10},{10,2},{3,11},{11,3},{4,12},{12,4},... | collective-permute-start | bytes 688136 | tf_op jit(solution)/shard_map/ppermute | solution.py:287
  148.6 4.1 %collective-permute-start.8 = (bf16[64,1792]{1,0:T(8,128)(2,1)S(1)}, bf16[64,1792]{1,0:T(8,128)(2,1)S(1)}, u32[]{:S(2)}, u32[]{:S(2)}) collective-permute-start(bf16[64,1792]{1,0:T(8,128)(2,1)S(1)} %collective-permute-done.6.refs_0_), channel_id=1, source_target_pairs={{0,8},{8,0},{1,9},{9,1},{2,10},{10,2},{3,11},{11,3},{4,12},{12,4},... | collective-permute-start | bytes 688136 | tf_op jit(solution)/shard_map/ppermute | solution.py:286

commit v11 on v7

--- a/solution.py
+++ b/solution.py
@@ -16,6 +16,7 @@
 BETA_TWO = 0.95
 EPS = 1e-08
 
+Z_HI, Z_LO = 4, 2
 Z, Y_LO, CORE, Y_HI, X = 8, 4, 2, 2, 4
 OWNERS = Z * Y_LO
 VMEM_LIMIT = 24 * 1024 * 1024
@@ -62,9 +63,11 @@
 
 def stack(*refs):
     *block_refs, out_ref = refs
-    rows = block_refs[0].shape[0]
-    for step, ref in enumerate(block_refs):
-        out_ref[step * rows : (step + 1) * rows, :] = ref[...]
+    start = 0
+    for ref in block_refs:
+        rows = ref.shape[0]
+        out_ref[start : start + rows, :] = ref[...]
+        start += rows
 
 
 def class_part(tokens_ref, basis_ref, side):
@@ -161,17 +164,20 @@
 
 
 def arrange_basis(gathered_ref, out_ref):
-    core = lax.axis_index("core")
+    core, parity = lax.axis_index("core"), lax.axis_index("z_lo")
     chunk = gathered_ref.shape[0] // 8
     basis = jnp.concatenate(
         [gathered_ref[t * chunk + chunk - 16 : (t + 1) * chunk, :] for t in range(8)], axis=0
     )
     rank = basis.shape[1]
     r, place = iota((rank, rank), 0), iota((rank, rank), 1)
+    owner = (place & (rank // 2 - 1)) >> 3
+    z = (owner >> 2) * 2 + jnp.where(place < rank // 2, parity, 1 - parity)
     for which in range(CORE):
         side = core if which == 0 else 1 - core
+        held = (z * Y_LO + (owner & 3)) * 8 + side * 4 + (place & 3)
         for half in range(2):
-            move = one_hot((r == rank_of(place, side)) & (((place >> 2) & 1) == half))
+            move = one_hot((r == held) & (((place >> 2) & 1) == half))
             out_ref[2 * which + half] = jnp.dot(
                 basis, move, preferred_element_type=F32
             ).astype(BF16)
@@ -217,7 +223,7 @@
 
     copies = Z * Y_LO * Y_HI
     basis_copies = jnp.broadcast_to(basis[None], (copies, own, rank))
-    class_basis = exchange(basis_copies, ("z", "y_lo", "y_hi")).reshape(copies * own, rank)
+    class_basis = exchange(basis_copies, ("z_hi", "z_lo", "y_lo", "y_hi")).reshape(copies * own, rank)
     block = shape((rows, features // X), BF16)
     blocks = call(split_features, (block,) * X, 2 * rows * features * 512, 0)(tokens)
     held = [blocks[0]] + [
@@ -259,18 +265,25 @@
     theirs = lax.ppermute(projected(False, BF16), "core", swap)
     mine = projected(True, F32)
     pair = call(add_halves, shape((rank, half), BF16), rank * half, 8 * rank * half)(mine, theirs)
-    owned = exchange(pair, ("z", "y_lo"))
+    owned = exchange(pair, ("z_hi", "z_lo", "y_lo"))
     first_out, second_out, direction = call(
         adam,
         (
             shape(first_moment.shape, F32),
             shape(second_moment.shape, F32),
-            shape((rank, half), BF16),
+            shape((rank // Z_LO, half), BF16),
         ),
         rank * half,
         4 * rank * half,
     )(owned, first_moment, second_moment)
-    directions = exchange(direction, ("z", "y_lo"))
+    same = exchange(direction, ("z_hi", "y_lo"))
+    middle = same.shape[0] // 2
+
+    def along_z(array, step):
+        return lax.ppermute(array, ("z_hi", "z_lo"), [(z, (z + step) % Z) for z in range(Z)])
+
+    upper, lower = along_z(same[:middle], 1), along_z(same[middle:], -1)
+    directions = call(stack, shape((rank, half), BF16), 0, 4 * rank * half)(same, upper, lower)
     others = lax.ppermute(directions, "core", swap)
     update_rows = own * takers
     bases = call(
@@ -283,9 +296,9 @@
 
 
 def solution(mesh):
-    names = ("z", "y_lo", "core", "y_hi", "x")
-    fine = Mesh(mesh.devices.reshape(Z, Y_LO, CORE, Y_HI, X), names)
-    data, tensor = names[:3], names[3:]
+    names = ("z_hi", "z_lo", "y_lo", "core", "y_hi", "x")
+    fine = Mesh(mesh.devices.reshape(Z_HI, Z_LO, Y_LO, CORE, Y_HI, X), names)
+    data, tensor = names[:4], names[4:]
     placed = (P(names, None), P(data, tensor), P(names, None), P(data, tensor), P(data, tensor))
     return jax.shard_map(
         per_device,

time: 149 us -> 152 us (1.020)
  blocking collectives: 85.1 us -> 77.6 us
  waiting for transfers between devices: 9.38 us -> 14.8 us
  starting transfers between devices: 42.3 us -> 47.6 us
    all_to_all x4, blocking collectives: 85.1 us -> 77.6 us  [exchange(): return lax.all_to_all(array, axes, 0, 0, tiled=True)]
    ppermute x0 -> x2, waiting for transfers between devices: none -> 5.42 us  [along_z(): lax.ppermute(array, ('z_hi', 'z_lo'), [(z, (z + step) % Z) for z in range...]
    ppermute x0 -> x2, starting transfers between devices: none -> 5.28 us  [along_z(): lax.ppermute(array, ('z_hi', 'z_lo'), [(z, (z + step) % Z) for z in range...]
  transfers between devices with their start and end apart: 7 -> 9, of which waited for: 6 -> 8; matrix products, arithmetic and copies ran while one was open for 0% -> 0% of each run, Pallas kernels for 3% -> 3%
where the time goes in v11:
time: 152 us
  blocking collectives  77.6 us (51%)
  starting transfers between devices  47.6 us (31%)
  waiting for transfers between devices  14.8 us (10%)
  Pallas kernels  7.94 us (5%)
  local copies, waits for them, and re-layouts  2.71 us (2%)
    all_to_all x4, blocking collectives, exchange(): return lax.all_to_all(array, axes, 0, 0, tiled=True)  77.6 us
    all_to_all x1, starting transfers between devices, exchange(): return lax.all_to_all(array, axes, 0, 0, tiled=True)  17.1 us
    ppermute x3, starting transfers between devices, per_device(): lax.ppermute(blocks[step], 'x', [(x, (x + step) % X) for x in range(X)])  10.5 us
    ppermute x2, waiting for transfers between devices, along_z(): lax.ppermute(array, ('z_hi', 'z_lo'), [(z, (z + step) % Z) for z in range...  5.42 us
    ppermute x2, starting transfers between devices, along_z(): lax.ppermute(array, ('z_hi', 'z_lo'), [(z, (z + step) % Z) for z in range...  5.28 us
    ppermute x1, starting transfers between devices, per_device(): others = lax.ppermute(directions, 'core', swap)  5.24 us
    ppermute x1, starting transfers between devices, per_device(): theirs = lax.ppermute(projected(False, BF16), 'core', swap)  5.12 us
    ppermute x3, waiting for transfers between devices, per_device(): lax.ppermute(blocks[step], 'x', [(x, (x + step) % X) for x in range(X)])  4.53 us
  transfers between devices with their start and end apart: 9, of which 8 were waited for; matrix products, arithmetic and copies ran while one was open for 0% of the time, Pallas kernels for 3%

profile of v11, /device:TPU:1, one launch (start us, length us, event | category | flops | bytes accessed | tf_op | source)
XLA Modules:
  0.0 151.5 jit_solution(6704547031090923122)
XLA Ops:
  0.6 1.5 %broadcast_in_dim.2 = bf16[64,16,256]{2,1,0:T(8,128)(2,1)} broadcast(bf16[16,256]{1,0:T(8,128)(2,1)} %basis_ref.1), dimensions={1,2} | broadcast | bytes 532480 | tf_op jit(solution)/shard_map/broadcast_in_dim | solution.py:225
  2.2 17.1 %all-to-all-start = ((bf16[64,16,256]{2,1,0:T(8,128)(2,1)}), bf16[64,16,256]{2,1,0:T(8,128)(2,1)S(1)}, u32[]{:S(2)}, u32[]{:S(2)}) async-start(bf16[64,16,256]{2,1,0:T(8,128)(2,1)} %broadcast_in_dim.2), calls=%async_computation | async-start | bytes 1048576 | tf_op jit(solution)/shard_map/all_to_all | solution.py:222
  20.4 1.7 %shard_map.76 = (bf16[48,2048]{1,0:T(8,128)(2,1)S(1)}, bf16[48,2048]{1,0:T(8,128)(2,1)S(1)}, bf16[48,2048]{1,0:T(8,128)(2,1)S(1)}, bf16[48,2048]{1,0:T(8,128)(2,1)S(1)}) custom-call(bf16[48,8192]{1,0:T(8,128)(2,1)S(1)} %copy-done.4), custom_call_target="tpu_custom_call" | custom-call | flops 402653184 | tf_op jit(solution)/shard_map/pallas_call | solution.py:228
  22.2 3.1 %collective-permute-start = (bf16[48,2048]{1,0:T(8,128)(2,1)S(1)}, bf16[48,2048]{1,0:T(8,128)(2,1)S(1)}, u32[]{:S(2)}, u32[]{:S(2)}) collective-permute-start(bf16[48,2048]{1,0:T(8,128)(2,1)S(1)} %get-tuple-element.13), channel_id=1, source_target_pairs={{0,1},{1,2},{2,3},{3,0},{4,5},{5,6},{6,7},{7,4},{8,9},{9,10},{10,1... | collective-permute-start | bytes 589832 | tf_op jit(solution)/shard_map/ppermute | solution.py:230
  25.3 4.4 %collective-permute-start.1 = (bf16[48,2048]{1,0:T(8,128)(2,1)S(1)}, bf16[48,2048]{1,0:T(8,128)(2,1)S(1)}, u32[]{:S(2)}, u32[]{:S(2)}) collective-permute-start(bf16[48,2048]{1,0:T(8,128)(2,1)S(1)} %get-tuple-element.14), channel_id=1, source_target_pairs={{0,2},{1,3},{2,0},{3,1},{4,6},{5,7},{6,4},{7,5},{8,10},{9,11},{10,... | collective-permute-start | bytes 589832 | tf_op jit(solution)/shard_map/ppermute | solution.py:230
  29.7 3.1 %collective-permute-start.2 = (bf16[48,2048]{1,0:T(8,128)(2,1)S(1)}, bf16[48,2048]{1,0:T(8,128)(2,1)S(1)}, u32[]{:S(2)}, u32[]{:S(2)}) collective-permute-start(bf16[48,2048]{1,0:T(8,128)(2,1)S(1)} %get-tuple-element.15), channel_id=1, source_target_pairs={{0,3},{1,0},{2,1},{3,2},{4,7},{5,4},{6,5},{7,6},{8,11},{9,8},{10,9... | collective-permute-start | bytes 589832 | tf_op jit(solution)/shard_map/ppermute | solution.py:230
  32.8 3.2 %collective-permute-done.1.refs_2_ = bf16[48,2048]{1,0:T(8,128)(2,1)S(1)} collective-permute-done((bf16[48,2048]{1,0:T(8,128)(2,1)S(1)}, bf16[48,2048]{1,0:T(8,128)(2,1)S(1)}, u32[]{:S(2)}, u32[]{:S(2)}) %collective-permute-start.1) | collective-permute-done | bytes 196640 | tf_op jit(solution)/shard_map/ppermute | solution.py:230
  35.9 1.4 collective-permute-done.2.refs_3_
  37.4 1.5 all-to-all-done
  38.8 4.3 %collective-permute-start.3 = (bf16[1024,256]{1,0:T(8,128)(2,1)S(1)}, bf16[1024,256]{1,0:T(8,128)(2,1)S(1)}, u32[]{:S(2)}, u32[]{:S(2)}) collective-permute-start(bf16[1024,256]{1,0:T(8,128)(2,1)S(1)} %bitcast.16), channel_id=1, source_target_pairs={{0,8},{8,0},{1,9},{9,1},{2,10},{10,2},{3,11},{11,3},{4,12},{12,4},... | collective-permute-start | bytes 1572872 | tf_op jit(solution)/shard_map/ppermute | solution.py:237
  44.9 9.1 %all_to_all.37.parts_ref = f32[4,48,256]{2,1,0:T(8,128)S(1)} all-to-all(f32[4,48,256]{2,1,0:T(8,128)S(1)} %shard_map.79), channel_id=1, replica_groups=mesh['z_hi'=4,'z_lo'=2,'y_lo'=4,'core'=2,'y_hi'=2,'x'=4] {'x'}, dimensions={0} | all-to-all | bytes 393216 | tf_op jit(solution)/shard_map/all_to_all | solution.py:222
  54.1 14.8 %all_to_all.38 = bf16[8,64,256]{2,1,0:T(8,128)(2,1)S(1)} all-to-all(bf16[8,64,256]{2,1,0:T(8,128)(2,1)S(1)} %shard_map.80), channel_id=1, replica_groups=mesh['z_hi'=4,'z_lo'=2,'y_lo'=4,'core'=2,'y_hi'=2,'x'=4] {'y_hi','x'}, dimensions={0} | all-to-all | bytes 524288 | tf_op jit(solution)/shard_map/all_to_all | solution.py:222
  68.8 1.3 shard_map.83
  70.1 5.1 %collective-permute-start.4 = (bf16[256,1792]{1,0:T(8,128)(2,1)S(1)}, bf16[256,1792]{1,0:T(8,128)(2,1)S(1)}, u32[]{:S(2)}, u32[]{:S(2)}) collective-permute-start(bf16[256,1792]{1,0:T(8,128)(2,1)S(1)} %shard_map.83), channel_id=1, source_target_pairs={{0,8},{8,0},{1,9},{9,1},{2,10},{10,2},{3,11},{11,3},{4,12},{12,4},... | collective-permute-start | bytes 2752520 | tf_op jit(solution)/shard_map/ppermute | solution.py:265
  75.3 1.3 shard_map.82.mine_ref
  77.5 31.5 %all_to_all.39 = bf16[32,8,1792]{2,1,0:T(8,128)(2,1)S(1)} all-to-all(bf16[32,8,1792]{2,1,0:T(8,128)(2,1)S(1)} %bitcast.14), channel_id=1, replica_groups=mesh['z_hi'=4,'z_lo'=2,'y_lo'=4,'core'=2,'y_hi'=2,'x'=4] {'z_hi','z_lo',..., dimensions={0} | all-to-all | bytes 1835008 | tf_op jit(solution)/shard_map/all_to_all | solution.py:222
  109.8 22.3 %all_to_all.40 = bf16[16,8,1792]{2,1,0:T(8,128)(2,1)S(1)} all-to-all(bf16[16,8,1792]{2,1,0:T(8,128)(2,1)S(1)} %bitcast.18), channel_id=1, replica_groups=mesh['z_hi'=4,'z_lo'=2,'y_lo'=4,'core'=2,'y_hi'=2,'x'=4] {'z_hi','y_lo'}, dimensions={0} | all-to-all | bytes 917504 | tf_op jit(solution)/shard_map/all_to_all | solution.py:222
  132.1 2.7 %collective-permute-start.6 = (bf16[64,1792]{1,0:T(8,128)(2,1)S(1)}, bf16[64,1792]{1,0:T(8,128)(2,1)S(1)}, u32[]{:S(2)}, u32[]{:S(2)}) collective-permute-start(bf16[64,1792]{1,0:T(8,128)(2,1)S(1)} %get-tuple-element.21), channel_id=1, source_target_pairs={{0,448},{64,0},{128,64},{192,128},{256,192},{320,256},{384,320},{4... | collective-permute-start | bytes 688136 | tf_op jit(solution)/shard_map/ppermute | solution.py:283
  134.8 2.6 %collective-permute-start.5 = (bf16[64,1792]{1,0:T(8,128)(2,1)S(1)}, bf16[64,1792]{1,0:T(8,128)(2,1)S(1)}, u32[]{:S(2)}, u32[]{:S(2)}) collective-permute-start(bf16[64,1792]{1,0:T(8,128)(2,1)S(1)} %get-tuple-element.22), channel_id=1, source_target_pairs={{0,64},{64,128},{128,192},{192,256},{256,320},{320,384},{384,448},... | collective-permute-start | bytes 688136 | tf_op jit(solution)/shard_map/ppermute | solution.py:283
  137.4 2.1 %collective-permute-done.6.refs_2_ = bf16[64,1792]{1,0:T(8,128)(2,1)S(1)} collective-permute-done((bf16[64,1792]{1,0:T(8,128)(2,1)S(1)}, bf16[64,1792]{1,0:T(8,128)(2,1)S(1)}, u32[]{:S(2)}, u32[]{:S(2)}) %collective-permute-start.6) | collective-permute-done | bytes 229408 | tf_op jit(solution)/shard_map/ppermute | solution.py:283
  139.4 3.3 %collective-permute-done.5.refs_1_ = bf16[64,1792]{1,0:T(8,128)(2,1)S(1)} collective-permute-done((bf16[64,1792]{1,0:T(8,128)(2,1)S(1)}, bf16[64,1792]{1,0:T(8,128)(2,1)S(1)}, u32[]{:S(2)}, u32[]{:S(2)}) %collective-permute-start.5) | collective-permute-done | bytes 229408 | tf_op jit(solution)/shard_map/ppermute | solution.py:283
  142.8 5.2 %collective-permute-start.7 = (bf16[256,1792]{1,0:T(8,128)(2,1)S(1)}, bf16[256,1792]{1,0:T(8,128)(2,1)S(1)}, u32[]{:S(2)}, u32[]{:S(2)}) collective-permute-start(bf16[256,1792]{1,0:T(8,128)(2,1)S(1)} %shard_map.86.directions_ref), channel_id=1, source_target_pairs={{0,8},{8,0},{1,9},{9,1},{2,10},{10,2},{3,11},{11,3},{4,12},{12,4},... | collective-permute-start | bytes 2752520 | tf_op jit(solution)/shard_map/ppermute | solution.py:287
  148.8 1.4 collective-permute-done.7.directions_ref
  150.2 1.3 shard_map.88
  (23 shorter events, 5.5 us)
Async XLA Ops:
  2.2 36.6 %all-to-all-start = ((bf16[64,16,256]{2,1,0:T(8,128)(2,1)}), bf16[64,16,256]{2,1,0:T(8,128)(2,1)S(1)}, u32[]{:S(2)}, u32[]{:S(2)}) async-start(bf16[64,16,256]{2,1,0:T(8,128)(2,1)} %broadcast_in_dim.2), calls=%async_computation | async-start | bytes 1048576 | tf_op jit(solution)/shard_map/all_to_all | solution.py:222
  19.3 1.1 copy-start.4
  22.2 10.6 %collective-permute-start = (bf16[48,2048]{1,0:T(8,128)(2,1)S(1)}, bf16[48,2048]{1,0:T(8,128)(2,1)S(1)}, u32[]{:S(2)}, u32[]{:S(2)}) collective-permute-start(bf16[48,2048]{1,0:T(8,128)(2,1)S(1)} %get-tuple-element.13), channel_id=1, source_target_pairs={{0,1},{1,2},{2,3},{3,0},{4,5},{5,6},{6,7},{7,4},{8,9},{9,10},{10,1... | collective-permute-start | bytes 589832 | tf_op jit(solution)/shard_map/ppermute | solution.py:230
  25.3 10.6 %collective-permute-start.1 = (bf16[48,2048]{1,0:T(8,128)(2,1)S(1)}, bf16[48,2048]{1,0:T(8,128)(2,1)S(1)}, u32[]{:S(2)}, u32[]{:S(2)}) collective-permute-start(bf16[48,2048]{1,0:T(8,128)(2,1)S(1)} %get-tuple-element.14), channel_id=1, source_target_pairs={{0,2},{1,3},{2,0},{3,1},{4,6},{5,7},{6,4},{7,5},{8,10},{9,11},{10,... | collective-permute-start | bytes 589832 | tf_op jit(solution)/shard_map/ppermute | solution.py:230
  29.7 7.6 %collective-permute-start.2 = (bf16[48,2048]{1,0:T(8,128)(2,1)S(1)}, bf16[48,2048]{1,0:T(8,128)(2,1)S(1)}, u32[]{:S(2)}, u32[]{:S(2)}) collective-permute-start(bf16[48,2048]{1,0:T(8,128)(2,1)S(1)} %get-tuple-element.15), channel_id=1, source_target_pairs={{0,3},{1,0},{2,1},{3,2},{4,7},{5,4},{6,5},{7,6},{8,11},{9,8},{10,9... | collective-permute-start | bytes 589832 | tf_op jit(solution)/shard_map/ppermute | solution.py:230
  37.3 16.7 %copy-start.3 = (bf16[16,256]{1,0:T(8,128)(2,1)S(1)}, bf16[16,256]{1,0:T(8,128)(2,1)}, u32[]{:S(2)}) copy-start(bf16[16,256]{1,0:T(8,128)(2,1)} %basis_ref.1) | copy-start | bytes 24580
  38.8 5.8 %collective-permute-start.3 = (bf16[1024,256]{1,0:T(8,128)(2,1)S(1)}, bf16[1024,256]{1,0:T(8,128)(2,1)S(1)}, u32[]{:S(2)}, u32[]{:S(2)}) collective-permute-start(bf16[1024,256]{1,0:T(8,128)(2,1)S(1)} %bitcast.16), channel_id=1, source_target_pairs={{0,8},{8,0},{1,9},{9,1},{2,10},{10,2},{3,11},{11,3},{4,12},{12,4},... | collective-permute-start | bytes 1572872 | tf_op jit(solution)/shard_map/ppermute | solution.py:237
  43.4 25.4 %copy-start = (bf16[384,3584]{1,0:T(8,128)(2,1)S(1)}, bf16[384,3584]{1,0:T(8,128)(2,1)}, u32[]{:S(2)}) copy-start(bf16[384,3584]{1,0:T(8,128)(2,1)} %grad_ref.3) | copy-start | bytes 8257540
  70.1 7.2 %collective-permute-start.4 = (bf16[256,1792]{1,0:T(8,128)(2,1)S(1)}, bf16[256,1792]{1,0:T(8,128)(2,1)S(1)}, u32[]{:S(2)}, u32[]{:S(2)}) collective-permute-start(bf16[256,1792]{1,0:T(8,128)(2,1)S(1)} %shard_map.83), channel_id=1, source_target_pairs={{0,8},{8,0},{1,9},{9,1},{2,10},{10,2},{3,11},{11,3},{4,12},{12,4},... | collective-permute-start | bytes 2752520 | tf_op jit(solution)/shard_map/ppermute | solution.py:265
  77.5 31.5 %copy-start.1 = (f32[4,3584]{1,0:T(4,128)S(1)}, f32[4,3584]{1,0:T(4,128)}, u32[]{:S(2)}) copy-start(f32[4,3584]{1,0:T(4,128)} %first_ref.1) | copy-start | bytes 172036
  77.5 31.5 %copy-start.2 = (f32[4,3584]{1,0:T(4,128)S(1)}, f32[4,3584]{1,0:T(4,128)}, u32[]{:S(2)}) copy-start(f32[4,3584]{1,0:T(4,128)} %second_ref.1) | copy-start | bytes 172036
  132.1 7.4 %collective-permute-start.6 = (bf16[64,1792]{1,0:T(8,128)(2,1)S(1)}, bf16[64,1792]{1,0:T(8,128)(2,1)S(1)}, u32[]{:S(2)}, u32[]{:S(2)}) collective-permute-start(bf16[64,1792]{1,0:T(8,128)(2,1)S(1)} %get-tuple-element.21), channel_id=1, source_target_pairs={{0,448},{64,0},{128,64},{192,128},{256,192},{320,256},{384,320},{4... | collective-permute-start | bytes 688136 | tf_op jit(solution)/shard_map/ppermute | solution.py:283
  134.8 8.0 %collective-permute-start.5 = (bf16[64,1792]{1,0:T(8,128)(2,1)S(1)}, bf16[64,1792]{1,0:T(8,128)(2,1)S(1)}, u32[]{:S(2)}, u32[]{:S(2)}) collective-permute-start(bf16[64,1792]{1,0:T(8,128)(2,1)S(1)} %get-tuple-element.22), channel_id=1, source_target_pairs={{0,64},{64,128},{128,192},{192,256},{256,320},{320,384},{384,448},... | collective-permute-start | bytes 688136 | tf_op jit(solution)/shard_map/ppermute | solution.py:283
  142.8 7.3 %collective-permute-start.7 = (bf16[256,1792]{1,0:T(8,128)(2,1)S(1)}, bf16[256,1792]{1,0:T(8,128)(2,1)S(1)}, u32[]{:S(2)}, u32[]{:S(2)}) collective-permute-start(bf16[256,1792]{1,0:T(8,128)(2,1)S(1)} %shard_map.86.directions_ref), channel_id=1, source_target_pairs={{0,8},{8,0},{1,9},{9,1},{2,10},{10,2},{3,11},{11,3},{4,12},{12,4},... | collective-permute-start | bytes 2752520 | tf_op jit(solution)/shard_map/ppermute | solution.py:287

commit v12 on v7

--- a/solution.py
+++ b/solution.py
@@ -118,7 +118,7 @@
     arranged = lax.dot_general(
         place, coefficients, (((1,), (1,)), ((), ())), preferred_element_type=F32
     ).astype(BF16)
-    tile = 256
+    tile = 896
     first_half = (iota((rows, tile), 0) & 4) == 0
     for start in range(0, width, tile):
         low = jnp.dot(
@@ -179,7 +179,7 @@
 
 def expand_own(basis_ref, directions_ref, out_ref):
     width = directions_ref.shape[1]
-    tile = 256
+    tile = 896
     for half in range(2):
         basis = basis_ref[half]
         for start in range(0, width, tile):
@@ -190,7 +190,7 @@
 
 def expand(basis_ref, part_ref, directions_ref, out_ref):
     width = directions_ref.shape[1]
-    tile = 256
+    tile = 896
     for half in range(2):
         basis = basis_ref[2 + half]
         for start in range(0, width, tile):

time: 149 us -> 149 us (level)
  no operation moved by 1% of the time
where the time goes in v12:
time: 149 us; the launch traced here: 148 us
  blocking collectives  85.1 us (57%)
  starting transfers between devices  42.3 us (28%)
  waiting for transfers between devices  9.27 us (6%)
  Pallas kernels  8.09 us (5%)
  local copies, waits for them, and re-layouts  2.68 us (2%)
    all_to_all x4, blocking collectives, exchange(): return lax.all_to_all(array, axes, 0, 0, tiled=True)  85.1 us
    all_to_all x1, starting transfers between devices, exchange(): return lax.all_to_all(array, axes, 0, 0, tiled=True)  17.1 us
    ppermute x3, starting transfers between devices, per_device(): lax.ppermute(blocks[step], 'x', [(x, (x + step) % X) for x in range(X)])  10.5 us
    ppermute x1, starting transfers between devices, per_device(): others = lax.ppermute(directions, 'core', swap)  5.13 us
    ppermute x1, starting transfers between devices, per_device(): theirs = lax.ppermute(projected(False, BF16), 'core', swap)  5.12 us
    ppermute x3, waiting for transfers between devices, per_device(): lax.ppermute(blocks[step], 'x', [(x, (x + step) % X) for x in range(X)])  4.53 us
    ppermute x1, starting transfers between devices, per_device(): sibling_basis = lax.ppermute(class_basis, 'core', swap)  4.32 us
  transfers between devices with their start and end apart: 7, of which 6 were waited for; matrix products, arithmetic and copies ran while one was open for 0% of the time, Pallas kernels for 3%

profile of v12, /device:TPU:1, one launch (start us, length us, event | category | flops | bytes accessed | tf_op | source)
XLA Modules:
  0.0 148.2 jit_solution(9180471440768113185)
XLA Ops:
  0.6 1.5 %broadcast_in_dim.2 = bf16[64,16,256]{2,1,0:T(8,128)(2,1)} broadcast(bf16[16,256]{1,0:T(8,128)(2,1)} %basis_ref.1), dimensions={1,2} | broadcast | bytes 532480 | tf_op jit(solution)/shard_map/broadcast_in_dim | solution.py:219
  2.2 17.1 %all-to-all-start = ((bf16[64,16,256]{2,1,0:T(8,128)(2,1)}), bf16[64,16,256]{2,1,0:T(8,128)(2,1)S(1)}, u32[]{:S(2)}, u32[]{:S(2)}) async-start(bf16[64,16,256]{2,1,0:T(8,128)(2,1)} %broadcast_in_dim.2), calls=%async_computation | async-start | bytes 1048576 | tf_op jit(solution)/shard_map/all_to_all | solution.py:216
  19.3 1.1 copy-done.4
  20.4 1.7 %shard_map.76 = (bf16[48,2048]{1,0:T(8,128)(2,1)S(1)}, bf16[48,2048]{1,0:T(8,128)(2,1)S(1)}, bf16[48,2048]{1,0:T(8,128)(2,1)S(1)}, bf16[48,2048]{1,0:T(8,128)(2,1)S(1)}) custom-call(bf16[48,8192]{1,0:T(8,128)(2,1)S(1)} %copy-done.4), custom_call_target="tpu_custom_call" | custom-call | flops 402653184 | tf_op jit(solution)/shard_map/pallas_call | solution.py:222
  22.2 3.1 %collective-permute-start = (bf16[48,2048]{1,0:T(8,128)(2,1)S(1)}, bf16[48,2048]{1,0:T(8,128)(2,1)S(1)}, u32[]{:S(2)}, u32[]{:S(2)}) collective-permute-start(bf16[48,2048]{1,0:T(8,128)(2,1)S(1)} %get-tuple-element.13), channel_id=1, source_target_pairs={{0,1},{1,2},{2,3},{3,0},{4,5},{5,6},{6,7},{7,4},{8,9},{9,10},{10,1... | collective-permute-start | bytes 589832 | tf_op jit(solution)/shard_map/ppermute | solution.py:224
  25.3 4.4 %collective-permute-start.1 = (bf16[48,2048]{1,0:T(8,128)(2,1)S(1)}, bf16[48,2048]{1,0:T(8,128)(2,1)S(1)}, u32[]{:S(2)}, u32[]{:S(2)}) collective-permute-start(bf16[48,2048]{1,0:T(8,128)(2,1)S(1)} %get-tuple-element.14), channel_id=1, source_target_pairs={{0,2},{1,3},{2,0},{3,1},{4,6},{5,7},{6,4},{7,5},{8,10},{9,11},{10,... | collective-permute-start | bytes 589832 | tf_op jit(solution)/shard_map/ppermute | solution.py:224
  29.7 3.1 %collective-permute-start.2 = (bf16[48,2048]{1,0:T(8,128)(2,1)S(1)}, bf16[48,2048]{1,0:T(8,128)(2,1)S(1)}, u32[]{:S(2)}, u32[]{:S(2)}) collective-permute-start(bf16[48,2048]{1,0:T(8,128)(2,1)S(1)} %get-tuple-element.15), channel_id=1, source_target_pairs={{0,3},{1,0},{2,1},{3,2},{4,7},{5,4},{6,5},{7,6},{8,11},{9,8},{10,9... | collective-permute-start | bytes 589832 | tf_op jit(solution)/shard_map/ppermute | solution.py:224
  32.8 3.2 %collective-permute-done.1.refs_2_ = bf16[48,2048]{1,0:T(8,128)(2,1)S(1)} collective-permute-done((bf16[48,2048]{1,0:T(8,128)(2,1)S(1)}, bf16[48,2048]{1,0:T(8,128)(2,1)S(1)}, u32[]{:S(2)}, u32[]{:S(2)}) %collective-permute-start.1) | collective-permute-done | bytes 196640 | tf_op jit(solution)/shard_map/ppermute | solution.py:224
  35.9 1.4 collective-permute-done.2.refs_3_
  37.4 1.5 all-to-all-done
  38.8 4.3 %collective-permute-start.3 = (bf16[1024,256]{1,0:T(8,128)(2,1)S(1)}, bf16[1024,256]{1,0:T(8,128)(2,1)S(1)}, u32[]{:S(2)}, u32[]{:S(2)}) collective-permute-start(bf16[1024,256]{1,0:T(8,128)(2,1)S(1)} %bitcast.13), channel_id=1, source_target_pairs={{0,8},{8,0},{1,9},{9,1},{2,10},{10,2},{3,11},{11,3},{4,12},{12,4},... | collective-permute-start | bytes 1572872 | tf_op jit(solution)/shard_map/ppermute | solution.py:231
  43.4 1.2 collective-permute-done.3.basis_ref
  44.9 9.1 %all_to_all.37.parts_ref = f32[4,48,256]{2,1,0:T(8,128)S(1)} all-to-all(f32[4,48,256]{2,1,0:T(8,128)S(1)} %shard_map.79), channel_id=1, replica_groups=mesh['z'=8,'y_lo'=4,'core'=2,'y_hi'=2,'x'=4] {'x'}, dimensions={0} | all-to-all | bytes 393216 | tf_op jit(solution)/shard_map/all_to_all | solution.py:216
  54.1 14.8 %all_to_all.38 = bf16[8,64,256]{2,1,0:T(8,128)(2,1)S(1)} all-to-all(bf16[8,64,256]{2,1,0:T(8,128)(2,1)S(1)} %shard_map.80), channel_id=1, replica_groups=mesh['z'=8,'y_lo'=4,'core'=2,'y_hi'=2,'x'=4] {'y_hi','x'}, dimensions={0} | all-to-all | bytes 524288 | tf_op jit(solution)/shard_map/all_to_all | solution.py:216
  68.8 1.4 shard_map.83
  70.2 5.1 %collective-permute-start.4 = (bf16[256,1792]{1,0:T(8,128)(2,1)S(1)}, bf16[256,1792]{1,0:T(8,128)(2,1)S(1)}, u32[]{:S(2)}, u32[]{:S(2)}) collective-permute-start(bf16[256,1792]{1,0:T(8,128)(2,1)S(1)} %shard_map.83), channel_id=1, source_target_pairs={{0,8},{8,0},{1,9},{9,1},{2,10},{10,2},{3,11},{11,3},{4,12},{12,4},... | collective-permute-start | bytes 2752520 | tf_op jit(solution)/shard_map/ppermute | solution.py:259
  75.3 1.4 shard_map.82.mine_ref
  76.7 0.7 collective-permute-done.4.theirs_ref
  77.6 31.5 %all_to_all.39 = bf16[32,8,1792]{2,1,0:T(8,128)(2,1)S(1)} all-to-all(bf16[32,8,1792]{2,1,0:T(8,128)(2,1)S(1)} %bitcast.9), channel_id=1, replica_groups=mesh['z'=8,'y_lo'=4,'core'=2,'y_hi'=2,'x'=4] {'z','y_lo'}, dimensions={0} | all-to-all | bytes 1835008 | tf_op jit(solution)/shard_map/all_to_all | solution.py:216
  109.1 0.8 shard_map.85
  109.8 29.8 %all_to_all.40 = bf16[32,8,1792]{2,1,0:T(8,128)(2,1)S(1)} all-to-all(bf16[32,8,1792]{2,1,0:T(8,128)(2,1)S(1)} %bitcast.15), channel_id=1, replica_groups=mesh['z'=8,'y_lo'=4,'core'=2,'y_hi'=2,'x'=4] {'z','y_lo'}, dimensions={0} | all-to-all | bytes 1835008 | tf_op jit(solution)/shard_map/all_to_all | solution.py:216
  139.6 5.1 %collective-permute-start.5 = (bf16[256,1792]{1,0:T(8,128)(2,1)S(1)}, bf16[256,1792]{1,0:T(8,128)(2,1)S(1)}, u32[]{:S(2)}, u32[]{:S(2)}) collective-permute-start(bf16[256,1792]{1,0:T(8,128)(2,1)S(1)} %bitcast.10), channel_id=1, source_target_pairs={{0,8},{8,0},{1,9},{9,1},{2,10},{10,2},{3,11},{11,3},{4,12},{12,4},... | collective-permute-start | bytes 2752520 | tf_op jit(solution)/shard_map/ppermute | solution.py:274
  145.5 1.4 collective-permute-done.5.directions_ref
  146.8 1.4 shard_map.87
  (17 shorter events, 1.5 us)
Async XLA Ops:
  2.2 36.6 %all-to-all-start = ((bf16[64,16,256]{2,1,0:T(8,128)(2,1)}), bf16[64,16,256]{2,1,0:T(8,128)(2,1)S(1)}, u32[]{:S(2)}, u32[]{:S(2)}) async-start(bf16[64,16,256]{2,1,0:T(8,128)(2,1)} %broadcast_in_dim.2), calls=%async_computation | async-start | bytes 1048576 | tf_op jit(solution)/shard_map/all_to_all | solution.py:216
  19.3 1.1 copy-start.4
  22.2 10.6 %collective-permute-start = (bf16[48,2048]{1,0:T(8,128)(2,1)S(1)}, bf16[48,2048]{1,0:T(8,128)(2,1)S(1)}, u32[]{:S(2)}, u32[]{:S(2)}) collective-permute-start(bf16[48,2048]{1,0:T(8,128)(2,1)S(1)} %get-tuple-element.13), channel_id=1, source_target_pairs={{0,1},{1,2},{2,3},{3,0},{4,5},{5,6},{6,7},{7,4},{8,9},{9,10},{10,1... | collective-permute-start | bytes 589832 | tf_op jit(solution)/shard_map/ppermute | solution.py:224
  25.3 10.6 %collective-permute-start.1 = (bf16[48,2048]{1,0:T(8,128)(2,1)S(1)}, bf16[48,2048]{1,0:T(8,128)(2,1)S(1)}, u32[]{:S(2)}, u32[]{:S(2)}) collective-permute-start(bf16[48,2048]{1,0:T(8,128)(2,1)S(1)} %get-tuple-element.14), channel_id=1, source_target_pairs={{0,2},{1,3},{2,0},{3,1},{4,6},{5,7},{6,4},{7,5},{8,10},{9,11},{10,... | collective-permute-start | bytes 589832 | tf_op jit(solution)/shard_map/ppermute | solution.py:224
  29.7 7.6 %collective-permute-start.2 = (bf16[48,2048]{1,0:T(8,128)(2,1)S(1)}, bf16[48,2048]{1,0:T(8,128)(2,1)S(1)}, u32[]{:S(2)}, u32[]{:S(2)}) collective-permute-start(bf16[48,2048]{1,0:T(8,128)(2,1)S(1)} %get-tuple-element.15), channel_id=1, source_target_pairs={{0,3},{1,0},{2,1},{3,2},{4,7},{5,4},{6,5},{7,6},{8,11},{9,8},{10,9... | collective-permute-start | bytes 589832 | tf_op jit(solution)/shard_map/ppermute | solution.py:224
  37.3 16.7 %copy-start.3 = (bf16[16,256]{1,0:T(8,128)(2,1)S(1)}, bf16[16,256]{1,0:T(8,128)(2,1)}, u32[]{:S(2)}) copy-start(bf16[16,256]{1,0:T(8,128)(2,1)} %basis_ref.1) | copy-start | bytes 24580
  38.8 5.8 %collective-permute-start.3 = (bf16[1024,256]{1,0:T(8,128)(2,1)S(1)}, bf16[1024,256]{1,0:T(8,128)(2,1)S(1)}, u32[]{:S(2)}, u32[]{:S(2)}) collective-permute-start(bf16[1024,256]{1,0:T(8,128)(2,1)S(1)} %bitcast.13), channel_id=1, source_target_pairs={{0,8},{8,0},{1,9},{9,1},{2,10},{10,2},{3,11},{11,3},{4,12},{12,4},... | collective-permute-start | bytes 1572872 | tf_op jit(solution)/shard_map/ppermute | solution.py:231
  43.4 25.4 %copy-start = (bf16[384,3584]{1,0:T(8,128)(2,1)S(1)}, bf16[384,3584]{1,0:T(8,128)(2,1)}, u32[]{:S(2)}) copy-start(bf16[384,3584]{1,0:T(8,128)(2,1)} %grad_ref.3) | copy-start | bytes 8257540
  70.2 7.2 %collective-permute-start.4 = (bf16[256,1792]{1,0:T(8,128)(2,1)S(1)}, bf16[256,1792]{1,0:T(8,128)(2,1)S(1)}, u32[]{:S(2)}, u32[]{:S(2)}) collective-permute-start(bf16[256,1792]{1,0:T(8,128)(2,1)S(1)} %shard_map.83), channel_id=1, source_target_pairs={{0,8},{8,0},{1,9},{9,1},{2,10},{10,2},{3,11},{11,3},{4,12},{12,4},... | collective-permute-start | bytes 2752520 | tf_op jit(solution)/shard_map/ppermute | solution.py:259
  77.6 31.5 %copy-start.1 = (f32[4,3584]{1,0:T(4,128)S(1)}, f32[4,3584]{1,0:T(4,128)}, u32[]{:S(2)}) copy-start(f32[4,3584]{1,0:T(4,128)} %first_ref.1) | copy-start | bytes 172036
  77.6 31.5 %copy-start.2 = (f32[4,3584]{1,0:T(4,128)S(1)}, f32[4,3584]{1,0:T(4,128)}, u32[]{:S(2)}) copy-start(f32[4,3584]{1,0:T(4,128)} %second_ref.1) | copy-start | bytes 172036
  139.6 7.2 %collective-permute-start.5 = (bf16[256,1792]{1,0:T(8,128)(2,1)S(1)}, bf16[256,1792]{1,0:T(8,128)(2,1)S(1)}, u32[]{:S(2)}, u32[]{:S(2)}) collective-permute-start(bf16[256,1792]{1,0:T(8,128)(2,1)S(1)} %bitcast.10), channel_id=1, source_target_pairs={{0,8},{8,0},{1,9},{9,1},{2,10},{10,2},{3,11},{11,3},{4,12},{12,4},... | collective-permute-start | bytes 2752520 | tf_op jit(solution)/shard_map/ppermute | solution.py:274

commit v13 on v7

--- a/solution.py
+++ b/solution.py
@@ -220,10 +220,11 @@
     class_basis = exchange(basis_copies, ("z", "y_lo", "y_hi")).reshape(copies * own, rank)
     block = shape((rows, features // X), BF16)
     blocks = call(split_features, (block,) * X, 2 * rows * features * 512, 0)(tokens)
-    held = [blocks[0]] + [
-        lax.ppermute(blocks[step], "x", [(x, (x + step) % X) for x in range(X)])
-        for step in range(1, X)
-    ]
+    arrived = {
+        step: lax.ppermute(blocks[step], "x", [(x, (x + step) % X) for x in range(X)])
+        for step in (2, 1, 3)
+    }
+    held = [blocks[0]] + [arrived[step] for step in range(1, X)]
     stacked = call(
         stack, shape((X * rows, features // X), BF16), rows * features, 4 * rows * features
     )(*held)

time: 149 us -> 149 us (level)
  no operation moved by 1% of the time
where the time goes in v13:
time: 149 us; the launch traced here: 148 us
  blocking collectives  85.1 us (57%)
  starting transfers between devices  42.3 us (28%)
  waiting for transfers between devices  9.38 us (6%)
  Pallas kernels  7.88 us (5%)
  local copies, waits for them, and re-layouts  2.68 us (2%)
    all_to_all x4, blocking collectives, exchange(): return lax.all_to_all(array, axes, 0, 0, tiled=True)  85.1 us
    all_to_all x1, starting transfers between devices, exchange(): return lax.all_to_all(array, axes, 0, 0, tiled=True)  17.1 us
    ppermute x3, starting transfers between devices, per_device(): lax.ppermute(blocks[step], 'x', [(x, (x + step) % X) for x in range(X)])  10.5 us
    ppermute x1, starting transfers between devices, per_device(): others = lax.ppermute(directions, 'core', swap)  5.13 us
    ppermute x1, starting transfers between devices, per_device(): theirs = lax.ppermute(projected(False, BF16), 'core', swap)  5.12 us
    ppermute x3, waiting for transfers between devices, per_device(): lax.ppermute(blocks[step], 'x', [(x, (x + step) % X) for x in range(X)])  4.53 us
    ppermute x1, starting transfers between devices, per_device(): sibling_basis = lax.ppermute(class_basis, 'core', swap)  4.32 us
  transfers between devices with their start and end apart: 7, of which 6 were waited for; matrix products, arithmetic and copies ran while one was open for 0% of the time, Pallas kernels for 3%

profile of v13, /device:TPU:1, one launch (start us, length us, event | category | flops | bytes accessed | tf_op | source)
XLA Modules:
  0.0 148.1 jit_solution(17952114923134679244)
XLA Ops:
  0.6 1.5 %broadcast_in_dim.2 = bf16[64,16,256]{2,1,0:T(8,128)(2,1)} broadcast(bf16[16,256]{1,0:T(8,128)(2,1)} %basis_ref.1), dimensions={1,2} | broadcast | bytes 532480 | tf_op jit(solution)/shard_map/broadcast_in_dim | solution.py:219
  2.2 17.1 %all-to-all-start = ((bf16[64,16,256]{2,1,0:T(8,128)(2,1)}), bf16[64,16,256]{2,1,0:T(8,128)(2,1)S(1)}, u32[]{:S(2)}, u32[]{:S(2)}) async-start(bf16[64,16,256]{2,1,0:T(8,128)(2,1)} %broadcast_in_dim.2), calls=%async_computation | async-start | bytes 1048576 | tf_op jit(solution)/shard_map/all_to_all | solution.py:216
  19.3 1.1 copy-done.4
  20.4 1.7 %shard_map.76 = (bf16[48,2048]{1,0:T(8,128)(2,1)S(1)}, bf16[48,2048]{1,0:T(8,128)(2,1)S(1)}, bf16[48,2048]{1,0:T(8,128)(2,1)S(1)}, bf16[48,2048]{1,0:T(8,128)(2,1)S(1)}) custom-call(bf16[48,8192]{1,0:T(8,128)(2,1)S(1)} %copy-done.4), custom_call_target="tpu_custom_call" | custom-call | flops 402653184 | tf_op jit(solution)/shard_map/pallas_call | solution.py:222
  22.2 3.1 %collective-permute-start = (bf16[48,2048]{1,0:T(8,128)(2,1)S(1)}, bf16[48,2048]{1,0:T(8,128)(2,1)S(1)}, u32[]{:S(2)}, u32[]{:S(2)}) collective-permute-start(bf16[48,2048]{1,0:T(8,128)(2,1)S(1)} %get-tuple-element.13), channel_id=1, source_target_pairs={{0,1},{1,2},{2,3},{3,0},{4,5},{5,6},{6,7},{7,4},{8,9},{9,10},{10,1... | collective-permute-start | bytes 589832 | tf_op jit(solution)/shard_map/ppermute | solution.py:224
  25.3 4.4 %collective-permute-start.1 = (bf16[48,2048]{1,0:T(8,128)(2,1)S(1)}, bf16[48,2048]{1,0:T(8,128)(2,1)S(1)}, u32[]{:S(2)}, u32[]{:S(2)}) collective-permute-start(bf16[48,2048]{1,0:T(8,128)(2,1)S(1)} %get-tuple-element.14), channel_id=1, source_target_pairs={{0,2},{1,3},{2,0},{3,1},{4,6},{5,7},{6,4},{7,5},{8,10},{9,11},{10,... | collective-permute-start | bytes 589832 | tf_op jit(solution)/shard_map/ppermute | solution.py:224
  29.7 3.1 %collective-permute-start.2 = (bf16[48,2048]{1,0:T(8,128)(2,1)S(1)}, bf16[48,2048]{1,0:T(8,128)(2,1)S(1)}, u32[]{:S(2)}, u32[]{:S(2)}) collective-permute-start(bf16[48,2048]{1,0:T(8,128)(2,1)S(1)} %get-tuple-element.15), channel_id=1, source_target_pairs={{0,3},{1,0},{2,1},{3,2},{4,7},{5,4},{6,5},{7,6},{8,11},{9,8},{10,9... | collective-permute-start | bytes 589832 | tf_op jit(solution)/shard_map/ppermute | solution.py:224
  32.8 3.2 %collective-permute-done.1.refs_2_ = bf16[48,2048]{1,0:T(8,128)(2,1)S(1)} collective-permute-done((bf16[48,2048]{1,0:T(8,128)(2,1)S(1)}, bf16[48,2048]{1,0:T(8,128)(2,1)S(1)}, u32[]{:S(2)}, u32[]{:S(2)}) %collective-permute-start.1) | collective-permute-done | bytes 196640 | tf_op jit(solution)/shard_map/ppermute | solution.py:224
  35.9 1.4 collective-permute-done.2.refs_3_
  37.4 1.5 all-to-all-done
  38.8 4.3 %collective-permute-start.3 = (bf16[1024,256]{1,0:T(8,128)(2,1)S(1)}, bf16[1024,256]{1,0:T(8,128)(2,1)S(1)}, u32[]{:S(2)}, u32[]{:S(2)}) collective-permute-start(bf16[1024,256]{1,0:T(8,128)(2,1)S(1)} %bitcast.13), channel_id=1, source_target_pairs={{0,8},{8,0},{1,9},{9,1},{2,10},{10,2},{3,11},{11,3},{4,12},{12,4},... | collective-permute-start | bytes 1572872 | tf_op jit(solution)/shard_map/ppermute | solution.py:232
  43.4 1.2 collective-permute-done.3.basis_ref
  44.9 9.1 %all_to_all.37.parts_ref = f32[4,48,256]{2,1,0:T(8,128)S(1)} all-to-all(f32[4,48,256]{2,1,0:T(8,128)S(1)} %shard_map.79), channel_id=1, replica_groups=mesh['z'=8,'y_lo'=4,'core'=2,'y_hi'=2,'x'=4] {'x'}, dimensions={0} | all-to-all | bytes 393216 | tf_op jit(solution)/shard_map/all_to_all | solution.py:216
  54.1 14.8 %all_to_all.38 = bf16[8,64,256]{2,1,0:T(8,128)(2,1)S(1)} all-to-all(bf16[8,64,256]{2,1,0:T(8,128)(2,1)S(1)} %shard_map.80), channel_id=1, replica_groups=mesh['z'=8,'y_lo'=4,'core'=2,'y_hi'=2,'x'=4] {'y_hi','x'}, dimensions={0} | all-to-all | bytes 524288 | tf_op jit(solution)/shard_map/all_to_all | solution.py:216
  68.8 1.3 shard_map.83
  70.1 5.1 %collective-permute-start.4 = (bf16[256,1792]{1,0:T(8,128)(2,1)S(1)}, bf16[256,1792]{1,0:T(8,128)(2,1)S(1)}, u32[]{:S(2)}, u32[]{:S(2)}) collective-permute-start(bf16[256,1792]{1,0:T(8,128)(2,1)S(1)} %shard_map.83), channel_id=1, source_target_pairs={{0,8},{8,0},{1,9},{9,1},{2,10},{10,2},{3,11},{11,3},{4,12},{12,4},... | collective-permute-start | bytes 2752520 | tf_op jit(solution)/shard_map/ppermute | solution.py:260
  75.3 1.3 shard_map.82.mine_ref
  76.6 0.8 collective-permute-done.4.theirs_ref
  77.5 31.5 %all_to_all.39 = bf16[32,8,1792]{2,1,0:T(8,128)(2,1)S(1)} all-to-all(bf16[32,8,1792]{2,1,0:T(8,128)(2,1)S(1)} %bitcast.9), channel_id=1, replica_groups=mesh['z'=8,'y_lo'=4,'core'=2,'y_hi'=2,'x'=4] {'z','y_lo'}, dimensions={0} | all-to-all | bytes 1835008 | tf_op jit(solution)/shard_map/all_to_all | solution.py:216
  109.0 0.8 shard_map.85
  109.8 29.8 %all_to_all.40 = bf16[32,8,1792]{2,1,0:T(8,128)(2,1)S(1)} all-to-all(bf16[32,8,1792]{2,1,0:T(8,128)(2,1)S(1)} %bitcast.15), channel_id=1, replica_groups=mesh['z'=8,'y_lo'=4,'core'=2,'y_hi'=2,'x'=4] {'z','y_lo'}, dimensions={0} | all-to-all | bytes 1835008 | tf_op jit(solution)/shard_map/all_to_all | solution.py:216
  139.6 5.1 %collective-permute-start.5 = (bf16[256,1792]{1,0:T(8,128)(2,1)S(1)}, bf16[256,1792]{1,0:T(8,128)(2,1)S(1)}, u32[]{:S(2)}, u32[]{:S(2)}) collective-permute-start(bf16[256,1792]{1,0:T(8,128)(2,1)S(1)} %bitcast.10), channel_id=1, source_target_pairs={{0,8},{8,0},{1,9},{9,1},{2,10},{10,2},{3,11},{11,3},{4,12},{12,4},... | collective-permute-start | bytes 2752520 | tf_op jit(solution)/shard_map/ppermute | solution.py:275
  145.4 1.4 collective-permute-done.5.directions_ref
  146.8 1.3 shard_map.87
  (17 shorter events, 1.5 us)
Async XLA Ops:
  2.2 36.6 %all-to-all-start = ((bf16[64,16,256]{2,1,0:T(8,128)(2,1)}), bf16[64,16,256]{2,1,0:T(8,128)(2,1)S(1)}, u32[]{:S(2)}, u32[]{:S(2)}) async-start(bf16[64,16,256]{2,1,0:T(8,128)(2,1)} %broadcast_in_dim.2), calls=%async_computation | async-start | bytes 1048576 | tf_op jit(solution)/shard_map/all_to_all | solution.py:216
  19.3 1.1 copy-start.4
  22.2 10.6 %collective-permute-start = (bf16[48,2048]{1,0:T(8,128)(2,1)S(1)}, bf16[48,2048]{1,0:T(8,128)(2,1)S(1)}, u32[]{:S(2)}, u32[]{:S(2)}) collective-permute-start(bf16[48,2048]{1,0:T(8,128)(2,1)S(1)} %get-tuple-element.13), channel_id=1, source_target_pairs={{0,1},{1,2},{2,3},{3,0},{4,5},{5,6},{6,7},{7,4},{8,9},{9,10},{10,1... | collective-permute-start | bytes 589832 | tf_op jit(solution)/shard_map/ppermute | solution.py:224
  25.3 10.6 %collective-permute-start.1 = (bf16[48,2048]{1,0:T(8,128)(2,1)S(1)}, bf16[48,2048]{1,0:T(8,128)(2,1)S(1)}, u32[]{:S(2)}, u32[]{:S(2)}) collective-permute-start(bf16[48,2048]{1,0:T(8,128)(2,1)S(1)} %get-tuple-element.14), channel_id=1, source_target_pairs={{0,2},{1,3},{2,0},{3,1},{4,6},{5,7},{6,4},{7,5},{8,10},{9,11},{10,... | collective-permute-start | bytes 589832 | tf_op jit(solution)/shard_map/ppermute | solution.py:224
  29.7 7.6 %collective-permute-start.2 = (bf16[48,2048]{1,0:T(8,128)(2,1)S(1)}, bf16[48,2048]{1,0:T(8,128)(2,1)S(1)}, u32[]{:S(2)}, u32[]{:S(2)}) collective-permute-start(bf16[48,2048]{1,0:T(8,128)(2,1)S(1)} %get-tuple-element.15), channel_id=1, source_target_pairs={{0,3},{1,0},{2,1},{3,2},{4,7},{5,4},{6,5},{7,6},{8,11},{9,8},{10,9... | collective-permute-start | bytes 589832 | tf_op jit(solution)/shard_map/ppermute | solution.py:224
  37.3 16.7 %copy-start.3 = (bf16[16,256]{1,0:T(8,128)(2,1)S(1)}, bf16[16,256]{1,0:T(8,128)(2,1)}, u32[]{:S(2)}) copy-start(bf16[16,256]{1,0:T(8,128)(2,1)} %basis_ref.1) | copy-start | bytes 24580
  38.8 5.8 %collective-permute-start.3 = (bf16[1024,256]{1,0:T(8,128)(2,1)S(1)}, bf16[1024,256]{1,0:T(8,128)(2,1)S(1)}, u32[]{:S(2)}, u32[]{:S(2)}) collective-permute-start(bf16[1024,256]{1,0:T(8,128)(2,1)S(1)} %bitcast.13), channel_id=1, source_target_pairs={{0,8},{8,0},{1,9},{9,1},{2,10},{10,2},{3,11},{11,3},{4,12},{12,4},... | collective-permute-start | bytes 1572872 | tf_op jit(solution)/shard_map/ppermute | solution.py:232
  43.4 25.4 %copy-start = (bf16[384,3584]{1,0:T(8,128)(2,1)S(1)}, bf16[384,3584]{1,0:T(8,128)(2,1)}, u32[]{:S(2)}) copy-start(bf16[384,3584]{1,0:T(8,128)(2,1)} %grad_ref.3) | copy-start | bytes 8257540
  70.1 7.2 %collective-permute-start.4 = (bf16[256,1792]{1,0:T(8,128)(2,1)S(1)}, bf16[256,1792]{1,0:T(8,128)(2,1)S(1)}, u32[]{:S(2)}, u32[]{:S(2)}) collective-permute-start(bf16[256,1792]{1,0:T(8,128)(2,1)S(1)} %shard_map.83), channel_id=1, source_target_pairs={{0,8},{8,0},{1,9},{9,1},{2,10},{10,2},{3,11},{11,3},{4,12},{12,4},... | collective-permute-start | bytes 2752520 | tf_op jit(solution)/shard_map/ppermute | solution.py:260
  77.5 31.5 %copy-start.1 = (f32[4,3584]{1,0:T(4,128)S(1)}, f32[4,3584]{1,0:T(4,128)}, u32[]{:S(2)}) copy-start(f32[4,3584]{1,0:T(4,128)} %first_ref.1) | copy-start | bytes 172036
  77.5 31.5 %copy-start.2 = (f32[4,3584]{1,0:T(4,128)S(1)}, f32[4,3584]{1,0:T(4,128)}, u32[]{:S(2)}) copy-start(f32[4,3584]{1,0:T(4,128)} %second_ref.1) | copy-start | bytes 172036
  139.6 7.2 %collective-permute-start.5 = (bf16[256,1792]{1,0:T(8,128)(2,1)S(1)}, bf16[256,1792]{1,0:T(8,128)(2,1)S(1)}, u32[]{:S(2)}, u32[]{:S(2)}) collective-permute-start(bf16[256,1792]{1,0:T(8,128)(2,1)S(1)} %bitcast.10), channel_id=1, source_target_pairs={{0,8},{8,0},{1,9},{9,1},{2,10},{10,2},{3,11},{11,3},{4,12},{12,4},... | collective-permute-start | bytes 2752520 | tf_op jit(solution)/shard_map/ppermute | solution.py:275
